TPU v7x, 512 devices: a whole 4x4x16 slice. The times are simulated.
512 devices in a mesh: op: 16 (over y_hi, x, core), sec: 32 (over y_lo, z).
Axes of the slice: x: 4, y: 4 (y_hi: 2, y_lo: 2; y = y_hi * 2 + y_lo), z: 16, core: 2. Of those that a mesh axis runs over, the one named last changes fastest.
Arguments:
- start_vector: bfloat16 [64, 512, 512], P('sec'), may hold values from -100 to 100
- left_operators: bfloat16 [16, 64, 512, 512], P('op', 'sec'), may hold values from -0.25 to 0.25
- right_operators: bfloat16 [16, 64, 512, 512], P('op', 'sec'), may hold values from -0.25 to 0.25
- left_energy: float32 [64, 512], P('sec'), may hold values from -2 to 2
- right_energy: float32 [64, 512], P('sec'), may hold values from -2 to 2
- sector_size: int32 [64], replicated, may hold values from 64 to 512, as said below
- sector_spin: int32 [64], replicated, may hold values from 0 to 8
Outputs:
- ritz_vector: bfloat16 [64, 512, 512], P('sec', 'op')
- ritz_residual: bfloat16 [64, 512, 512], P('sec', 'op')
- energies: float32 [2], replicated
Inputs may be any that keep to these rules, and one draw needn't show every extreme that they name: `sector_size`: at least one sector has exactly 512 states and one exactly 64.
All inputs are finite; a program needn't handle non-finite values.
Results may differ from a plain program's by a relative error of at most 0.033.
Values may be sent and summed in bfloat16 or wider, within the bound.
No kernel may reach another device: no remote copies, remote signals or barrier semaphores. Data moves between devices by JAX's collectives and lax.ppermute only.
A program may use at most 64 MiB of HBM per device.

v0:
```python
import jax
import jax.numpy as jnp
from jax import lax
from jax.sharding import PartitionSpec as P


def from_behind(block, axis, distance):
    devices = range(lax.axis_size(axis))
    route = [(i - distance, i) for i in devices if i - distance in devices]
    return lax.ppermute(block, axis, route)


def tile_product(first_operand, first_axis, second_operand, second_axis, tiles_used, tile_size):
    out_rows = first_operand.shape[1 - first_axis]
    out_columns = second_operand.shape[1 - second_axis]

    def accumulate(position, running):
        first_piece = lax.dynamic_slice_in_dim(
            first_operand, position * tile_size, tile_size, first_axis
        )
        second_piece = lax.dynamic_slice_in_dim(
            second_operand, position * tile_size, tile_size, second_axis
        )
        return running + lax.dot_general(
            first_piece,
            second_piece,
            (((first_axis,), (second_axis,)), ((), ())),
            preferred_element_type=jnp.float32,
        )

    return lax.fori_loop(0, tiles_used, accumulate, jnp.zeros((out_rows, out_columns), jnp.float32))


def raised_term(left_block, right_block, source, factor, tiles_used, tile_size):
    right_image = tile_product(source, 1, right_block, 1, tiles_used, tile_size).astype(
        jnp.bfloat16
    )
    return factor * tile_product(left_block, 1, right_image, 0, tiles_used, tile_size)


def lowered_term(left_block, right_block, target, factor, tiles_used, tile_size):
    left_image = tile_product(left_block, 0, target, 0, tiles_used, tile_size).astype(jnp.bfloat16)
    return factor * tile_product(left_image, 1, right_block, 0, tiles_used, tile_size)


def body(
    start_vector,
    left_operators,
    right_operators,
    left_energy,
    right_energy,
    sector_size,
    sector_spin,
):
    sectors_held = start_vector.shape[0]
    block_width = start_vector.shape[1]
    tile_size = min(128, block_width)
    row_share = block_width // lax.axis_size("op")
    first_sector = lax.axis_index("sec") * sectors_held
    padding = jnp.zeros((1,), jnp.int32)
    padded_size = jnp.concatenate([padding, sector_size, padding])
    padded_spin = jnp.concatenate([padding, sector_spin, padding])
    near_size = lax.dynamic_slice_in_dim(padded_size, first_sector, sectors_held + 2)
    near_spin = lax.dynamic_slice_in_dim(padded_spin, first_sector, sectors_held + 2).astype(
        jnp.float32
    )
    linked = (near_size[:-1] > 0) & (near_size[1:] > 0)
    coupling = jnp.where(linked, jnp.sqrt((near_spin[1:] + 1.0) / (near_spin[:-1] + 1.0)), 0.0)
    raise_tiles = jnp.where(linked, (near_size[:-1] + tile_size - 1) // tile_size, 0)
    lower_tiles = jnp.where(linked, (near_size[1:] + tile_size - 1) // tile_size, 0)
    own_size = near_size[1 : sectors_held + 1]
    positions = jnp.arange(block_width, dtype=jnp.int32)
    local_positions = jnp.arange(block_width, dtype=jnp.int32)
    inside_rows = local_positions[None, :] < own_size[:, None]
    inside_columns = positions[None, :] < own_size[:, None]
    cell_mask = inside_rows[:, :, None] & inside_columns[:, None, :]
    whole_mask = (positions[None, :, None] < own_size[:, None, None]) & inside_columns[:, None, :]
    diagonal = left_energy[:, :, None] + right_energy[:, None, :]
    masked_start = jnp.where(whole_mask, start_vector, jnp.zeros_like(start_vector))

    def apply_operator(vector):
        following = from_behind(vector[0], "sec", -1)
        extended = jnp.concatenate([vector, following[None]], axis=0)
        partial_terms = [
            jnp.zeros((block_width, block_width), jnp.float32)
            for sector_slot in range(sectors_held)
        ]
        leaving = jnp.zeros((block_width, block_width), jnp.float32)
        for sector_slot in range(sectors_held):
            left_block = left_operators[0, sector_slot]
            right_block = right_operators[0, sector_slot]
            partial_terms[sector_slot] = partial_terms[sector_slot] + lowered_term(
                left_block,
                right_block,
                extended[sector_slot + 1],
                coupling[sector_slot + 1],
                lower_tiles[sector_slot + 1],
                tile_size,
            )
            if sector_slot + 1 < sectors_held:
                partial_terms[sector_slot + 1] = raised_term(
                    left_block,
                    right_block,
                    vector[sector_slot],
                    coupling[sector_slot + 1],
                    raise_tiles[sector_slot + 1],
                    tile_size,
                )
            else:
                leaving = raised_term(
                    left_block,
                    right_block,
                    vector[sector_slot],
                    coupling[sector_slot + 1],
                    raise_tiles[sector_slot + 1],
                    tile_size,
                )
        partial_terms[0] = partial_terms[0] + from_behind(
            leaving.astype(jnp.bfloat16), "sec", 1
        ).astype(leaving.dtype)
        partial_image = jnp.stack(partial_terms)
        summed = lax.psum(partial_image.astype(jnp.bfloat16), "op").astype(jnp.float32)
        local_vector = vector.astype(jnp.float32)
        return jnp.where(cell_mask, summed + diagonal * local_vector, 0.0)

    def paired_total(first_amount, second_amount):
        return lax.psum((first_amount, second_amount), "sec")

    def single_total(amount):
        return lax.psum(amount, "sec")

    def own_rows(array):
        return lax.dynamic_slice_in_dim(array, lax.axis_index("op") * row_share, row_share, 1)

    first_image = apply_operator(masked_start)
    start_values = masked_start.astype(jnp.float32)
    start_norm, start_energy = paired_total(
        jnp.sum(start_values * start_values), jnp.sum(start_values * first_image)
    )
    rayleigh = start_energy / start_norm
    start_scale = jnp.sqrt(start_norm)
    unit_start = start_values / start_scale
    unit_image = first_image / start_scale
    residual_first = unit_image - rayleigh * unit_start
    correction = residual_first / (jnp.abs(diagonal - rayleigh) + 1.0)
    correlation = single_total(jnp.sum(unit_start * correction))
    remainder = correction - correlation * unit_start
    spread = single_total(jnp.sum(remainder * remainder))
    unit_second = remainder / jnp.sqrt(spread)
    second_local = unit_second.astype(jnp.bfloat16)
    second_image = apply_operator(second_local)
    cross_term, second_energy = paired_total(
        jnp.sum(unit_start * second_image), jnp.sum(unit_second * second_image)
    )
    half_gap = 0.5 * (rayleigh - second_energy)
    lowest = 0.5 * (rayleigh + second_energy) - jnp.sqrt(
        half_gap * half_gap + cross_term * cross_term
    )
    rotation = 0.5 * jnp.arctan2(2.0 * cross_term, rayleigh - second_energy)
    sine_angle = jnp.sin(rotation)
    cosine_angle = jnp.cos(rotation)
    ritz_unit = sine_angle * unit_start - cosine_angle * unit_second
    ritz_vector = (start_scale * ritz_unit).astype(jnp.bfloat16)
    ritz_residual = (
        start_scale * (sine_angle * unit_image - cosine_angle * second_image - lowest * ritz_unit)
    ).astype(jnp.bfloat16)
    return (own_rows(ritz_vector), own_rows(ritz_residual), jnp.stack([rayleigh, lowest]))


def solution(mesh):
    return jax.shard_map(
        body,
        mesh=mesh,
        in_specs=(
            P("sec", None, None),
            P("op", "sec", None, None),
            P("op", "sec", None, None),
            P("sec", None),
            P("sec", None),
            P(),
            P(),
        ),
        out_specs=(P("sec", "op", None), P("sec", "op", None), P()),
        check_vma=False,
    )
```

profile of v0, /device:TPU:16, one launch (start us, length us, event | category | flops | bytes accessed | tf_op | source)
XLA Modules:
  0.0 748.6 jit_solution(9253146166622665946)
XLA Ops:
  9.1 1.7 and_select_fusion.2
  12.0 6.3 while.162
  20.1 6.2 while.163
  27.0 1.6 multiply_convert_fusion.1
  28.5 2.1 collective-permute-start
  30.6 1.3 collective-permute-start.1
  32.6 6.4 while.160
  39.2 3.6 while.161
  42.9 6.0 while.164
  50.0 5.9 while.165
  56.9 2.6 while.166
  57.6 1.3 convolution_add_fusion.38
  60.5 2.6 while.167
  61.2 1.3 convolution_add_fusion.39
  63.1 1.4 fusion.57
  64.6 1.8 fusion.56
  67.5 180.7 %all-reduce.5.cloned.1.call-done = bf16[2,512,512]{2,1,0:T(8,128)(2,1)} async-done(((bf16[2,512,512]{2,1,0:T(8,128)(2,1)}), bf16[2,512,512]{2,1,0:T(8,128)(2,1)}) %all-reduce.5.cloned.1.call-update) | async-done | bytes 1048592 | tf_op jit(solution)/shard_map/psum | solution.py:122
  248.3 3.1 fusion.49
  251.4 65.3 %all-reduce.1 = (f32[]{:T(128)}, f32[]{:T(128)}) all-reduce(f32[]{:T(128)} %get-tuple-element.470, f32[]{:T(128)} %get-tuple-element.469), channel_id=1, replica_groups=mesh['op'=16,'sec'=32] {'sec'}, use_global_device_ids=true, to_apply=%region_1.2 | all-reduce | flops 2 | bytes 16 | tf_op jit(solution)/shard_map/psum | solution.py:127
  318.7 3.3 multiply_reduce_fusion.3
  321.9 60.6 %psum.59 = f32[]{:T(128)} all-reduce(f32[]{:T(128)} %get-tuple-element.638), channel_id=1, replica_groups=mesh['op'=16,'sec'=32] {'sec'}, use_global_device_ids=true, to_apply=%region_22.23 | all-reduce | flops 1 | bytes 8 | tf_op jit(solution)/shard_map/psum | solution.py:130
  382.5 4.1 multiply_reduce_fusion.2
  386.6 62.5 %psum.60 = f32[]{:T(128)} all-reduce(f32[]{:T(128)} %get-tuple-element.636), channel_id=1, replica_groups=mesh['op'=16,'sec'=32] {'sec'}, use_global_device_ids=true, to_apply=%region_24.25 | all-reduce | flops 1 | bytes 8 | tf_op jit(solution)/shard_map/psum | solution.py:130
  451.4 6.5 while.170
  452.0 1.3 convolution_add_fusion.42
  454.0 1.3 convolution_add_fusion.42
  455.9 1.3 convolution_add_fusion.42
  458.0 6.2 while.171
  464.2 1.6 multiply_convert_fusion
  465.8 2.1 collective-permute-start.2
  468.1 6.4 while.168
  468.7 1.2 convolution_add_fusion.40
  470.6 1.2 convolution_add_fusion.40
  472.6 1.2 convolution_add_fusion.40
  475.5 3.6 while.169
  479.1 1.3 collective-permute-start.3
  480.5 6.0 while.172
  486.7 3.2 while.173
  490.6 2.6 while.174
  491.3 1.3 convolution_add_fusion.46
  494.2 2.6 while.175
  494.9 1.3 convolution_add_fusion.47
  496.8 1.4 fusion.59
  498.3 1.8 fusion.58
  501.2 165.0 %all-reduce.7.cloned.1.call-done = bf16[2,512,512]{2,1,0:T(8,128)(2,1)} async-done(((bf16[2,512,512]{2,1,0:T(8,128)(2,1)}), bf16[2,512,512]{2,1,0:T(8,128)(2,1)}) %all-reduce.7.cloned.1.call-update) | async-done | bytes 1048592 | tf_op jit(solution)/shard_map/psum | solution.py:122
  666.2 3.9 multiply_reduce_fusion
  670.1 65.3 %all-reduce = (f32[]{:T(128)}, f32[]{:T(128)}) all-reduce(f32[]{:T(128)} %get-tuple-element.468, f32[]{:T(128)} %get-tuple-element.467), channel_id=1, replica_groups=mesh['op'=16,'sec'=32] {'sec'}, use_global_device_ids=true, to_apply=%region_43.44 | all-reduce | flops 2 | bytes 16 | tf_op jit(solution)/shard_map/psum | solution.py:127
  740.1 1.7 fusion.63
  (111 shorter events, 46.2 us)
Async XLA Ops:
  7.2 241.1 %all-reduce.5.cloned.1.call-start = ((), (), s32[]{:S(2)}) async-start(), calls=%async_computation | async-start | bytes 2097152 | tf_op jit(solution)/shard_map/psum | solution.py:122
  9.1 2.7 copy-start.11
  18.3 1.8 copy-start.4
  18.3 1.6 copy-start.12
  26.3 6.3 copy-start.5
  28.5 36.0 %collective-permute-start = (bf16[512,512]{1,0:T(8,128)(2,1)}, bf16[512,512]{1,0:T(8,128)(2,1)}, u32[]{:S(2)}, u32[]{:S(2)}) collective-permute-start(bf16[512,512]{1,0:T(8,128)(2,1)} %multiply_convert_fusion.1), channel_id=1, source_target_pairs={{0,1},{1,2},{2,3},{3,4},{4,5},{5,6},{6,7},{7,8},{8,9},{9,10},{10,1... | collective-permute-start | bytes 1572872 | tf_op jit(solution)/shard_map/ppermute | solution.py:10
  30.6 25.4 %collective-permute-start.1 = (bf16[512,512]{1,0:T(8,128)(2,1)}, bf16[512,512]{1,0:T(8,128)(2,1)}, u32[]{:S(2)}, u32[]{:S(2)}) collective-permute-start(bf16[512,512]{1,0:T(8,128)(2,1)} %get-tuple-element.1231), channel_id=1, source_target_pairs={{1,0},{2,1},{3,2},{4,3},{5,4},{6,5},{7,6},{8,7},{9,8},{10,9},{11,1... | collective-permute-start | bytes 1572872 | tf_op jit(solution)/shard_map/ppermute | solution.py:10
  49.0 1.1 copy-start.6
  56.0 0.8 copy-start.8
  66.4 181.9 %copy-start = (bf16[2,512,512]{2,1,0:T(8,128)(2,1)S(1)}, bf16[2,512,512]{2,1,0:T(8,128)(2,1)}, u32[]{:S(2)}) copy-start(bf16[2,512,512]{2,1,0:T(8,128)(2,1)} %param.39) | copy-start | bytes 3145732
  66.4 181.9 %copy-start.13 = (f32[2,512]{1,0:T(2,128)S(1)}, f32[2,512]{1,0:T(2,128)}, u32[]{:S(2)}) copy-start(f32[2,512]{1,0:T(2,128)} %param.43) | copy-start | bytes 12292
  66.4 181.9 %copy-start.14 = (f32[2,512]{1,0:T(2,128)S(1)}, f32[2,512]{1,0:T(2,128)}, u32[]{:S(2)}) copy-start(f32[2,512]{1,0:T(2,128)} %param.42) | copy-start | bytes 12292
  67.5 598.7 %all-reduce.7.cloned.1.call-start = ((), (), s32[]{:S(2)}) async-start(), calls=%async_computation.1 | async-start | bytes 2097152 | tf_op jit(solution)/shard_map/psum | solution.py:122
  248.3 70.4 %copy-start.10 = (bf16[2,512,512]{2,1,0:T(8,128)(2,1)S(1)}, bf16[2,512,512]{2,1,0:T(8,128)(2,1)}, u32[]{:S(2)}) copy-start(bf16[2,512,512]{2,1,0:T(8,128)(2,1)} %all-reduce.5.cloned.1.call-done) | copy-start | bytes 3145732
  386.6 64.7 %copy-start.2 = (f32[2,512,512]{2,1,0:T(8,128)}, f32[2,512,512]{2,1,0:T(8,128)S(1)}, u32[]{:S(2)}) copy-start(f32[2,512,512]{2,1,0:T(8,128)S(1)} %get-tuple-element.637) | copy-start | bytes 6291460
  464.2 3.8 copy-start.9
  465.8 32.4 %collective-permute-start.2 = (bf16[512,512]{1,0:T(8,128)(2,1)}, bf16[512,512]{1,0:T(8,128)(2,1)}, u32[]{:S(2)}, u32[]{:S(2)}) collective-permute-start(bf16[512,512]{1,0:T(8,128)(2,1)} %multiply_convert_fusion), channel_id=1, source_target_pairs={{0,1},{1,2},{2,3},{3,4},{4,5},{5,6},{6,7},{7,8},{8,9},{9,10},{10,1... | collective-permute-start | bytes 1572872 | tf_op jit(solution)/shard_map/ppermute | solution.py:10
  474.5 1.0 copy-start.7
  479.1 11.4 %collective-permute-start.3 = (bf16[512,512]{1,0:T(8,128)(2,1)}, bf16[512,512]{1,0:T(8,128)(2,1)}, u32[]{:S(2)}, u32[]{:S(2)}) collective-permute-start(bf16[512,512]{1,0:T(8,128)(2,1)} %get-tuple-element.1447), channel_id=1, source_target_pairs={{1,0},{2,1},{3,2},{4,3},{5,4},{6,5},{7,6},{8,7},{9,8},{10,9},{11,1... | collective-permute-start | bytes 1572872 | tf_op jit(solution)/shard_map/ppermute | solution.py:10
  500.0 166.1 %copy-start.1 = (bf16[2,512,512]{2,1,0:T(8,128)(2,1)S(1)}, bf16[2,512,512]{2,1,0:T(8,128)(2,1)}, u32[]{:S(2)}) copy-start(bf16[2,512,512]{2,1,0:T(8,128)(2,1)} %param.39) | copy-start | bytes 3145732
  500.1 166.1 %copy-start.3 = (f32[2,512,512]{2,1,0:T(8,128)S(1)}, f32[2,512,512]{2,1,0:T(8,128)}, u32[]{:S(2)}) copy-start(f32[2,512,512]{2,1,0:T(8,128)} %copy-done.2) | copy-start | bytes 6291460
Sparse Core Ops, SparseCore 0:
  67.6 180.5 all-reduce.4
  501.3 164.8 all-reduce.6
where the time goes:
time: 751 us; the launch traced here: 749 us
  waiting for transfers between devices  346 us (46%)
  blocking collectives  254 us (34%)
  matrix products  41.1 us (5%)
  other arithmetic  35.9 us (5%)
  loops' own time  35.5 us (5%)
  between operations  20.8 us (3%)
  local copies, waits for them, and re-layouts  8.6 us (1%)
    psum x2, waiting for transfers between devices, apply_operator(): lax.psum(partial_image.astype(jnp.bfloat16), 'op').astype(jnp.float32)  346 us
    psum x2, blocking collectives, paired_total(): return lax.psum((first_amount, second_amount), 'sec')  131 us
    psum x2, blocking collectives, single_total(): return lax.psum(amount, 'sec')  123 us
    dot_general x40, matrix products, accumulate(): lax.dot_general(first_piece, second_piece, (((first_axis,), (second_axis,...  41.1 us
    another operation x16, loops' own time, tile_product(): lax.fori_loop(0, tiles_used, accumulate, jnp.zeros((out_rows, out_columns...  35.5 us
  transfers between devices with their start and end apart: 6, of which 3 were waited for; matrix products, arithmetic and copies ran while one was open for 5% of the time, Pallas kernels for 0%

commit v1 on v0

v1 whole, which is shorter than its diff:
```python
import functools

import jax
import jax.numpy as jnp
from jax import lax
from jax.experimental import pallas as pl
from jax.experimental.pallas import tpu as pltpu
from jax.sharding import Mesh, PartitionSpec as P

F32 = jnp.float32
BF16 = jnp.bfloat16
OP = ("yh", "x", "c")
CHIPS = ("yh", "x")
SEC = ("yl", "z")
WIDTH = 512
ROWS = 32
HALF = 256
NCHIP = 8
BLOCKS = 3
PART = BLOCKS * ROWS + 16
VMEM_LIMIT = 48 * 1024 * 1024


def call(kernel, out_shape, in_specs, scratch=(), flops=0, nbytes=1 << 20):
    return pl.pallas_call(
        kernel,
        out_shape=out_shape,
        in_specs=in_specs,
        out_specs=jax.tree.map(lambda _: pl.BlockSpec(memory_space=pltpu.VMEM), out_shape),
        scratch_shapes=list(scratch),
        compiler_params=pltpu.CompilerParams(vmem_limit_bytes=VMEM_LIMIT),
        cost_estimate=pl.CostEstimate(flops=flops, bytes_accessed=nbytes, transcendentals=0),
    )


VM = pl.BlockSpec(memory_space=pltpu.VMEM)
SM = pl.BlockSpec(memory_space=pltpu.SMEM)


def product(first, second, second_axis=0):
    return lax.dot_general(
        first, second, (((1,), (second_axis,)), ((), ())), preferred_element_type=F32
    )


def group(chip, core):
    return pl.multiple_of((2 * chip + core) * ROWS, ROWS)


def total(array):
    return jnp.sum(jnp.sum(array, axis=0, keepdims=True), axis=1, keepdims=True)


def lanes(values, width):
    place = lax.broadcasted_iota(jnp.int32, (1, width), 1)
    row = jnp.zeros((1, width), F32)
    for index, value in enumerate(values):
        row = jnp.where(place == index, value, row)
    return row


def sort_kernel(place_ref, left_ref, keep_ref, send_ref, turned):
    core = place_ref[0]
    for sector in range(2):
        turned[...] = left_ref[0, sector].T
        for chip in range(NCHIP):
            here = pl.ds(chip * ROWS, ROWS)
            keep_ref[sector, here] = left_ref[0, sector, pl.ds(group(chip, core), ROWS)]
            send_ref[sector, here] = left_ref[0, sector, pl.ds(group(chip, 1 - core), ROWS)]
            keep_ref[2 + sector, here] = turned[pl.ds(group(chip, core), ROWS)]
            send_ref[2 + sector, here] = turned[pl.ds(group(chip, 1 - core), ROWS)]


def image_blocks(place_ref, spin_ref, keep_ref, other_ref, right_ref, swapped_ref, field):
    first = place_ref[2]
    blocks = [None, None, None]
    for sector in range(2):
        here = first + sector
        following = jnp.minimum(here + 1, spin_ref.shape[0] - 1)
        above = jnp.full((1, WIDTH), spin_ref[following], jnp.int32).astype(F32) + 1.0
        below = jnp.full((1, WIDTH), spin_ref[here], jnp.int32).astype(F32) + 1.0
        linked = jnp.full((1, WIDTH), here, jnp.int32) + 1 < spin_ref.shape[0]
        coupling = jnp.where(linked, jnp.sqrt(above / below), 0.0)
        lowered = raised = None
        for left, right in ((keep_ref, right_ref.at[0]), (other_ref, swapped_ref.at[0])):
            left_image = product(left[2 + sector], field[sector + 1]).astype(BF16)
            down = product(left_image, right[sector])
            left_product = product(left[sector], field[sector]).astype(BF16)
            up = product(left_product, right[sector], 1)
            lowered = down if lowered is None else lowered + down
            raised = up if raised is None else raised + up
        lowered = coupling * lowered
        blocks[sector] = lowered if blocks[sector] is None else blocks[sector] + lowered
        blocks[sector + 1] = coupling * raised
    return blocks


def put_parts(place_ref, blocks, field, scalars, parts_ref):
    core = place_ref[0]
    energy = jnp.zeros((ROWS, WIDTH), F32)
    for index, block in enumerate(blocks):
        rounded = block.astype(BF16)
        for chip in range(NCHIP):
            piece = rounded[chip * ROWS : (chip + 1) * ROWS]
            parts_ref[chip, index * ROWS : (index + 1) * ROWS] = piece
            own = field[index, pl.ds(group(chip, core), ROWS)]
            energy = energy + piece.astype(F32) * own.astype(F32)
    row = lanes([total(energy)], WIDTH) + scalars
    high = row.astype(BF16)
    rest = row - high.astype(F32)
    middle = rest.astype(BF16)
    low = (rest - middle.astype(F32)).astype(BF16)
    place = lax.broadcasted_iota(jnp.int32, (16, WIDTH), 0)
    coded = jnp.where(
        place == 0,
        high.astype(F32),
        jnp.where(place == 1, middle.astype(F32), jnp.where(place == 2, low.astype(F32), 0.0)),
    ).astype(BF16)
    for chip in range(NCHIP):
        parts_ref[chip, BLOCKS * ROWS :] = coded


def inside(size, first_row, shape):
    rows = lax.broadcasted_iota(jnp.int32, shape, 0) + first_row
    columns = lax.broadcasted_iota(jnp.int32, shape, 1)
    return (rows < size) & (columns < size)


def size_of(place_ref, size_ref, block):
    return size_ref[jnp.minimum(place_ref[2] + block, size_ref.shape[0] - 1)]


def first_kernel(
    place_ref, size_ref, spin_ref, start_ref, halo_ref, diagonal_ref,
    keep_ref, other_ref, right_ref, swapped_ref, parts_ref, rows_ref, field,
):
    for block in range(BLOCKS):
        source = halo_ref[...] if block == 2 else start_ref[block]
        mask = inside(size_of(place_ref, size_ref, block), 0, (WIDTH, WIDTH))
        field[block] = jnp.where(mask, source.astype(F32), 0.0).astype(BF16)
    norm = jnp.zeros((ROWS, WIDTH), F32)
    energy = jnp.zeros((ROWS, WIDTH), F32)
    for block in range(BLOCKS):
        own = field[block, pl.ds(group(place_ref[1], place_ref[0]), ROWS)].astype(F32)
        rows_ref[block] = own
        if block < 2:
            norm = norm + own * own
            energy = energy + diagonal_ref[block] * (own * own)
    blocks = image_blocks(place_ref, spin_ref, keep_ref, other_ref, right_ref, swapped_ref, field)
    put_parts(place_ref, blocks, field, lanes([total(energy), total(norm)], WIDTH), parts_ref)


def second_kernel(
    place_ref, spin_ref, near_ref, far_ref, scalar_ref,
    keep_ref, other_ref, right_ref, swapped_ref, parts_ref, field,
):
    core = place_ref[0]
    for chip in range(NCHIP):
        for block in range(BLOCKS):
            there = pl.ds(block * ROWS, ROWS)
            field[block, pl.ds(group(chip, core), ROWS)] = near_ref[chip, there]
            field[block, pl.ds(group(chip, 1 - core), ROWS)] = far_ref[chip, there]
    blocks = image_blocks(place_ref, spin_ref, keep_ref, other_ref, right_ref, swapped_ref, field)
    put_parts(place_ref, blocks, field, scalar_ref[...], parts_ref)


def sum_kernel(received_ref, first_ref, second_ref, leaving_ref, scalar_ref):
    for index, out_ref in enumerate((first_ref, second_ref, leaving_ref)):
        running = jnp.zeros((ROWS, WIDTH), F32)
        for chip in range(NCHIP):
            running = running + received_ref[chip, index * ROWS : (index + 1) * ROWS].astype(F32)
        out_ref[...] = running
    coded = jnp.zeros((16, WIDTH), F32)
    for chip in range(NCHIP):
        coded = coded + received_ref[chip, BLOCKS * ROWS :].astype(F32)
    row = jnp.sum(coded, axis=0, keepdims=True)[:, :128]
    scalar_ref[...] = jnp.broadcast_to(row[None], scalar_ref.shape)


def scalars_of(gathered_ref, count):
    row = jnp.sum(jnp.sum(gathered_ref[...], axis=0), axis=0, keepdims=True) * (
        1.0 / gathered_ref.shape[1]
    )
    return [row[:, index : index + 1] for index in range(count)]


def correction_kernel(
    place_ref, size_ref, gathered_ref, first_ref, second_ref, leaving_ref, arrived_ref,
    ahead_ref, diagonal_ref, rows_ref, spread_ref, image_ref, change_ref, scalar_ref, known_ref,
):
    energy, norm = scalars_of(gathered_ref, 2)
    rayleigh = energy / norm
    scale = jnp.sqrt(norm)
    first_row = group(place_ref[1], place_ref[0])
    sums = [first_ref[...] + arrived_ref[...], second_ref[...], leaving_ref[...] + ahead_ref[...]]
    amounts = [jnp.zeros((ROWS, WIDTH), F32) for _ in range(4)]
    for block in range(BLOCKS):
        mask = inside(size_of(place_ref, size_ref, block), first_row, (ROWS, WIDTH))
        values = rows_ref[block]
        diagonal = diagonal_ref[block]
        unit = values / scale
        image = jnp.where(mask, sums[block] + diagonal * values, 0.0) / scale
        residual = image - rayleigh * unit
        change = residual / (jnp.abs(diagonal - rayleigh) + 1.0)
        rounded = change.astype(BF16)
        for chip in range(NCHIP):
            spread_ref[chip, block * ROWS : (block + 1) * ROWS] = rounded
        if block < 2:
            image_ref[block] = image
            change_ref[block] = change
            again = rounded.astype(F32)
            amounts[0] = amounts[0] + diagonal * again * again
            amounts[1] = amounts[1] + unit * change
            amounts[2] = amounts[2] + change * change
            amounts[3] = amounts[3] + change * image
    scalar_ref[...] = lanes([total(amount) for amount in amounts], WIDTH)
    known_ref[...] = lanes([rayleigh, scale], 128)


def ritz_kernel(
    place_ref, size_ref, gathered_ref, known_ref, first_ref, second_ref, arrived_ref,
    diagonal_ref, rows_ref, image_ref, change_ref, vector_ref, residual_ref, energies_ref,
):
    change_energy, correlation, square, change_image = scalars_of(gathered_ref, 4)
    rayleigh = known_ref[:, 0:1]
    scale = known_ref[:, 1:2]
    spread = square - correlation * correlation
    deviation = jnp.sqrt(spread)
    cross_term = (change_image - correlation * rayleigh) / deviation
    second_energy = (
        change_energy - 2.0 * correlation * change_image + correlation * correlation * rayleigh
    ) / spread
    half_gap = 0.5 * (rayleigh - second_energy)
    length = jnp.sqrt(half_gap * half_gap + cross_term * cross_term)
    lowest = 0.5 * (rayleigh + second_energy) - length
    apart = length > 0.0
    divisor = jnp.where(apart, length, 1.0)
    double_cosine = jnp.where(apart, half_gap / divisor, 1.0)
    double_sine = jnp.where(apart, cross_term / divisor, 0.0)
    larger = jnp.sqrt(0.5 * (1.0 + jnp.abs(double_cosine)))
    smaller = 0.5 * double_sine / larger
    ahead = double_cosine >= 0.0
    sign = jnp.where(cross_term < 0.0, -1.0, 1.0)
    cosine_angle = jnp.where(ahead, larger, jnp.abs(smaller))
    sine_angle = jnp.where(ahead, smaller, sign * larger)
    first_row = group(place_ref[1], place_ref[0])
    sums = [first_ref[...] + arrived_ref[...], second_ref[...]]
    for block in range(2):
        mask = inside(size_of(place_ref, size_ref, block), first_row, (ROWS, WIDTH))
        unit = rows_ref[block] / scale
        image = image_ref[block]
        change = change_ref[block]
        rounded = change.astype(BF16).astype(F32)
        change_picture = jnp.where(mask, sums[block] + diagonal_ref[block] * rounded, 0.0)
        unit_second = (change - correlation * unit) / deviation
        second_image = (change_picture - correlation * image) / deviation
        ritz_unit = sine_angle * unit - cosine_angle * unit_second
        vector_ref[block] = (scale * ritz_unit).astype(BF16)
        residual_ref[block] = (
            scale * (sine_angle * image - cosine_angle * second_image - lowest * ritz_unit)
        ).astype(BF16)
    energies_ref[...] = lanes([rayleigh, lowest], 128)


def shaped(shape, dtype):
    return jax.ShapeDtypeStruct(shape, dtype)


def line(distance):
    devices = range(lax.axis_size(SEC))
    return [(i, i + distance) for i in devices if i + distance in devices]


def body(start, left, right, left_energy, right_energy, sector_size, sector_spin):
    core = lax.axis_index("c")
    chip = lax.axis_index(CHIPS)
    place = jnp.stack([core, chip, 2 * lax.axis_index(SEC)]).astype(jnp.int32)
    swap = [(0, 1), (1, 0)]
    halo = lax.ppermute(start[0], SEC, line(-1))
    levels = jnp.concatenate([left_energy[:1], right_energy[:1]]).reshape(8, 128)
    levels = lax.ppermute(levels, SEC, line(-1)).reshape(2, WIDTH)
    swapped = lax.ppermute(right, "c", swap)
    operators = shaped((4, HALF, WIDTH), BF16)
    keep, send = call(
        sort_kernel, (operators, operators), [SM, VM], [pltpu.VMEM((WIDTH, WIDTH), BF16)]
    )(place, left)
    other = lax.ppermute(send, "c", swap)
    left_levels = jnp.concatenate([left_energy, levels[:1]])
    right_levels = jnp.concatenate([right_energy, levels[1:]])
    own_levels = lax.dynamic_slice_in_dim(left_levels, (2 * chip + core) * ROWS, ROWS, 1)
    diagonal = own_levels[:, :, None] + right_levels[:, None, :]

    field = pltpu.VMEM((BLOCKS, WIDTH, WIDTH), BF16)
    parts_shape = shaped((NCHIP, PART, WIDTH), BF16)
    rows_shape = shaped((BLOCKS, ROWS, WIDTH), F32)
    own_shape = shaped((2, ROWS, WIDTH), F32)
    row_shape = shaped((ROWS, WIDTH), F32)
    many = lax.axis_size(("c",) + SEC)
    work = 32 * HALF * WIDTH * WIDTH

    def summed(parts):
        received = lax.all_to_all(parts, CHIPS, 0, 0)
        return call(
            sum_kernel, (row_shape, row_shape, row_shape, shaped((many, 8, 128), F32)), [VM]
        )(received)

    parts, rows = call(
        first_kernel, (parts_shape, rows_shape), [SM] * 3 + [VM] * 7, [field], work, 6 << 20
    )(place, sector_size, sector_spin, start, halo, diagonal, keep, other, right, swapped)
    first, second, leaving, scalars = summed(parts)
    gathered = lax.all_to_all(scalars, ("c",) + SEC, 0, 0)
    arrived = lax.ppermute(leaving, SEC, line(1))
    ahead = lax.ppermute(first, SEC, line(-1))
    spread, image, change, amounts, known = call(
        correction_kernel,
        (
            shaped((NCHIP, BLOCKS * ROWS, WIDTH), BF16), own_shape, own_shape,
            shaped((1, WIDTH), F32), shaped((1, 128), F32),
        ),
        [SM] * 2 + [VM] * 8,
    )(place, sector_size, gathered, first, second, leaving, arrived, ahead, diagonal, rows)
    near = lax.all_to_all(spread, CHIPS, 0, 0)
    far = lax.ppermute(near, "c", swap)
    parts = call(second_kernel, parts_shape, [SM] * 2 + [VM] * 7, [field], work, 6 << 20)(
        place, sector_spin, near, far, amounts, keep, other, right, swapped
    )
    first, second, leaving, scalars = summed(parts)
    gathered = lax.all_to_all(scalars, ("c",) + SEC, 0, 0)
    arrived = lax.ppermute(leaving, SEC, line(1))
    result = shaped((2, ROWS, WIDTH), BF16)
    vector, residual, energies = call(
        ritz_kernel, (result, result, shaped((1, 128), F32)), [SM] * 2 + [VM] * 9
    )(
        place, sector_size, gathered, known, first, second, arrived,
        diagonal, rows, image, change,
    )
    return vector, residual, energies[0, :2]


def solution(mesh):
    fine = Mesh(mesh.devices.reshape(2, 4, 2, 2, 16), ("yh", "x", "c", "yl", "z"))
    return jax.shard_map(
        body,
        mesh=fine,
        in_specs=(
            P(SEC, None, None),
            P(OP, SEC, None, None),
            P(OP, SEC, None, None),
            P(SEC, None),
            P(SEC, None),
            P(),
            P(),
        ),
        out_specs=(P(SEC, OP, None), P(SEC, OP, None), P()),
        check_vma=False,
    )
```

time: 751 us -> 172 us (0.23)
  the two profiles are of different devices: /device:TPU:16 before, /device:TPU:1 now
where the time goes in v1:
time: 172 us
  blocking collectives  50.6 us (29%)
  starting transfers between devices  50.3 us (29%)
  waiting for transfers between devices  49.1 us (29%)
  Pallas kernels  15.2 us (9%)
  local copies, waits for them, and re-layouts  5.45 us (3%)
    all_to_all x2, blocking collectives, summed(): received = lax.all_to_all(parts, CHIPS, 0, 0)  34.7 us
    all_to_all x2, starting transfers between devices, body(): gathered = lax.all_to_all(scalars, ('c',) + SEC, 0, 0)  24.2 us
    all_to_all x2, waiting for transfers between devices, body(): gathered = lax.all_to_all(scalars, ('c',) + SEC, 0, 0)  18.8 us
    all_to_all x1, blocking collectives, body(): near = lax.all_to_all(spread, CHIPS, 0, 0)  15.9 us
    ppermute x1, waiting for transfers between devices, body(): halo = lax.ppermute(start[0], SEC, line(-1))  12.7 us
    ppermute x1, starting transfers between devices, body(): swapped = lax.ppermute(right, 'c', swap)  8.79 us
    ppermute x1, waiting for transfers between devices, body(): ahead = lax.ppermute(first, SEC, line(-1))  8.44 us
    ppermute x2, starting transfers between devices, body(): arrived = lax.ppermute(leaving, SEC, line(1))  7.25 us
  transfers between devices with their start and end apart: 10, of which 7 were waited for; matrix products, arithmetic and copies ran while one was open for 1% of the time, Pallas kernels for 1%

profile of v1, /device:TPU:1, one launch (start us, length us, event | category | flops | bytes accessed | tf_op | source)
XLA Modules:
  0.0 171.7 jit_solution(15664465600835381142)
XLA Ops:
  0.6 8.8 %collective-permute-start.3 = (bf16[1,2,512,512]{3,2,1,0:T(8,128)(2,1)}, bf16[1,2,512,512]{3,2,1,0:T(8,128)(2,1)}, u32[]{:S(2)}, u32[]{:S(2)}) collective-permute-start(bf16[1,2,512,512]{3,2,1,0:T(8,128)(2,1)} %right_ref.3), channel_id=1, source_target_pairs={{0,32},{32,0},{1,33},{33,1},{2,34},{34,2},{3,35},{35,3},{4,36},{36... | collective-permute-start | bytes 3145736 | tf_op jit(solution)/shard_map/ppermute | solution.py:282
  9.4 0.0 slice-start
  9.4 0.0 slice-start.1
  9.5 0.1 pad_add_fusion.place_ref
  9.5 1.2 copy-done
  10.8 1.9 %shard_map.94 = (bf16[4,256,512]{2,1,0:T(8,128)(2,1)S(1)}, bf16[4,256,512]{2,1,0:T(8,128)(2,1)}) custom-call(s32[3]{0:T(128)S(1)} %pad_add_fusion.place_ref, bf16[1,2,512,512]{3,2,1,0:T(8,128)(2,1)S(1)} %copy-done), custom_call_target="tpu_custom_call" | custom-call | bytes 1048576 | tf_op jit(solution)/shard_map/pallas_call | solution.py:284
  12.7 1.0 copy-done.4
  13.7 1.9 %collective-permute-start.2 = (bf16[4,256,512]{2,1,0:T(8,128)(2,1)}, bf16[4,256,512]{2,1,0:T(8,128)(2,1)}, u32[]{:S(2)}, u32[]{:S(2)}) collective-permute-start(bf16[4,256,512]{2,1,0:T(8,128)(2,1)} %get-tuple-element.24), channel_id=1, source_target_pairs={{0,32},{32,0},{1,33},{33,1},{2,34},{34,2},{3,35},{35,3},{4,36},{36... | collective-permute-start | bytes 3145736 | tf_op jit(solution)/shard_map/ppermute | solution.py:287
  15.6 0.0 slice-done
  15.6 0.0 slice-done.1
  15.6 1.3 collective-permute-start.1
  16.9 0.0 copy-done.1
  16.9 0.8 slice_bitcast_fusion
  17.8 1.3 collective-permute-start
  19.1 0.0 copy-start.9
  19.1 0.9 collective-permute-done.1
  20.0 0.0 copy-done.9
  20.0 0.1 fusion
  20.1 0.6 copy-done.8
  20.7 0.1 broadcast_add_fusion.diagonal_ref
  20.8 0.0 copy-start.2
  20.8 0.0 copy-start.7
  20.8 12.7 %collective-permute-done.halo_ref = bf16[512,512]{1,0:T(8,128)(2,1)S(1)} collective-permute-done((bf16[512,512]{1,0:T(8,128)(2,1)}, bf16[512,512]{1,0:T(8,128)(2,1)S(1)}, u32[]{:S(2)}, u32[]{:S(2)}) %collective-permute-start) | collective-permute-done | bytes 524320 | tf_op jit(solution)/shard_map/ppermute | solution.py:279
  33.5 0.0 collective-permute-done.3.swapped_ref
  33.5 0.0 collective-permute-done.2.other_ref
  33.5 1.2 copy-done.5
  34.7 4.7 %shard_map.95 = (bf16[8,112,512]{2,1,0:T(8,128)(2,1)S(1)}, f32[3,32,512]{2,1,0:T(8,128)S(1)}) custom-call(s32[3]{0:T(128)S(1)} %pad_add_fusion.place_ref, s32[64]{0:T(128)S(1)} %copy-done.2, s32[64]{0:T(128)S(1)} %copy-done.7, bf16[2,512,512]{2,1,0:T(8,128)(2,1)S(1)} %copy-done.1, bf16[512,512]{1,0:T(8,128)(2,1)S(1)} %collective-permute-done.halo_ref, ...), custom_call_target="tpu_custom_call" | custom-call | flops 2147483648 | bytes 6291456 | tf_op jit(solution)/shard_map/pallas_call | solution.py:307
  39.5 16.6 %all_to_all.25.received_ref = bf16[8,112,512]{2,1,0:T(8,128)(2,1)S(1)} all-to-all(bf16[8,112,512]{2,1,0:T(8,128)(2,1)S(1)} %get-tuple-element.25), channel_id=1, replica_groups=mesh['yh'=2,'x'=4,'c'=2,'yl'=2,'z'=16] {'yh','x'}, dimensions={0} | all-to-all | bytes 1835008 | tf_op jit(solution)/shard_map/all_to_all | solution.py:302
  56.1 0.7 shard_map.96
  56.8 17.3 %all-to-all-start.1 = ((f32[64,8,128]{2,1,0:T(8,128)}), f32[64,8,128]{2,1,0:T(8,128)S(1)}, u32[]{:S(2)}, u32[]{:S(2)}) async-start(f32[64,8,128]{2,1,0:T(8,128)} %get-tuple-element.26), calls=%async_computation.1 | async-start | bytes 524288 | tf_op jit(solution)/shard_map/all_to_all | solution.py:311
  74.2 1.3 collective-permute-start.5
  75.5 4.0 %collective-permute-start.4 = (f32[32,512]{1,0:T(8,128)S(1)}, f32[32,512]{1,0:T(8,128)S(1)}, u32[]{:S(2)}, u32[]{:S(2)}) collective-permute-start(f32[32,512]{1,0:T(8,128)S(1)} %get-tuple-element.29.leaving_ref), channel_id=1, source_target_pairs={{0,1},{1,2},{2,3},{3,4},{4,5},{5,6},{6,7},{7,8},{8,9},{9,10},{10,1... | collective-permute-start | bytes 196616 | tf_op jit(solution)/shard_map/ppermute | solution.py:312
  79.5 8.4 %collective-permute-done.5.ahead_ref = f32[32,512]{1,0:T(8,128)S(1)} collective-permute-done((f32[32,512]{1,0:T(8,128)S(1)}, f32[32,512]{1,0:T(8,128)S(1)}, u32[]{:S(2)}, u32[]{:S(2)}) %collective-permute-start.5) | collective-permute-done | bytes 65568 | tf_op jit(solution)/shard_map/ppermute | solution.py:313
  87.9 0.0 collective-permute-done.4.arrived_ref
  87.9 7.4 %all-to-all-done.1.gathered_ref = f32[64,8,128]{2,1,0:T(8,128)S(1)} async-done(((f32[64,8,128]{2,1,0:T(8,128)}), f32[64,8,128]{2,1,0:T(8,128)S(1)}, u32[]{:S(2)}, u32[]{:S(2)}) %all-to-all-start.1) | async-done | bytes 262176 | tf_op jit(solution)/shard_map/all_to_all | solution.py:311
  95.3 0.9 shard_map.97
  96.2 15.9 %all_to_all.26.near_ref = bf16[8,96,512]{2,1,0:T(8,128)(2,1)S(1)} all-to-all(bf16[8,96,512]{2,1,0:T(8,128)(2,1)S(1)} %get-tuple-element.31), channel_id=1, replica_groups=mesh['yh'=2,'x'=4,'c'=2,'yl'=2,'z'=16] {'yh','x'}, dimensions={0} | all-to-all | bytes 1572864 | tf_op jit(solution)/shard_map/all_to_all | solution.py:322
  112.1 4.2 %collective-permute-start.6 = (bf16[8,96,512]{2,1,0:T(8,128)(2,1)S(1)}, bf16[8,96,512]{2,1,0:T(8,128)(2,1)S(1)}, u32[]{:S(2)}, u32[]{:S(2)}) collective-permute-start(bf16[8,96,512]{2,1,0:T(8,128)(2,1)S(1)} %all_to_all.26.near_ref), channel_id=1, source_target_pairs={{0,32},{32,0},{1,33},{33,1},{2,34},{34,2},{3,35},{35,3},{4,36},{36... | collective-permute-start | bytes 2359304 | tf_op jit(solution)/shard_map/ppermute | solution.py:323
  116.3 1.9 %collective-permute-done.6.far_ref = bf16[8,96,512]{2,1,0:T(8,128)(2,1)S(1)} collective-permute-done((bf16[8,96,512]{2,1,0:T(8,128)(2,1)S(1)}, bf16[8,96,512]{2,1,0:T(8,128)(2,1)S(1)}, u32[]{:S(2)}, u32[]{:S(2)}) %collective-permute-start.6) | collective-permute-done | bytes 786464 | tf_op jit(solution)/shard_map/ppermute | solution.py:323
  118.2 4.5 %shard_map.98 = bf16[8,112,512]{2,1,0:T(8,128)(2,1)S(1)} custom-call(s32[3]{0:T(128)S(1)} %pad_add_fusion.place_ref, s32[64]{0:T(128)S(1)} %copy-done.7, bf16[8,96,512]{2,1,0:T(8,128)(2,1)S(1)} %all_to_all.26.near_ref, bf16[8,96,512]{2,1,0:T(8,128)(2,1)S(1)} %collective-permute-done.6.far_ref, f32[1,512]{1,0:T(1,128)S(1)} %get-tuple-element.32.scalar_ref, ...), custom_call_target="tpu_custom_call" | custom-call | flops 2147483648 | bytes 6291456 | tf_op jit(solution)/shard_map/pallas_call | solution.py:324
  122.7 18.0 %all_to_all.27.received_ref = bf16[8,112,512]{2,1,0:T(8,128)(2,1)S(1)} all-to-all(bf16[8,112,512]{2,1,0:T(8,128)(2,1)S(1)} %shard_map.98), channel_id=1, replica_groups=mesh['yh'=2,'x'=4,'c'=2,'yl'=2,'z'=16] {'yh','x'}, dimensions={0} | all-to-all | bytes 1835008 | tf_op jit(solution)/shard_map/all_to_all | solution.py:302
  140.7 0.7 shard_map.99
  141.4 6.9 %all-to-all-start.4 = ((f32[64,8,128]{2,1,0:T(8,128)}), f32[64,8,128]{2,1,0:T(8,128)S(1)}, u32[]{:S(2)}, u32[]{:S(2)}) async-start(f32[64,8,128]{2,1,0:T(8,128)} %get-tuple-element.33), calls=%async_computation.4 | async-start | bytes 524288 | tf_op jit(solution)/shard_map/all_to_all | solution.py:328
  148.3 3.3 %collective-permute-start.7 = (f32[32,512]{1,0:T(8,128)S(1)}, f32[32,512]{1,0:T(8,128)S(1)}, u32[]{:S(2)}, u32[]{:S(2)}) collective-permute-start(f32[32,512]{1,0:T(8,128)S(1)} %get-tuple-element.37), channel_id=1, source_target_pairs={{0,1},{1,2},{2,3},{3,4},{4,5},{5,6},{6,7},{7,8},{8,9},{9,10},{10,1... | collective-permute-start | bytes 196616 | tf_op jit(solution)/shard_map/ppermute | solution.py:329
  151.6 6.4 %collective-permute-done.7.arrived_ref = f32[32,512]{1,0:T(8,128)S(1)} collective-permute-done((f32[32,512]{1,0:T(8,128)S(1)}, f32[32,512]{1,0:T(8,128)S(1)}, u32[]{:S(2)}, u32[]{:S(2)}) %collective-permute-start.7) | collective-permute-done | bytes 65568 | tf_op jit(solution)/shard_map/ppermute | solution.py:329
  158.0 11.5 %all-to-all-done.4.gathered_ref = f32[64,8,128]{2,1,0:T(8,128)S(1)} async-done(((f32[64,8,128]{2,1,0:T(8,128)}), f32[64,8,128]{2,1,0:T(8,128)S(1)}, u32[]{:S(2)}, u32[]{:S(2)}) %all-to-all-start.4) | async-done | bytes 262176 | tf_op jit(solution)/shard_map/all_to_all | solution.py:328
  169.4 1.8 %shard_map.100 = (bf16[2,32,512]{2,1,0:T(8,128)(2,1)}, bf16[2,32,512]{2,1,0:T(8,128)(2,1)}, f32[1,128]{1,0:T(1,128)S(1)}) custom-call(s32[3]{0:T(128)S(1)} %pad_add_fusion.place_ref, s32[64]{0:T(128)S(1)} %copy-done.2, f32[64,8,128]{2,1,0:T(8,128)S(1)} %all-to-all-done.4.gathered_ref, f32[1,128]{1,0:T(1,128)S(1)} %get-tuple-element.34.known_ref, ...), custom_call_target="tpu_custom_call" | custom-call | bytes 1048576 | tf_op jit(solution)/shard_map/pallas_call | solution.py:331
  171.2 0.5 slice_bitcast_fusion.1
  (15 shorter events, 0.1 us)
Async XLA Ops:
  0.6 32.9 %collective-permute-start.3 = (bf16[1,2,512,512]{3,2,1,0:T(8,128)(2,1)}, bf16[1,2,512,512]{3,2,1,0:T(8,128)(2,1)}, u32[]{:S(2)}, u32[]{:S(2)}) collective-permute-start(bf16[1,2,512,512]{3,2,1,0:T(8,128)(2,1)} %right_ref.3), channel_id=1, source_target_pairs={{0,32},{32,0},{1,33},{33,1},{2,34},{34,2},{3,35},{35,3},{4,36},{36... | collective-permute-start | bytes 3145736 | tf_op jit(solution)/shard_map/ppermute | solution.py:282
  9.4 6.1 %slice-start = ((f32[2,512]{1,0:T(2,128)}), f32[1,512]{1,0:T(1,128)S(1)}, s32[]{:S(2)}) async-start(f32[2,512]{1,0:T(2,128)} %param.11), calls=%async_computation.5 | async-start | bytes 4096 | tf_op jit(solution)/shard_map/slice | solution.py:280
  9.4 6.1 %slice-start.1 = ((f32[2,512]{1,0:T(2,128)}), f32[1,512]{1,0:T(1,128)S(1)}, s32[]{:S(2)}) async-start(f32[2,512]{1,0:T(2,128)} %param.10), calls=%async_computation.6 | async-start | bytes 4096 | tf_op jit(solution)/shard_map/slice | solution.py:280
  9.5 1.2 copy-start
  10.8 6.2 %copy-start.1 = (bf16[2,512,512]{2,1,0:T(8,128)(2,1)S(1)}, bf16[2,512,512]{2,1,0:T(8,128)(2,1)}, u32[]{:S(2)}) copy-start(bf16[2,512,512]{2,1,0:T(8,128)(2,1)} %start_ref.1) | copy-start | bytes 3145732
  10.8 22.7 %copy-start.3 = (bf16[1,2,512,512]{3,2,1,0:T(8,128)(2,1)S(1)}, bf16[1,2,512,512]{3,2,1,0:T(8,128)(2,1)}, u32[]{:S(2)}) copy-start(bf16[1,2,512,512]{3,2,1,0:T(8,128)(2,1)} %right_ref.3) | copy-start | bytes 3145732
  12.7 1.0 copy-start.4
  13.7 19.8 %collective-permute-start.2 = (bf16[4,256,512]{2,1,0:T(8,128)(2,1)}, bf16[4,256,512]{2,1,0:T(8,128)(2,1)}, u32[]{:S(2)}, u32[]{:S(2)}) collective-permute-start(bf16[4,256,512]{2,1,0:T(8,128)(2,1)} %get-tuple-element.24), channel_id=1, source_target_pairs={{0,32},{32,0},{1,33},{33,1},{2,34},{34,2},{3,35},{35,3},{4,36},{36... | collective-permute-start | bytes 3145736 | tf_op jit(solution)/shard_map/ppermute | solution.py:287
  15.6 4.4 %collective-permute-start.1 = (f32[8,128]{1,0:T(8,128)S(1)}, f32[8,128]{1,0:T(8,128)S(1)}, u32[]{:S(2)}, u32[]{:S(2)}) collective-permute-start(f32[8,128]{1,0:T(8,128)S(1)} %reshape.14), channel_id=1, source_target_pairs={{1,0},{2,1},{3,2},{4,3},{5,4},{6,5},{7,6},{8,7},{9,8},{10,9},{11,1... | collective-permute-start | bytes 12296 | tf_op jit(solution)/shard_map/ppermute | solution.py:281
  17.8 15.7 %collective-permute-start = (bf16[512,512]{1,0:T(8,128)(2,1)}, bf16[512,512]{1,0:T(8,128)(2,1)S(1)}, u32[]{:S(2)}, u32[]{:S(2)}) collective-permute-start(bf16[512,512]{1,0:T(8,128)(2,1)} %slice_bitcast_fusion), channel_id=1, source_target_pairs={{1,0},{2,1},{3,2},{4,3},{5,4},{6,5},{7,6},{8,7},{9,8},{10,9},{11,1... | collective-permute-start | bytes 1572872 | tf_op jit(solution)/shard_map/ppermute | solution.py:279
  19.1 0.9 copy-start.9
  20.0 0.7 copy-start.8
  20.8 12.7 %copy-start.2 = (s32[64]{0:T(128)S(1)}, s32[64]{0:T(128)}, u32[]{:S(2)}) copy-start(s32[64]{0:T(128)} %size_ref.5) | copy-start | bytes 772
  20.8 12.7 %copy-start.7 = (s32[64]{0:T(128)S(1)}, s32[64]{0:T(128)}, u32[]{:S(2)}) copy-start(s32[64]{0:T(128)} %spin_ref.3) | copy-start | bytes 772
  33.5 1.2 copy-start.5
  56.8 38.4 %all-to-all-start.1 = ((f32[64,8,128]{2,1,0:T(8,128)}), f32[64,8,128]{2,1,0:T(8,128)S(1)}, u32[]{:S(2)}, u32[]{:S(2)}) async-start(f32[64,8,128]{2,1,0:T(8,128)} %get-tuple-element.26), calls=%async_computation.1 | async-start | bytes 524288 | tf_op jit(solution)/shard_map/all_to_all | solution.py:311
  74.2 13.7 %collective-permute-start.5 = (f32[32,512]{1,0:T(8,128)S(1)}, f32[32,512]{1,0:T(8,128)S(1)}, u32[]{:S(2)}, u32[]{:S(2)}) collective-permute-start(f32[32,512]{1,0:T(8,128)S(1)} %get-tuple-element.27.first_ref), channel_id=1, source_target_pairs={{1,0},{2,1},{3,2},{4,3},{5,4},{6,5},{7,6},{8,7},{9,8},{10,9},{11,1... | collective-permute-start | bytes 196616 | tf_op jit(solution)/shard_map/ppermute | solution.py:313
  75.5 12.4 %collective-permute-start.4 = (f32[32,512]{1,0:T(8,128)S(1)}, f32[32,512]{1,0:T(8,128)S(1)}, u32[]{:S(2)}, u32[]{:S(2)}) collective-permute-start(f32[32,512]{1,0:T(8,128)S(1)} %get-tuple-element.29.leaving_ref), channel_id=1, source_target_pairs={{0,1},{1,2},{2,3},{3,4},{4,5},{5,6},{6,7},{7,8},{8,9},{9,10},{10,1... | collective-permute-start | bytes 196616 | tf_op jit(solution)/shard_map/ppermute | solution.py:312
  95.3 22.9 %copy-start.6 = (bf16[4,256,512]{2,1,0:T(8,128)(2,1)S(1)}, bf16[4,256,512]{2,1,0:T(8,128)(2,1)}, u32[]{:S(2)}) copy-start(bf16[4,256,512]{2,1,0:T(8,128)(2,1)} %copy-done.4) | copy-start | bytes 3145732
  112.1 6.1 %collective-permute-start.6 = (bf16[8,96,512]{2,1,0:T(8,128)(2,1)S(1)}, bf16[8,96,512]{2,1,0:T(8,128)(2,1)S(1)}, u32[]{:S(2)}, u32[]{:S(2)}) collective-permute-start(bf16[8,96,512]{2,1,0:T(8,128)(2,1)S(1)} %all_to_all.26.near_ref), channel_id=1, source_target_pairs={{0,32},{32,0},{1,33},{33,1},{2,34},{34,2},{3,35},{35,3},{4,36},{36... | collective-permute-start | bytes 2359304 | tf_op jit(solution)/shard_map/ppermute | solution.py:323
  141.4 28.0 %all-to-all-start.4 = ((f32[64,8,128]{2,1,0:T(8,128)}), f32[64,8,128]{2,1,0:T(8,128)S(1)}, u32[]{:S(2)}, u32[]{:S(2)}) async-start(f32[64,8,128]{2,1,0:T(8,128)} %get-tuple-element.33), calls=%async_computation.4 | async-start | bytes 524288 | tf_op jit(solution)/shard_map/all_to_all | solution.py:328
  148.3 9.6 %collective-permute-start.7 = (f32[32,512]{1,0:T(8,128)S(1)}, f32[32,512]{1,0:T(8,128)S(1)}, u32[]{:S(2)}, u32[]{:S(2)}) collective-permute-start(f32[32,512]{1,0:T(8,128)S(1)} %get-tuple-element.37), channel_id=1, source_target_pairs={{0,1},{1,2},{2,3},{3,4},{4,5},{5,6},{6,7},{7,8},{8,9},{9,10},{10,1... | collective-permute-start | bytes 196616 | tf_op jit(solution)/shard_map/ppermute | solution.py:329

commit v2 on v1

--- a/solution.py
+++ b/solution.py
@@ -130,14 +130,17 @@
     return size_ref[jnp.minimum(place_ref[2] + block, size_ref.shape[0] - 1)]
 
 
-def first_kernel(
-    place_ref, size_ref, spin_ref, start_ref, halo_ref, diagonal_ref,
-    keep_ref, other_ref, right_ref, swapped_ref, parts_ref, rows_ref, field,
-):
+def mask_kernel(place_ref, size_ref, start_ref, halo_ref, field_ref):
     for block in range(BLOCKS):
         source = halo_ref[...] if block == 2 else start_ref[block]
         mask = inside(size_of(place_ref, size_ref, block), 0, (WIDTH, WIDTH))
-        field[block] = jnp.where(mask, source.astype(F32), 0.0).astype(BF16)
+        field_ref[block] = jnp.where(mask, source.astype(F32), 0.0).astype(BF16)
+
+
+def first_kernel(
+    place_ref, spin_ref, field, diagonal_ref,
+    keep_ref, other_ref, right_ref, swapped_ref, parts_ref, rows_ref,
+):
     norm = jnp.zeros((ROWS, WIDTH), F32)
     energy = jnp.zeros((ROWS, WIDTH), F32)
     for block in range(BLOCKS):
@@ -178,15 +181,13 @@
 
 
 def scalars_of(gathered_ref, count):
-    row = jnp.sum(jnp.sum(gathered_ref[...], axis=0), axis=0, keepdims=True) * (
-        1.0 / gathered_ref.shape[1]
-    )
+    row = jnp.sum(gathered_ref[...], axis=0)
     return [row[:, index : index + 1] for index in range(count)]
 
 
 def correction_kernel(
     place_ref, size_ref, gathered_ref, first_ref, second_ref, leaving_ref, arrived_ref,
-    ahead_ref, diagonal_ref, rows_ref, spread_ref, image_ref, change_ref, scalar_ref, known_ref,
+    ahead_ref, diagonal_ref, next_ref, rows_ref, spread_ref, image_ref, change_ref, scalar_ref, known_ref,
 ):
     energy, norm = scalars_of(gathered_ref, 2)
     rayleigh = energy / norm
@@ -197,7 +198,7 @@
     for block in range(BLOCKS):
         mask = inside(size_of(place_ref, size_ref, block), first_row, (ROWS, WIDTH))
         values = rows_ref[block]
-        diagonal = diagonal_ref[block]
+        diagonal = next_ref[...] if block == 2 else diagonal_ref[block]
         unit = values / scale
         image = jnp.where(mask, sums[block] + diagonal * values, 0.0) / scale
         residual = image - rayleigh * unit
@@ -279,16 +280,20 @@
     halo = lax.ppermute(start[0], SEC, line(-1))
     levels = jnp.concatenate([left_energy[:1], right_energy[:1]]).reshape(8, 128)
     levels = lax.ppermute(levels, SEC, line(-1)).reshape(2, WIDTH)
+    first_row = (2 * chip + core) * ROWS
+
+    def diagonal_rows(left_levels, right_levels):
+        own_levels = lax.dynamic_slice_in_dim(left_levels, first_row, ROWS, 1)
+        return own_levels[:, :, None] + right_levels[:, None, :]
+
     swapped = lax.ppermute(right, "c", swap)
     operators = shaped((4, HALF, WIDTH), BF16)
     keep, send = call(
         sort_kernel, (operators, operators), [SM, VM], [pltpu.VMEM((WIDTH, WIDTH), BF16)]
     )(place, left)
     other = lax.ppermute(send, "c", swap)
-    left_levels = jnp.concatenate([left_energy, levels[:1]])
-    right_levels = jnp.concatenate([right_energy, levels[1:]])
-    own_levels = lax.dynamic_slice_in_dim(left_levels, (2 * chip + core) * ROWS, ROWS, 1)
-    diagonal = own_levels[:, :, None] + right_levels[:, None, :]
+    diagonal = diagonal_rows(left_energy, right_energy)
+    next_diagonal = diagonal_rows(levels[:1], levels[1:])[0]
 
     field = pltpu.VMEM((BLOCKS, WIDTH, WIDTH), BF16)
     parts_shape = shaped((NCHIP, PART, WIDTH), BF16)
@@ -301,12 +306,15 @@
     def summed(parts):
         received = lax.all_to_all(parts, CHIPS, 0, 0)
         return call(
-            sum_kernel, (row_shape, row_shape, row_shape, shaped((many, 8, 128), F32)), [VM]
+            sum_kernel, (row_shape, row_shape, row_shape, shaped((many, 1, 128), F32)), [VM]
         )(received)
 
+    masked = call(
+        mask_kernel, shaped((BLOCKS, WIDTH, WIDTH), BF16), [SM] * 2 + [VM] * 2, (), 4 * work, 3 << 20
+    )(place, sector_size, start, halo)
     parts, rows = call(
-        first_kernel, (parts_shape, rows_shape), [SM] * 3 + [VM] * 7, [field], work, 6 << 20
-    )(place, sector_size, sector_spin, start, halo, diagonal, keep, other, right, swapped)
+        first_kernel, (parts_shape, rows_shape), [SM] * 2 + [VM] * 6, (), work, 6 << 20
+    )(place, sector_spin, masked, diagonal, keep, other, right, swapped)
     first, second, leaving, scalars = summed(parts)
     gathered = lax.all_to_all(scalars, ("c",) + SEC, 0, 0)
     arrived = lax.ppermute(leaving, SEC, line(1))
@@ -317,8 +325,11 @@
             shaped((NCHIP, BLOCKS * ROWS, WIDTH), BF16), own_shape, own_shape,
             shaped((1, WIDTH), F32), shaped((1, 128), F32),
         ),
-        [SM] * 2 + [VM] * 8,
-    )(place, sector_size, gathered, first, second, leaving, arrived, ahead, diagonal, rows)
+        [SM] * 2 + [VM] * 9,
+    )(
+        place, sector_size, gathered, first, second, leaving, arrived, ahead,
+        diagonal, next_diagonal, rows,
+    )
     near = lax.all_to_all(spread, CHIPS, 0, 0)
     far = lax.ppermute(near, "c", swap)
     parts = call(second_kernel, parts_shape, [SM] * 2 + [VM] * 7, [field], work, 6 << 20)(

time: 172 us -> 152 us (0.88)
  waiting for transfers between devices: 49.1 us -> 32.3 us
  blocking collectives: 50.6 us -> 34 us
  starting transfers between devices: 50.3 us -> 60 us
  Pallas kernels: 15.2 us -> 17.9 us
    all_to_all x2 -> x1, blocking collectives: 34.7 us -> 18 us  [summed(): received = lax.all_to_all(parts, CHIPS, 0, 0)]
    ppermute x1, waiting for transfers between devices: 12.7 us -> 0.01 us  [body(): halo = lax.ppermute(start[0], SEC, line(-1))]
    all_to_all x0 -> x1, waiting for transfers between devices: none -> 11.2 us  [summed(): received = lax.all_to_all(parts, CHIPS, 0, 0)]
    ppermute x1, waiting for transfers between devices: 8.44 us -> 0.11 us  [body(): ahead = lax.ppermute(first, SEC, line(-1))]
    all_to_all x0 -> x1, starting transfers between devices: none -> 7.63 us  [summed(): received = lax.all_to_all(parts, CHIPS, 0, 0)]
    all_to_all x2, waiting for transfers between devices: 18.8 us -> 13.3 us  [body(): gathered = lax.all_to_all(scalars, ('c',) + SEC, 0, 0)]
    ppermute x2, waiting for transfers between devices: 6.37 us -> 2.49 us  [body(): arrived = lax.ppermute(leaving, SEC, line(1))]
    pallas_call x3 -> x4, Pallas kernels: 6.18 us -> 8.76 us  [the longest x1 5.84 us: body(): call(first_kernel, (parts_shape, rows_shape), [SM] * 2 + [VM] * 6, (), wo...]
  transfers between devices with their start and end apart: 10 -> 11, of which waited for: 7 -> 8; matrix products, arithmetic and copies ran while one was open for 1% -> 0% of each run, Pallas kernels for 1% -> 2%
where the time goes in v2:
time: 152 us; the launch traced here: 151 us
  starting transfers between devices  60 us (39%)
  blocking collectives  34 us (22%)
  waiting for transfers between devices  32.3 us (21%)
  Pallas kernels  17.9 us (12%)
  local copies, waits for them, and re-layouts  6.09 us (4%)
    all_to_all x2, starting transfers between devices, body(): gathered = lax.all_to_all(scalars, ('c',) + SEC, 0, 0)  26.5 us
    all_to_all x1, blocking collectives, summed(): received = lax.all_to_all(parts, CHIPS, 0, 0)  18 us
    all_to_all x1, blocking collectives, body(): near = lax.all_to_all(spread, CHIPS, 0, 0)  16 us
    all_to_all x2, waiting for transfers between devices, body(): gathered = lax.all_to_all(scalars, ('c',) + SEC, 0, 0)  13.3 us
    all_to_all x1, waiting for transfers between devices, summed(): received = lax.all_to_all(parts, CHIPS, 0, 0)  11.2 us
    ppermute x1, starting transfers between devices, body(): swapped = lax.ppermute(right, 'c', swap)  8.79 us
    all_to_all x1, starting transfers between devices, summed(): received = lax.all_to_all(parts, CHIPS, 0, 0)  7.63 us
    ppermute x2, starting transfers between devices, body(): arrived = lax.ppermute(leaving, SEC, line(1))  7.25 us
  transfers between devices with their start and end apart: 11, of which 8 were waited for; matrix products, arithmetic and copies ran while one was open for 0% of the time, Pallas kernels for 2%

profile of v2, /device:TPU:1, one launch (start us, length us, event | category | flops | bytes accessed | tf_op | source)
XLA Modules:
  0.0 151.4 jit_solution(1999179569532075015)
XLA Ops:
  0.6 0.0 copy-start
  0.6 0.0 copy-start.1
  0.7 0.0 copy-start.10
  0.7 0.0 copy-start.9
  0.7 2.0 %slice_bitcast_fusion = bf16[512,512]{1,0:T(8,128)(2,1)} fusion(bf16[2,512,512]{2,1,0:T(8,128)(2,1)} %start_ref.1), kind=kLoop, calls=%fused_computation | loop fusion | bytes 1048576 | tf_op jit(solution)/shard_map/squeeze | solution.py:280
  2.7 1.3 collective-permute-start
  4.0 8.8 %collective-permute-start.2 = (bf16[1,2,512,512]{3,2,1,0:T(8,128)(2,1)}, bf16[1,2,512,512]{3,2,1,0:T(8,128)(2,1)}, u32[]{:S(2)}, u32[]{:S(2)}) collective-permute-start(bf16[1,2,512,512]{3,2,1,0:T(8,128)(2,1)} %right_ref.3), channel_id=1, source_target_pairs={{0,32},{32,0},{1,33},{33,1},{2,34},{34,2},{3,35},{35,3},{4,36},{36... | collective-permute-start | bytes 3145736 | tf_op jit(solution)/shard_map/ppermute | solution.py:289
  12.8 0.1 pad_add_fusion.place_ref
  12.9 1.9 %shard_map.95 = (bf16[4,256,512]{2,1,0:T(8,128)(2,1)S(1)}, bf16[4,256,512]{2,1,0:T(8,128)(2,1)}) custom-call(s32[3]{0:T(128)S(1)} %pad_add_fusion.place_ref, bf16[1,2,512,512]{3,2,1,0:T(8,128)(2,1)S(1)} %copy-done), custom_call_target="tpu_custom_call" | custom-call | bytes 1048576 | tf_op jit(solution)/shard_map/pallas_call | solution.py:291
  14.8 1.0 copy-done.4
  15.7 1.9 %collective-permute-start.1 = (bf16[4,256,512]{2,1,0:T(8,128)(2,1)}, bf16[4,256,512]{2,1,0:T(8,128)(2,1)}, u32[]{:S(2)}, u32[]{:S(2)}) collective-permute-start(bf16[4,256,512]{2,1,0:T(8,128)(2,1)} %get-tuple-element.24), channel_id=1, source_target_pairs={{0,32},{32,0},{1,33},{33,1},{2,34},{34,2},{3,35},{35,3},{4,36},{36... | collective-permute-start | bytes 3145736 | tf_op jit(solution)/shard_map/ppermute | solution.py:294
  17.7 0.1 constant_dynamic-slice_fusion
  17.8 0.1 broadcast_add_fusion.diagonal_ref
  17.8 0.0 copy-start.3
  17.9 0.0 copy-start.7
  17.9 0.0 collective-permute-done.halo_ref
  17.9 1.6 %shard_map.94.field = bf16[3,512,512]{2,1,0:T(8,128)(2,1)S(1)} custom-call(s32[3]{0:T(128)S(1)} %pad_add_fusion.place_ref, s32[64]{0:T(128)S(1)} %copy-done.2, bf16[2,512,512]{2,1,0:T(8,128)(2,1)S(1)} %copy-done.1, bf16[512,512]{1,0:T(8,128)(2,1)} %collective-permute-done.halo_ref), custom_call_target="tpu_custom_call" | custom-call | flops 8589934592 | bytes 3145728 | tf_op jit(solution)/shard_map/pallas_call | solution.py:312
  19.5 1.2 copy-done.8
  20.7 0.0 collective-permute-done.2.swapped_ref
  20.7 0.0 collective-permute-done.1.other_ref
  20.7 5.8 %shard_map.96 = (bf16[8,112,512]{2,1,0:T(8,128)(2,1)}, f32[3,32,512]{2,1,0:T(8,128)S(1)}) custom-call(s32[3]{0:T(128)S(1)} %pad_add_fusion.place_ref, s32[64]{0:T(128)S(1)} %copy-done.7, bf16[3,512,512]{2,1,0:T(8,128)(2,1)} %copy-done.8, f32[2,32,512]{2,1,0:T(8,128)S(1)} %broadcast_add_fusion.diagonal_ref, bf16[4,256,512]{2,1,0:T(8,128)(2,1)S(1)} %copy-done.5, ...), custom_call_target="tpu_custom_call" | custom-call | flops 2147483648 | bytes 6291456 | tf_op jit(solution)/shard_map/pallas_call | solution.py:315
  26.6 7.6 %all-to-all-start = ((bf16[8,112,512]{2,1,0:T(8,128)(2,1)}), bf16[8,112,512]{2,1,0:T(8,128)(2,1)S(1)}, u32[]{:S(2)}, u32[]{:S(2)}) async-start(bf16[8,112,512]{2,1,0:T(8,128)(2,1)} %get-tuple-element.25), calls=%async_computation | async-start | bytes 1835008 | tf_op jit(solution)/shard_map/all_to_all | solution.py:307
  34.2 1.3 collective-permute-start.5
  35.5 3.2 %collective-permute-done.5 = f32[8,128]{1,0:T(8,128)S(1)} collective-permute-done((f32[8,128]{1,0:T(8,128)S(1)}, f32[8,128]{1,0:T(8,128)S(1)}, u32[]{:S(2)}, u32[]{:S(2)}) %collective-permute-start.5) | collective-permute-done | bytes 4128 | tf_op jit(solution)/shard_map/ppermute | solution.py:282
  38.8 0.1 dynamic-slice_bitcast_fusion
  38.9 11.2 %all-to-all-done.received_ref = bf16[8,112,512]{2,1,0:T(8,128)(2,1)S(1)} async-done(((bf16[8,112,512]{2,1,0:T(8,128)(2,1)}), bf16[8,112,512]{2,1,0:T(8,128)(2,1)S(1)}, u32[]{:S(2)}, u32[]{:S(2)}) %all-to-all-start) | async-done | bytes 917536 | tf_op jit(solution)/shard_map/all_to_all | solution.py:307
  50.1 0.7 shard_map.97
  50.8 16.3 %all-to-all-start.1 = ((f32[64,1,128]{2,1,0:T(1,128)}), f32[64,1,128]{2,1,0:T(1,128)S(1)}, u32[]{:S(2)}, u32[]{:S(2)}) async-start(f32[64,1,128]{2,1,0:T(1,128)} %get-tuple-element.26), calls=%async_computation.1 | async-start | bytes 65536 | tf_op jit(solution)/shard_map/all_to_all | solution.py:319
  67.1 1.3 collective-permute-start.4
  68.4 4.0 %collective-permute-start.3 = (f32[32,512]{1,0:T(8,128)S(1)}, f32[32,512]{1,0:T(8,128)S(1)}, u32[]{:S(2)}, u32[]{:S(2)}) collective-permute-start(f32[32,512]{1,0:T(8,128)S(1)} %get-tuple-element.29.leaving_ref), channel_id=1, source_target_pairs={{0,1},{1,2},{2,3},{3,4},{4,5},{5,6},{6,7},{7,8},{8,9},{9,10},{10,1... | collective-permute-start | bytes 196616 | tf_op jit(solution)/shard_map/ppermute | solution.py:320
  72.4 0.1 broadcast_add_fusion.1.next_ref
  72.5 0.1 collective-permute-done.4.ahead_ref
  72.6 1.1 collective-permute-done.3.arrived_ref
  73.7 5.7 %all-to-all-done.1.gathered_ref = f32[64,1,128]{2,1,0:T(1,128)S(1)} async-done(((f32[64,1,128]{2,1,0:T(1,128)}), f32[64,1,128]{2,1,0:T(1,128)S(1)}, u32[]{:S(2)}, u32[]{:S(2)}) %all-to-all-start.1) | async-done | bytes 32800 | tf_op jit(solution)/shard_map/all_to_all | solution.py:319
  79.4 0.9 shard_map.98
  80.3 16.0 %all_to_all.25.near_ref = bf16[8,96,512]{2,1,0:T(8,128)(2,1)S(1)} all-to-all(bf16[8,96,512]{2,1,0:T(8,128)(2,1)S(1)} %get-tuple-element.31), channel_id=1, replica_groups=mesh['yh'=2,'x'=4,'c'=2,'yl'=2,'z'=16] {'yh','x'}, dimensions={0} | all-to-all | bytes 1572864 | tf_op jit(solution)/shard_map/all_to_all | solution.py:333
  96.3 4.1 %collective-permute-start.6 = (bf16[8,96,512]{2,1,0:T(8,128)(2,1)S(1)}, bf16[8,96,512]{2,1,0:T(8,128)(2,1)S(1)}, u32[]{:S(2)}, u32[]{:S(2)}) collective-permute-start(bf16[8,96,512]{2,1,0:T(8,128)(2,1)S(1)} %all_to_all.25.near_ref), channel_id=1, source_target_pairs={{0,32},{32,0},{1,33},{33,1},{2,34},{34,2},{3,35},{35,3},{4,36},{36... | collective-permute-start | bytes 2359304 | tf_op jit(solution)/shard_map/ppermute | solution.py:334
  100.4 1.9 %collective-permute-done.6.far_ref = bf16[8,96,512]{2,1,0:T(8,128)(2,1)S(1)} collective-permute-done((bf16[8,96,512]{2,1,0:T(8,128)(2,1)S(1)}, bf16[8,96,512]{2,1,0:T(8,128)(2,1)S(1)}, u32[]{:S(2)}, u32[]{:S(2)}) %collective-permute-start.6) | collective-permute-done | bytes 786464 | tf_op jit(solution)/shard_map/ppermute | solution.py:334
  102.3 1.2 copy-done.6
  103.5 4.5 %shard_map.99 = bf16[8,112,512]{2,1,0:T(8,128)(2,1)S(1)} custom-call(s32[3]{0:T(128)S(1)} %pad_add_fusion.place_ref, s32[64]{0:T(128)S(1)} %copy-done.7, bf16[8,96,512]{2,1,0:T(8,128)(2,1)S(1)} %all_to_all.25.near_ref, bf16[8,96,512]{2,1,0:T(8,128)(2,1)S(1)} %collective-permute-done.6.far_ref, f32[1,512]{1,0:T(1,128)S(1)} %get-tuple-element.32.scalar_ref, ...), custom_call_target="tpu_custom_call" | custom-call | flops 2147483648 | bytes 6291456 | tf_op jit(solution)/shard_map/pallas_call | solution.py:335
  108.0 18.0 %all_to_all.26.received_ref = bf16[8,112,512]{2,1,0:T(8,128)(2,1)S(1)} all-to-all(bf16[8,112,512]{2,1,0:T(8,128)(2,1)S(1)} %shard_map.99), channel_id=1, replica_groups=mesh['yh'=2,'x'=4,'c'=2,'yl'=2,'z'=16] {'yh','x'}, dimensions={0} | all-to-all | bytes 1835008 | tf_op jit(solution)/shard_map/all_to_all | solution.py:307
  126.0 0.7 shard_map.100
  126.7 10.2 %all-to-all-start.4 = ((f32[64,1,128]{2,1,0:T(1,128)}), f32[64,1,128]{2,1,0:T(1,128)S(1)}, u32[]{:S(2)}, u32[]{:S(2)}) async-start(f32[64,1,128]{2,1,0:T(1,128)} %get-tuple-element.33), calls=%async_computation.4 | async-start | bytes 65536 | tf_op jit(solution)/shard_map/all_to_all | solution.py:339
  136.9 3.3 %collective-permute-start.7 = (f32[32,512]{1,0:T(8,128)S(1)}, f32[32,512]{1,0:T(8,128)S(1)}, u32[]{:S(2)}, u32[]{:S(2)}) collective-permute-start(f32[32,512]{1,0:T(8,128)S(1)} %get-tuple-element.37), channel_id=1, source_target_pairs={{0,1},{1,2},{2,3},{3,4},{4,5},{5,6},{6,7},{7,8},{8,9},{9,10},{10,1... | collective-permute-start | bytes 196616 | tf_op jit(solution)/shard_map/ppermute | solution.py:340
  140.1 1.4 collective-permute-done.7.arrived_ref
  141.5 7.6 %all-to-all-done.4.gathered_ref = f32[64,1,128]{2,1,0:T(1,128)S(1)} async-done(((f32[64,1,128]{2,1,0:T(1,128)}), f32[64,1,128]{2,1,0:T(1,128)S(1)}, u32[]{:S(2)}, u32[]{:S(2)}) %all-to-all-start.4) | async-done | bytes 32800 | tf_op jit(solution)/shard_map/all_to_all | solution.py:339
  149.1 1.8 %shard_map.101 = (bf16[2,32,512]{2,1,0:T(8,128)(2,1)}, bf16[2,32,512]{2,1,0:T(8,128)(2,1)}, f32[1,128]{1,0:T(1,128)S(1)}) custom-call(s32[3]{0:T(128)S(1)} %pad_add_fusion.place_ref, s32[64]{0:T(128)S(1)} %copy-done.2, f32[64,1,128]{2,1,0:T(1,128)S(1)} %all-to-all-done.4.gathered_ref, f32[1,128]{1,0:T(1,128)S(1)} %get-tuple-element.34.known_ref, ...), custom_call_target="tpu_custom_call" | custom-call | bytes 1048576 | tf_op jit(solution)/shard_map/pallas_call | solution.py:342
  150.9 0.5 slice_bitcast_fusion.2
  (20 shorter events, 0.1 us)
Async XLA Ops:
  0.6 12.2 %copy-start = (bf16[1,2,512,512]{3,2,1,0:T(8,128)(2,1)S(1)}, bf16[1,2,512,512]{3,2,1,0:T(8,128)(2,1)}, u32[]{:S(2)}) copy-start(bf16[1,2,512,512]{3,2,1,0:T(8,128)(2,1)} %left_ref.1) | copy-start | bytes 3145732
  0.6 17.2 %copy-start.1 = (bf16[2,512,512]{2,1,0:T(8,128)(2,1)S(1)}, bf16[2,512,512]{2,1,0:T(8,128)(2,1)}, u32[]{:S(2)}) copy-start(bf16[2,512,512]{2,1,0:T(8,128)(2,1)} %start_ref.1) | copy-start | bytes 3145732
  0.7 17.0 %copy-start.10 = (f32[2,512]{1,0:T(2,128)S(1)}, f32[2,512]{1,0:T(2,128)}, u32[]{:S(2)}) copy-start(f32[2,512]{1,0:T(2,128)} %param.10) | copy-start | bytes 12292
  0.7 17.1 %copy-start.9 = (f32[2,512]{1,0:T(2,128)S(1)}, f32[2,512]{1,0:T(2,128)}, u32[]{:S(2)}) copy-start(f32[2,512]{1,0:T(2,128)} %param.11) | copy-start | bytes 12292
  0.7 17.2 %copy-start.2 = (s32[64]{0:T(128)S(1)}, s32[64]{0:T(128)}, u32[]{:S(2)}) copy-start(s32[64]{0:T(128)} %size_ref.5) | copy-start | bytes 772
  2.7 15.2 %collective-permute-start = (bf16[512,512]{1,0:T(8,128)(2,1)}, bf16[512,512]{1,0:T(8,128)(2,1)}, u32[]{:S(2)}, u32[]{:S(2)}) collective-permute-start(bf16[512,512]{1,0:T(8,128)(2,1)} %slice_bitcast_fusion), channel_id=1, source_target_pairs={{1,0},{2,1},{3,2},{4,3},{5,4},{6,5},{7,6},{8,7},{9,8},{10,9},{11,1... | collective-permute-start | bytes 1572872 | tf_op jit(solution)/shard_map/ppermute | solution.py:280
  4.0 16.7 %collective-permute-start.2 = (bf16[1,2,512,512]{3,2,1,0:T(8,128)(2,1)}, bf16[1,2,512,512]{3,2,1,0:T(8,128)(2,1)}, u32[]{:S(2)}, u32[]{:S(2)}) collective-permute-start(bf16[1,2,512,512]{3,2,1,0:T(8,128)(2,1)} %right_ref.3), channel_id=1, source_target_pairs={{0,32},{32,0},{1,33},{33,1},{2,34},{34,2},{3,35},{35,3},{4,36},{36... | collective-permute-start | bytes 3145736 | tf_op jit(solution)/shard_map/ppermute | solution.py:289
  14.8 1.0 copy-start.4
  15.7 4.9 %collective-permute-start.1 = (bf16[4,256,512]{2,1,0:T(8,128)(2,1)}, bf16[4,256,512]{2,1,0:T(8,128)(2,1)}, u32[]{:S(2)}, u32[]{:S(2)}) collective-permute-start(bf16[4,256,512]{2,1,0:T(8,128)(2,1)} %get-tuple-element.24), channel_id=1, source_target_pairs={{0,32},{32,0},{1,33},{33,1},{2,34},{34,2},{3,35},{35,3},{4,36},{36... | collective-permute-start | bytes 3145736 | tf_op jit(solution)/shard_map/ppermute | solution.py:294
  17.8 2.9 %copy-start.3 = (bf16[1,2,512,512]{3,2,1,0:T(8,128)(2,1)S(1)}, bf16[1,2,512,512]{3,2,1,0:T(8,128)(2,1)}, u32[]{:S(2)}) copy-start(bf16[1,2,512,512]{3,2,1,0:T(8,128)(2,1)} %right_ref.3) | copy-start | bytes 3145732
  17.9 2.8 %copy-start.5 = (bf16[4,256,512]{2,1,0:T(8,128)(2,1)S(1)}, bf16[4,256,512]{2,1,0:T(8,128)(2,1)}, u32[]{:S(2)}) copy-start(bf16[4,256,512]{2,1,0:T(8,128)(2,1)} %copy-done.4) | copy-start | bytes 3145732
  17.9 2.8 %copy-start.7 = (s32[64]{0:T(128)S(1)}, s32[64]{0:T(128)}, u32[]{:S(2)}) copy-start(s32[64]{0:T(128)} %spin_ref.3) | copy-start | bytes 772
  19.5 1.2 copy-start.8
  26.6 7.6 %slice-start = ((f32[2,512]{1,0:T(2,128)}), f32[1,512]{1,0:T(1,128)S(1)}, s32[]{:S(2)}) async-start(f32[2,512]{1,0:T(2,128)} %param.11), calls=%async_computation.5 | async-start | bytes 4096 | tf_op jit(solution)/shard_map/slice | solution.py:281
  26.6 7.6 %slice-start.1 = ((f32[2,512]{1,0:T(2,128)}), f32[1,512]{1,0:T(1,128)S(1)}, s32[]{:S(2)}) async-start(f32[2,512]{1,0:T(2,128)} %param.10), calls=%async_computation.6 | async-start | bytes 4096 | tf_op jit(solution)/shard_map/slice | solution.py:281
  26.6 23.5 %all-to-all-start = ((bf16[8,112,512]{2,1,0:T(8,128)(2,1)}), bf16[8,112,512]{2,1,0:T(8,128)(2,1)S(1)}, u32[]{:S(2)}, u32[]{:S(2)}) async-start(bf16[8,112,512]{2,1,0:T(8,128)(2,1)} %get-tuple-element.25), calls=%async_computation | async-start | bytes 1835008 | tf_op jit(solution)/shard_map/all_to_all | solution.py:307
  34.2 4.5 %collective-permute-start.5 = (f32[8,128]{1,0:T(8,128)S(1)}, f32[8,128]{1,0:T(8,128)S(1)}, u32[]{:S(2)}, u32[]{:S(2)}) collective-permute-start(f32[8,128]{1,0:T(8,128)S(1)} %reshape.39), channel_id=1, source_target_pairs={{1,0},{2,1},{3,2},{4,3},{5,4},{6,5},{7,6},{8,7},{9,8},{10,9},{11,1... | collective-permute-start | bytes 12296 | tf_op jit(solution)/shard_map/ppermute | solution.py:282
  50.8 28.6 %all-to-all-start.1 = ((f32[64,1,128]{2,1,0:T(1,128)}), f32[64,1,128]{2,1,0:T(1,128)S(1)}, u32[]{:S(2)}, u32[]{:S(2)}) async-start(f32[64,1,128]{2,1,0:T(1,128)} %get-tuple-element.26), calls=%async_computation.1 | async-start | bytes 65536 | tf_op jit(solution)/shard_map/all_to_all | solution.py:319
  67.1 5.5 %collective-permute-start.4 = (f32[32,512]{1,0:T(8,128)S(1)}, f32[32,512]{1,0:T(8,128)S(1)}, u32[]{:S(2)}, u32[]{:S(2)}) collective-permute-start(f32[32,512]{1,0:T(8,128)S(1)} %get-tuple-element.27.first_ref), channel_id=1, source_target_pairs={{1,0},{2,1},{3,2},{4,3},{5,4},{6,5},{7,6},{8,7},{9,8},{10,9},{11,1... | collective-permute-start | bytes 196616 | tf_op jit(solution)/shard_map/ppermute | solution.py:321
  68.4 5.3 %collective-permute-start.3 = (f32[32,512]{1,0:T(8,128)S(1)}, f32[32,512]{1,0:T(8,128)S(1)}, u32[]{:S(2)}, u32[]{:S(2)}) collective-permute-start(f32[32,512]{1,0:T(8,128)S(1)} %get-tuple-element.29.leaving_ref), channel_id=1, source_target_pairs={{0,1},{1,2},{2,3},{3,4},{4,5},{5,6},{6,7},{7,8},{8,9},{9,10},{10,1... | collective-permute-start | bytes 196616 | tf_op jit(solution)/shard_map/ppermute | solution.py:320
  96.3 6.0 %collective-permute-start.6 = (bf16[8,96,512]{2,1,0:T(8,128)(2,1)S(1)}, bf16[8,96,512]{2,1,0:T(8,128)(2,1)S(1)}, u32[]{:S(2)}, u32[]{:S(2)}) collective-permute-start(bf16[8,96,512]{2,1,0:T(8,128)(2,1)S(1)} %all_to_all.25.near_ref), channel_id=1, source_target_pairs={{0,32},{32,0},{1,33},{33,1},{2,34},{34,2},{3,35},{35,3},{4,36},{36... | collective-permute-start | bytes 2359304 | tf_op jit(solution)/shard_map/ppermute | solution.py:334
  102.3 1.2 copy-start.6
  126.7 22.4 %all-to-all-start.4 = ((f32[64,1,128]{2,1,0:T(1,128)}), f32[64,1,128]{2,1,0:T(1,128)S(1)}, u32[]{:S(2)}, u32[]{:S(2)}) async-start(f32[64,1,128]{2,1,0:T(1,128)} %get-tuple-element.33), calls=%async_computation.4 | async-start | bytes 65536 | tf_op jit(solution)/shard_map/all_to_all | solution.py:339
  136.9 4.6 %collective-permute-start.7 = (f32[32,512]{1,0:T(8,128)S(1)}, f32[32,512]{1,0:T(8,128)S(1)}, u32[]{:S(2)}, u32[]{:S(2)}) collective-permute-start(f32[32,512]{1,0:T(8,128)S(1)} %get-tuple-element.37), channel_id=1, source_target_pairs={{0,1},{1,2},{2,3},{3,4},{4,5},{5,6},{6,7},{7,8},{8,9},{9,10},{10,1... | collective-permute-start | bytes 196616 | tf_op jit(solution)/shard_map/ppermute | solution.py:340

commit v3 on v2

v3 whole, which is shorter than its diff:
```python
import jax
import jax.numpy as jnp
from jax import lax
from jax.experimental import pallas as pl
from jax.experimental.pallas import tpu as pltpu
from jax.sharding import Mesh, PartitionSpec as P

F32 = jnp.float32
BF16 = jnp.bfloat16
OP = ("yh", "x", "c")
SEC = ("yl", "z")
WIDTH = 512
ROWS = 32
NOP = 16
BLOCKS = 3
PART = 2 * ROWS + 8
VMEM_LIMIT = 24 * 1024 * 1024

VM = pl.BlockSpec(memory_space=pltpu.VMEM)
SM = pl.BlockSpec(memory_space=pltpu.SMEM)
HBM = pl.BlockSpec(memory_space=pltpu.HBM)


def call(kernel, out_shape, in_specs, scratch=(), flops=0, nbytes=1 << 20, out_spec=VM):
    return pl.pallas_call(
        kernel,
        out_shape=out_shape,
        in_specs=in_specs,
        out_specs=jax.tree.map(lambda _: out_spec, out_shape),
        scratch_shapes=list(scratch),
        compiler_params=pltpu.CompilerParams(vmem_limit_bytes=VMEM_LIMIT),
        cost_estimate=pl.CostEstimate(flops=flops, bytes_accessed=nbytes, transcendentals=0),
    )


def shaped(shape, dtype):
    return jax.ShapeDtypeStruct(shape, dtype)


def product(first, second, second_axis=0):
    return lax.dot_general(
        first, second, (((1,), (second_axis,)), ((), ())), preferred_element_type=F32
    )


def total(array):
    return jnp.sum(jnp.sum(array, axis=0, keepdims=True), axis=1, keepdims=True)


def lanes(values, width):
    place = lax.broadcasted_iota(jnp.int32, (1, width), 1)
    row = jnp.zeros((1, width), F32)
    for index, value in enumerate(values):
        row = jnp.where(place == index, value, row)
    return row


def own_rows(place_ref):
    return pl.multiple_of(place_ref[1] * ROWS, ROWS)


def inside(size, first_row, shape):
    rows = lax.broadcasted_iota(jnp.int32, shape, 0) + first_row
    columns = lax.broadcasted_iota(jnp.int32, shape, 1)
    return (rows < size) & (columns < size)


def size_of(place_ref, size_ref, block):
    return size_ref[jnp.minimum(place_ref[2] + block, size_ref.shape[0] - 1)]


def send_kernel(place_ref, start_ref, left_ref, right_ref, halo_ref, send_ref, semaphores):
    there = 1 - place_ref[0]
    copies = [
        pltpu.make_async_copy(start_ref.at[0], halo_ref, semaphores.at[0]),
        pltpu.make_async_copy(left_ref.at[0, there], send_ref.at[0], semaphores.at[1]),
        pltpu.make_async_copy(right_ref.at[0, there], send_ref.at[1], semaphores.at[2]),
    ]
    for copy in copies:
        copy.start()
    for copy in copies:
        copy.wait()


def mask_kernel(place_ref, size_ref, start_ref, halo_ref, field_ref, rows_ref):
    core = place_ref[0]

    def masked(source, block, first_row=0):
        mask = inside(size_of(place_ref, size_ref, block), first_row, source.shape)
        return jnp.where(mask, source.astype(F32), 0.0)

    field_ref[0] = masked(start_ref[core], core).astype(BF16)

    @pl.when(core == 0)
    def _():
        field_ref[1] = masked(start_ref[1], 1).astype(BF16)

    @pl.when(core == 1)
    def _():
        field_ref[1] = masked(halo_ref[...], 2).astype(BF16)

    first_row = own_rows(place_ref)
    for block in range(2):
        rows_ref[block] = masked(start_ref[block, pl.ds(first_row, ROWS)], block, first_row)


def images(place_ref, spin_ref, left_ref, right_ref, other_ref, field, after):
    core = place_ref[0]
    here = place_ref[2] + core
    following = jnp.minimum(here + 1, spin_ref.shape[0] - 1)
    above = jnp.full((1, WIDTH), spin_ref[following], jnp.int32).astype(F32) + 1.0
    below = jnp.full((1, WIDTH), spin_ref[here], jnp.int32).astype(F32) + 1.0
    linked = jnp.full((1, WIDTH), here, jnp.int32) + 1 < spin_ref.shape[0]
    coupling = jnp.where(linked, jnp.sqrt(above / below), 0.0)
    lowered = raised = None
    for left, right in (
        (left_ref[0, core], right_ref[0, core]),
        (other_ref[0], other_ref[1]),
    ):
        up = product(left, product(field, right, 1).astype(BF16))
        down = product(product(left.T, after).astype(BF16), right)
        raised = up if raised is None else raised + up
        lowered = down if lowered is None else lowered + down
    return coupling * lowered, coupling * raised


def put_parts(lowered, raised, after, scalars, parts_ref):
    energy = 2.0 * total(raised * after.astype(F32))
    row = lanes([energy], WIDTH) + scalars
    high = row.astype(BF16).astype(F32)
    middle = (row - high).astype(BF16).astype(F32)
    low = (row - high) - middle
    place = lax.broadcasted_iota(jnp.int32, (8, WIDTH), 0)
    coded = jnp.where(
        place == 0, high, jnp.where(place == 1, middle, jnp.where(place == 2, low, 0.0))
    ).astype(BF16)
    for device in range(NOP):
        here = slice(device * ROWS, (device + 1) * ROWS)
        parts_ref[device, :ROWS] = lowered[here].astype(BF16)
        parts_ref[device, ROWS : 2 * ROWS] = raised[here].astype(BF16)
        parts_ref[device, 2 * ROWS :] = coded


def first_kernel(
    place_ref, spin_ref, field_ref, rows_ref, diagonal_ref, left_ref, right_ref, other_ref, parts_ref
):
    norm = jnp.zeros((ROWS, WIDTH), F32)
    energy = jnp.zeros((ROWS, WIDTH), F32)
    for block in range(2):
        square = rows_ref[block] * rows_ref[block]
        norm = norm + square
        energy = energy + diagonal_ref[block] * square
    after = field_ref[1]
    lowered, raised = images(
        place_ref, spin_ref, left_ref, right_ref, other_ref, field_ref[0], after
    )
    put_parts(lowered, raised, after, lanes([total(energy), total(norm)], WIDTH), parts_ref)


def second_kernel(
    place_ref, spin_ref, gathered_ref, scalar_ref, left_ref, right_ref, other_ref, parts_ref
):
    field = gathered_ref[:, :ROWS].reshape(WIDTH, WIDTH)
    after = gathered_ref[:, ROWS:].reshape(WIDTH, WIDTH)
    lowered, raised = images(place_ref, spin_ref, left_ref, right_ref, other_ref, field, after)
    put_parts(lowered, raised, after, scalar_ref[...], parts_ref)


def scalar_kernel(received_ref, scalar_ref):
    coded = jnp.zeros((8, 128), F32)
    for device in range(NOP):
        coded = coded + received_ref[device, 2 * ROWS :, :128].astype(F32)
    row = jnp.sum(coded, axis=0, keepdims=True)
    scalar_ref[...] = jnp.broadcast_to(row[None], scalar_ref.shape)


def sum_kernel(received_ref, first_ref, second_ref, leaving_ref):
    sums = [jnp.zeros((ROWS, WIDTH), F32) for _ in range(BLOCKS)]
    for device in range(NOP):
        block = device % 2
        sums[block] = sums[block] + received_ref[device, :ROWS].astype(F32)
        sums[block + 1] = sums[block + 1] + received_ref[device, ROWS : 2 * ROWS].astype(F32)
    first_ref[...], second_ref[...], leaving_ref[...] = sums


def scalars_of(gathered_ref, count):
    row = jnp.sum(gathered_ref[...], axis=0)
    return [row[:, index : index + 1] for index in range(count)]


def correction_kernel(
    place_ref, size_ref, gathered_ref, first_ref, second_ref, leaving_ref, arrived_ref,
    ahead_ref, diagonal_ref, next_diagonal_ref, rows_ref, next_rows_ref,
    spread_ref, image_ref, change_ref, scalar_ref, known_ref,
):
    energy, norm = scalars_of(gathered_ref, 2)
    rayleigh = energy / norm
    scale = jnp.sqrt(norm)
    first_row = own_rows(place_ref)
    sums = [first_ref[...] + arrived_ref[...], second_ref[...], leaving_ref[...] + ahead_ref[...]]
    amounts = [jnp.zeros((ROWS, WIDTH), F32) for _ in range(4)]
    for block in range(BLOCKS):
        mask = inside(size_of(place_ref, size_ref, block), first_row, (ROWS, WIDTH))
        values = next_rows_ref[:ROWS] if block == 2 else rows_ref[block]
        diagonal = next_diagonal_ref[...] if block == 2 else diagonal_ref[block]
        unit = jnp.where(mask, values, 0.0) / scale
        image = jnp.where(mask, sums[block] + diagonal * values, 0.0) / scale
        residual = image - rayleigh * unit
        change = residual / (jnp.abs(diagonal - rayleigh) + 1.0)
        rounded = change.astype(BF16)
        for device in range(NOP):
            part = block - device % 2
            if part in (0, 1):
                spread_ref[device, part * ROWS : (part + 1) * ROWS] = rounded
        if block < 2:
            image_ref[block] = image
            change_ref[block] = change
            again = rounded.astype(F32)
            amounts[0] = amounts[0] + diagonal * again * again
            amounts[1] = amounts[1] + unit * change
            amounts[2] = amounts[2] + change * change
            amounts[3] = amounts[3] + change * image
    scalar_ref[...] = lanes([total(amount) for amount in amounts], WIDTH)
    known_ref[...] = lanes([rayleigh, scale], 128)


def ritz_kernel(
    place_ref, size_ref, gathered_ref, known_ref, first_ref, second_ref, arrived_ref,
    diagonal_ref, rows_ref, image_ref, change_ref, vector_ref, residual_ref, energies_ref,
):
    change_energy, correlation, square, change_image = scalars_of(gathered_ref, 4)
    rayleigh = known_ref[:, 0:1]
    scale = known_ref[:, 1:2]
    spread = square - correlation * correlation
    deviation = jnp.sqrt(spread)
    cross_term = (change_image - correlation * rayleigh) / deviation
    second_energy = (
        change_energy - 2.0 * correlation * change_image + correlation * correlation * rayleigh
    ) / spread
    half_gap = 0.5 * (rayleigh - second_energy)
    length = jnp.sqrt(half_gap * half_gap + cross_term * cross_term)
    lowest = 0.5 * (rayleigh + second_energy) - length
    apart = length > 0.0
    divisor = jnp.where(apart, length, 1.0)
    double_cosine = jnp.where(apart, half_gap / divisor, 1.0)
    double_sine = jnp.where(apart, cross_term / divisor, 0.0)
    larger = jnp.sqrt(0.5 * (1.0 + jnp.abs(double_cosine)))
    smaller = 0.5 * double_sine / larger
    ahead = double_cosine >= 0.0
    sign = jnp.where(cross_term < 0.0, -1.0, 1.0)
    cosine_angle = jnp.where(ahead, larger, jnp.abs(smaller))
    sine_angle = jnp.where(ahead, smaller, sign * larger)
    first_row = own_rows(place_ref)
    sums = [first_ref[...] + arrived_ref[...], second_ref[...]]
    for block in range(2):
        mask = inside(size_of(place_ref, size_ref, block), first_row, (ROWS, WIDTH))
        unit = rows_ref[block] / scale
        image = image_ref[block]
        change = change_ref[block]
        rounded = change.astype(BF16).astype(F32)
        change_picture = jnp.where(mask, sums[block] + diagonal_ref[block] * rounded, 0.0)
        unit_second = (change - correlation * unit) / deviation
        second_image = (change_picture - correlation * image) / deviation
        ritz_unit = sine_angle * unit - cosine_angle * unit_second
        vector_ref[block] = (scale * ritz_unit).astype(BF16)
        residual_ref[block] = (
            scale * (sine_angle * image - cosine_angle * second_image - lowest * ritz_unit)
        ).astype(BF16)
    energies_ref[...] = lanes([rayleigh, lowest], 2)


def line(distance):
    devices = range(lax.axis_size(SEC))
    return [(i, i + distance) for i in devices if i + distance in devices]


def body(start, left, right, left_energy, right_energy, sector_size, sector_spin):
    core = lax.axis_index("c")
    position = lax.axis_index(OP)
    sectors = lax.axis_size(SEC)
    place = jnp.stack([core, position, 2 * lax.axis_index(SEC)]).astype(jnp.int32)
    block_shape = shaped((WIDTH, WIDTH), BF16)
    own_shape = shaped((2, ROWS, WIDTH), F32)
    row_shape = shaped((ROWS, WIDTH), F32)
    parts_shape = shaped((NOP, PART, WIDTH), BF16)
    work = 16 * WIDTH * WIDTH * WIDTH

    halo_source, send = call(
        send_kernel,
        (block_shape, shaped((2, WIDTH, WIDTH), BF16)),
        [SM, HBM, HBM, HBM],
        [pltpu.SemaphoreType.DMA((3,))],
        out_spec=HBM,
    )(place, start, left, right)
    to_second_core = [(sectors + i + 1, sectors + i) for i in range(sectors - 1)]
    halo = lax.ppermute(halo_source, ("c",) + SEC, to_second_core)
    other = lax.ppermute(send, "c", [(0, 1), (1, 0)])

    first_row = position * ROWS

    def diagonal_rows(left_levels, right_levels):
        own_levels = lax.dynamic_slice_in_dim(left_levels, first_row, ROWS, 1)
        return own_levels[:, :, None] + right_levels[:, None, :]

    diagonal = diagonal_rows(left_energy, right_energy)
    before = jnp.concatenate(
        [
            lax.dynamic_slice_in_dim(start[0], first_row, ROWS, 0).astype(F32),
            left_energy[:1],
            right_energy[:1],
            jnp.zeros((6, WIDTH), F32),
        ]
    )
    beyond = lax.ppermute(before, SEC, line(-1))
    next_diagonal = diagonal_rows(beyond[ROWS : ROWS + 1], beyond[ROWS + 1 : ROWS + 2])[0]

    def summed(parts):
        received = lax.all_to_all(parts, OP, 0, 0)
        scalars = call(scalar_kernel, shaped((sectors, 1, 128), F32), [VM])(received)
        gathered = lax.all_to_all(scalars, SEC, 0, 0)
        sums = call(sum_kernel, (row_shape, row_shape, row_shape), [VM])(received)
        return (*sums, gathered)

    field, rows = call(
        mask_kernel,
        (shaped((2, WIDTH, WIDTH), BF16), own_shape),
        [SM] * 2 + [VM] * 2,
        flops=4 * work,
        nbytes=3 << 20,
    )(place, sector_size, start, halo)
    parts = call(first_kernel, parts_shape, [SM] * 2 + [VM] * 6, flops=work, nbytes=4 << 20)(
        place, sector_spin, field, rows, diagonal, left, right, other
    )
    first, second, leaving, gathered = summed(parts)
    arrived = lax.ppermute(leaving, SEC, line(1))
    ahead = lax.ppermute(first, SEC, line(-1))
    spread, image, change, amounts, known = call(
        correction_kernel,
        (
            shaped((NOP, 2 * ROWS, WIDTH), BF16), own_shape, own_shape,
            shaped((1, WIDTH), F32), shaped((1, 128), F32),
        ),
        [SM] * 2 + [VM] * 10,
    )(
        place, sector_size, gathered, first, second, leaving, arrived, ahead,
        diagonal, next_diagonal, rows, beyond,
    )
    fields = lax.all_to_all(spread, OP, 0, 0)
    parts = call(second_kernel, parts_shape, [SM] * 2 + [VM] * 5, flops=work, nbytes=4 << 20)(
        place, sector_spin, fields, amounts, left, right, other
    )
    first, second, leaving, gathered = summed(parts)
    arrived = lax.ppermute(leaving, SEC, line(1))
    result = shaped((2, ROWS, WIDTH), BF16)
    vector, residual, energies = call(
        ritz_kernel, (result, result, shaped((1, 2), F32)), [SM] * 2 + [VM] * 9
    )(
        place, sector_size, gathered, known, first, second, arrived,
        diagonal, rows, image, change,
    )
    return vector, residual, energies.reshape(2)


def solution(mesh):
    fine = Mesh(mesh.devices.reshape(2, 4, 2, 2, 16), ("yh", "x", "c", "yl", "z"))
    return jax.shard_map(
        body,
        mesh=fine,
        in_specs=(
            P(SEC, None, None),
            P(OP, SEC, None, None),
            P(OP, SEC, None, None),
            P(SEC, None),
            P(SEC, None),
            P(),
            P(),
        ),
        out_specs=(P(SEC, OP, None), P(SEC, OP, None), P()),
        check_vma=False,
    )
```

time: 152 us -> 152 us (level)
  blocking collectives: 34 us -> 61.1 us
  starting transfers between devices: 60 us -> 41.5 us
  Pallas kernels: 17.9 us -> 12.1 us
  waiting for transfers between devices: 32.3 us -> 30.7 us
    all_to_all x2 -> x3, blocking collectives: 34 us -> 61.1 us  [the longest x1 22.5 us: body(): fields = lax.all_to_all(spread, OP, 0, 0)]
    all_to_all x3 -> x2, starting transfers between devices: 34.1 us -> 23.8 us  [the longest x1 16.8 us: summed(): gathered = lax.all_to_all(scalars, SEC, 0, 0)]
    ppermute x5 -> x3, starting transfers between devices: 17.4 us -> 10.8 us  [the longest x1 8.19 us: body(): other = lax.ppermute(send, 'c', [(0, 1), (1, 0)])]
    pallas_call x8 -> x10, Pallas kernels: 17.9 us -> 12.1 us  [the longest x1 3.03 us: body(): call(first_kernel, parts_shape, [SM] * 2 + [VM] * 6, flops=work, nbytes=4...]
    squeeze x2 -> x0, local copies, waits for them, and re-layouts: 2.51 us -> none  [the longest x1 2 us: body(): halo = lax.ppermute(start[0], SEC, line(-1))]
    ppermute x2, waiting for transfers between devices: 2.49 us -> 0.01 us  [body(): arrived = lax.ppermute(leaving, SEC, line(1))]
    ppermute x2, starting transfers between devices: 7.25 us -> 5.64 us  [body(): arrived = lax.ppermute(leaving, SEC, line(1))]
    unnamed x22 -> x30, local copies, waits for them, and re-layouts: 3.41 us -> 4.75 us
  transfers between devices with their start and end apart: 11 -> 8, of which waited for: 8 -> 5; matrix products, arithmetic and copies ran while one was open for 0% -> 0% of each run, Pallas kernels for 2% -> 1%
where the time goes in v3:
time: 152 us
  blocking collectives  61.1 us (40%)
  starting transfers between devices  41.5 us (27%)
  waiting for transfers between devices  30.7 us (20%)
  Pallas kernels  12.1 us (8%)
  local copies, waits for them, and re-layouts  4.99 us (3%)
    all_to_all x1, blocking collectives, body(): fields = lax.all_to_all(spread, OP, 0, 0)  22.5 us
    all_to_all x1, blocking collectives, summed(): received = lax.all_to_all(parts, OP, 0, 0)  22.4 us
    all_to_all x1, starting transfers between devices, summed(): gathered = lax.all_to_all(scalars, SEC, 0, 0)  16.8 us
    all_to_all x1, blocking collectives, summed(): gathered = lax.all_to_all(scalars, SEC, 0, 0)  16.2 us
    all_to_all x1, waiting for transfers between devices, summed(): received = lax.all_to_all(parts, OP, 0, 0)  12.3 us
    all_to_all x1, waiting for transfers between devices, summed(): gathered = lax.all_to_all(scalars, SEC, 0, 0)  12.1 us
    ppermute x1, starting transfers between devices, body(): other = lax.ppermute(send, 'c', [(0, 1), (1, 0)])  8.19 us
    all_to_all x1, starting transfers between devices, summed(): received = lax.all_to_all(parts, OP, 0, 0)  7.06 us
  transfers between devices with their start and end apart: 8, of which 5 were waited for; matrix products, arithmetic and copies ran while one was open for 0% of the time, Pallas kernels for 1%

profile of v3, /device:TPU:1, one launch (start us, length us, event | category | flops | bytes accessed | tf_op | source)
XLA Modules:
  0.0 151.6 jit_solution(4619140999459570244)
XLA Ops:
  0.6 0.1 pad_add_fusion.place_ref
  0.7 1.2 copy-done
  1.9 1.2 copy-done.3
  3.2 1.2 copy-done.6
  4.4 1.6 %shard_map.94 = (bf16[512,512]{1,0:T(8,128)(2,1)S(1)}, bf16[2,512,512]{2,1,0:T(8,128)(2,1)}) custom-call(s32[3]{0:T(128)S(1)} %pad_add_fusion.place_ref, bf16[2,512,512]{2,1,0:T(8,128)(2,1)S(1)} %copy-done, bf16[1,2,512,512]{3,2,1,0:T(8,128)(2,1)S(1)} %copy-done.3, bf16[1,2,512,512]{3,2,1,0:T(8,128)(2,1)S(1)} %copy-done.6), custom_call_target="tpu_custom_call" | custom-call | bytes 1048576 | tf_op jit(solution)/shard_map/pallas_call | solution.py:288
  6.0 1.3 collective-permute-start
  7.3 8.2 %collective-permute-start.1 = (bf16[2,512,512]{2,1,0:T(8,128)(2,1)}, bf16[2,512,512]{2,1,0:T(8,128)(2,1)S(1)}, u32[]{:S(2)}, u32[]{:S(2)}) collective-permute-start(bf16[2,512,512]{2,1,0:T(8,128)(2,1)} %get-tuple-element.24), channel_id=1, source_target_pairs={{0,32},{32,0},{1,33},{33,1},{2,34},{34,2},{3,35},{35,3},{4,36},{36... | collective-permute-start | bytes 3145736 | tf_op jit(solution)/shard_map/ppermute | solution.py:297
  15.5 0.0 copy-done.14
  15.5 0.1 constant_dynamic-slice_fusion.1
  15.6 0.0 copy-done.13
  15.6 0.1 broadcast_add_fusion.diagonal_ref
  15.7 0.0 copy-start.4
  15.7 0.0 copy-start.7
  15.7 0.0 copy-start.12
  15.7 1.2 collective-permute-done.halo_ref
  16.9 0.0 copy-done.1
  16.9 0.0 copy-done.9
  16.9 0.9 shard_map.95
  17.8 0.2 collective-permute-done.1.other_ref
  18.0 0.0 copy-done.12
  18.0 3.0 %shard_map.96 = bf16[16,72,512]{2,1,0:T(8,128)(2,1)S(1)} custom-call(s32[3]{0:T(128)S(1)} %pad_add_fusion.place_ref, s32[64]{0:T(128)S(1)} %copy-done.12, bf16[2,512,512]{2,1,0:T(8,128)(2,1)S(1)} %get-tuple-element.22.field_ref, f32[2,32,512]{2,1,0:T(8,128)S(1)} %get-tuple-element.23.rows_ref, f32[2,32,512]{2,1,0:T(8,128)S(1)} %broadcast_add_fusion.diagonal_ref, ...), custom_call_target="tpu_custom_call" | custom-call | flops 2147483648 | bytes 4194304 | tf_op jit(solution)/shard_map/pallas_call | solution.py:331
  21.0 1.0 copy-done.2
  22.1 7.1 %all-to-all-start = ((bf16[16,72,512]{2,1,0:T(8,128)(2,1)}), bf16[16,72,512]{2,1,0:T(8,128)(2,1)S(1)}, u32[]{:S(2)}, u32[]{:S(2)}) async-start(bf16[16,72,512]{2,1,0:T(8,128)(2,1)} %copy-done.2), calls=%async_computation | async-start | bytes 2359296 | tf_op jit(solution)/shard_map/all_to_all | solution.py:318
  29.1 0.1 pad.3.clone
  29.2 0.1 maximum_maximum_fusion
  29.3 1.3 collective-permute-start.4
  30.6 4.9 %collective-permute-done.4.next_rows_ref = f32[40,512]{1,0:T(8,128)S(1)} collective-permute-done((f32[40,512]{1,0:T(8,128)S(1)}, f32[40,512]{1,0:T(8,128)S(1)}, u32[]{:S(2)}, u32[]{:S(2)}) %collective-permute-start.4) | collective-permute-done | bytes 81952 | tf_op jit(solution)/shard_map/ppermute | solution.py:314
  35.6 0.1 fusion
  35.6 12.3 %all-to-all-done.received_ref = bf16[16,72,512]{2,1,0:T(8,128)(2,1)S(1)} async-done(((bf16[16,72,512]{2,1,0:T(8,128)(2,1)}), bf16[16,72,512]{2,1,0:T(8,128)(2,1)S(1)}, u32[]{:S(2)}, u32[]{:S(2)}) %all-to-all-start) | async-done | bytes 1179680 | tf_op jit(solution)/shard_map/all_to_all | solution.py:318
  47.9 0.1 shard_map.98
  48.0 3.5 %collective-permute-start.2 = (f32[32,512]{1,0:T(8,128)S(1)}, f32[32,512]{1,0:T(8,128)S(1)}, u32[]{:S(2)}, u32[]{:S(2)}) collective-permute-start(f32[32,512]{1,0:T(8,128)S(1)} %get-tuple-element.27.leaving_ref), channel_id=1, source_target_pairs={{0,1},{1,2},{2,3},{3,4},{4,5},{5,6},{6,7},{7,8},{8,9},{9,10},{10,1... | collective-permute-start | bytes 196616 | tf_op jit(solution)/shard_map/ppermute | solution.py:335
  51.6 1.3 collective-permute-start.3
  52.9 0.6 shard_map.97
  53.5 16.8 %all-to-all-start.1 = ((f32[32,1,128]{2,1,0:T(1,128)}), f32[32,1,128]{2,1,0:T(1,128)S(1)}, u32[]{:S(2)}, u32[]{:S(2)}) async-start(f32[32,1,128]{2,1,0:T(1,128)} %shard_map.97), calls=%async_computation.1 | async-start | bytes 32768 | tf_op jit(solution)/shard_map/all_to_all | solution.py:320
  70.3 0.1 broadcast_add_fusion.1.next_diagonal_ref
  70.4 12.1 %all-to-all-done.1.gathered_ref = f32[32,1,128]{2,1,0:T(1,128)S(1)} async-done(((f32[32,1,128]{2,1,0:T(1,128)}), f32[32,1,128]{2,1,0:T(1,128)S(1)}, u32[]{:S(2)}, u32[]{:S(2)}) %all-to-all-start.1) | async-done | bytes 16416 | tf_op jit(solution)/shard_map/all_to_all | solution.py:320
  82.5 0.0 collective-permute-done.2.arrived_ref
  82.5 0.0 collective-permute-done.3.ahead_ref
  82.5 0.9 shard_map.99
  83.5 22.5 %all_to_all.25.gathered_ref = bf16[16,64,512]{2,1,0:T(8,128)(2,1)S(1)} all-to-all(bf16[16,64,512]{2,1,0:T(8,128)(2,1)S(1)} %get-tuple-element.28), channel_id=1, replica_groups=mesh['yh'=2,'x'=4,'c'=2,'yl'=2,'z'=16] {'yh','x','c'}, dimensions={0} | all-to-all | bytes 2097152 | tf_op jit(solution)/shard_map/all_to_all | solution.py:348
  106.0 0.0 copy-done.11
  106.0 3.0 %shard_map.100 = bf16[16,72,512]{2,1,0:T(8,128)(2,1)S(1)} custom-call(s32[3]{0:T(128)S(1)} %pad_add_fusion.place_ref, s32[64]{0:T(128)S(1)} %copy-done.12, bf16[16,64,512]{2,1,0:T(8,128)(2,1)S(1)} %all_to_all.25.gathered_ref, f32[1,512]{1,0:T(1,128)S(1)} %get-tuple-element.29.scalar_ref, bf16[1,2,512,512]{3,2,1,0:T(8,128)(2,1)S(1)} %copy-done.5, ...), custom_call_target="tpu_custom_call" | custom-call | flops 2147483648 | bytes 4194304 | tf_op jit(solution)/shard_map/pallas_call | solution.py:349
  109.0 22.4 %all_to_all.26.received_ref = bf16[16,72,512]{2,1,0:T(8,128)(2,1)S(1)} all-to-all(bf16[16,72,512]{2,1,0:T(8,128)(2,1)S(1)} %shard_map.100), channel_id=1, replica_groups=mesh['yh'=2,'x'=4,'c'=2,'yl'=2,'z'=16] {'yh','x','c'}, dimensions={0} | all-to-all | bytes 2359296 | tf_op jit(solution)/shard_map/all_to_all | solution.py:318
  131.4 0.1 shard_map.102
  131.6 2.1 %collective-permute-start.5 = (f32[32,512]{1,0:T(8,128)S(1)}, f32[32,512]{1,0:T(8,128)S(1)}, u32[]{:S(2)}, u32[]{:S(2)}) collective-permute-start(f32[32,512]{1,0:T(8,128)S(1)} %get-tuple-element.33), channel_id=1, source_target_pairs={{0,1},{1,2},{2,3},{3,4},{4,5},{5,6},{6,7},{7,8},{8,9},{9,10},{10,1... | collective-permute-start | bytes 196616 | tf_op jit(solution)/shard_map/ppermute | solution.py:353
  133.7 16.2 %all_to_all.27.gathered_ref = f32[32,1,128]{2,1,0:T(1,128)S(1)} all-to-all(f32[32,1,128]{2,1,0:T(1,128)S(1)} %shard_map.101), channel_id=1, replica_groups=mesh['yh'=2,'x'=4,'c'=2,'yl'=2,'z'=16] {'yl','z'}, dimensions={0} | all-to-all | bytes 32768 | tf_op jit(solution)/shard_map/all_to_all | solution.py:320
  149.9 0.0 collective-permute-done.5.arrived_ref
  149.9 1.8 %shard_map.103 = (bf16[2,32,512]{2,1,0:T(8,128)(2,1)}, bf16[2,32,512]{2,1,0:T(8,128)(2,1)}, f32[1,2]{1,0:T(1,128)}) custom-call(s32[3]{0:T(128)S(1)} %pad_add_fusion.place_ref, s32[64]{0:T(128)S(1)} %copy-done.9, f32[32,1,128]{2,1,0:T(1,128)S(1)} %all_to_all.27.gathered_ref, f32[1,128]{1,0:T(1,128)S(1)} %get-tuple-element.30.known_ref, ...), custom_call_target="tpu_custom_call" | custom-call | bytes 1048576 | tf_op jit(solution)/shard_map/pallas_call | solution.py:355
  (27 shorter events, 0.1 us)
Async XLA Ops:
  0.7 1.2 copy-start
  1.9 1.2 copy-start.3
  3.2 1.2 copy-start.6
  4.4 11.1 %copy-start.14 = (f32[2,512]{1,0:T(2,128)S(1)}, f32[2,512]{1,0:T(2,128)}, u32[]{:S(2)}) copy-start(f32[2,512]{1,0:T(2,128)} %param.10) | copy-start | bytes 12292
  4.4 11.2 %copy-start.13 = (f32[2,512]{1,0:T(2,128)S(1)}, f32[2,512]{1,0:T(2,128)}, u32[]{:S(2)}) copy-start(f32[2,512]{1,0:T(2,128)} %param.11) | copy-start | bytes 12292
  4.4 12.5 %copy-start.1 = (bf16[2,512,512]{2,1,0:T(8,128)(2,1)S(1)}, bf16[2,512,512]{2,1,0:T(8,128)(2,1)}, u32[]{:S(2)}) copy-start(bf16[2,512,512]{2,1,0:T(8,128)(2,1)} %start_ref.3) | copy-start | bytes 3145732
  4.4 12.5 %copy-start.9 = (s32[64]{0:T(128)S(1)}, s32[64]{0:T(128)}, u32[]{:S(2)}) copy-start(s32[64]{0:T(128)} %size_ref.5) | copy-start | bytes 772
  6.0 10.9 %collective-permute-start = (bf16[512,512]{1,0:T(8,128)(2,1)S(1)}, bf16[512,512]{1,0:T(8,128)(2,1)S(1)}, u32[]{:S(2)}, u32[]{:S(2)}) collective-permute-start(bf16[512,512]{1,0:T(8,128)(2,1)S(1)} %get-tuple-element.21), channel_id=1, source_target_pairs={{33,32},{34,33},{35,34},{36,35},{37,36},{38,37},{39,38},{40,39},{4... | collective-permute-start | bytes 1572872 | tf_op jit(solution)/shard_map/ppermute | solution.py:296
  7.3 10.7 %collective-permute-start.1 = (bf16[2,512,512]{2,1,0:T(8,128)(2,1)}, bf16[2,512,512]{2,1,0:T(8,128)(2,1)S(1)}, u32[]{:S(2)}, u32[]{:S(2)}) collective-permute-start(bf16[2,512,512]{2,1,0:T(8,128)(2,1)} %get-tuple-element.24), channel_id=1, source_target_pairs={{0,32},{32,0},{1,33},{33,1},{2,34},{34,2},{3,35},{35,3},{4,36},{36... | collective-permute-start | bytes 3145736 | tf_op jit(solution)/shard_map/ppermute | solution.py:297
  15.7 2.3 %copy-start.4 = (bf16[1,2,512,512]{3,2,1,0:T(8,128)(2,1)S(1)}, bf16[1,2,512,512]{3,2,1,0:T(8,128)(2,1)}, u32[]{:S(2)}) copy-start(bf16[1,2,512,512]{3,2,1,0:T(8,128)(2,1)} %left_ref.5) | copy-start | bytes 3145732
  15.7 2.3 %copy-start.7 = (bf16[1,2,512,512]{3,2,1,0:T(8,128)(2,1)S(1)}, bf16[1,2,512,512]{3,2,1,0:T(8,128)(2,1)}, u32[]{:S(2)}) copy-start(bf16[1,2,512,512]{3,2,1,0:T(8,128)(2,1)} %right_ref.5) | copy-start | bytes 3145732
  15.7 2.3 %copy-start.12 = (s32[64]{0:T(128)S(1)}, s32[64]{0:T(128)}, u32[]{:S(2)}) copy-start(s32[64]{0:T(128)} %spin_ref.3) | copy-start | bytes 772
  18.0 3.1 %copy-start.10 = (bf16[2,512,512]{2,1,0:T(8,128)(2,1)}, bf16[2,512,512]{2,1,0:T(8,128)(2,1)S(1)}, u32[]{:S(2)}) copy-start(bf16[2,512,512]{2,1,0:T(8,128)(2,1)S(1)} %collective-permute-done.1.other_ref) | copy-start | bytes 3145732
  21.0 1.0 copy-start.2
  22.1 7.1 %slice-start = ((bf16[2,512,512]{2,1,0:T(8,128)(2,1)}), bf16[1,512,512]{2,1,0:T(8,128)(2,1)S(1)}, s32[]{:S(2)}) async-start(bf16[2,512,512]{2,1,0:T(8,128)(2,1)} %start_ref.3), calls=%async_computation.5 | async-start | bytes 1048576 | tf_op jit(solution)/shard_map/slice | solution.py:308
  22.1 7.2 %slice-start.1 = ((f32[2,512]{1,0:T(2,128)}), f32[1,512]{1,0:T(1,128)S(1)}, s32[]{:S(2)}) async-start(f32[2,512]{1,0:T(2,128)} %param.11), calls=%async_computation.6 | async-start | bytes 4096 | tf_op jit(solution)/shard_map/slice | solution.py:310
  22.1 7.2 %slice-start.2 = ((f32[2,512]{1,0:T(2,128)}), f32[1,512]{1,0:T(1,128)S(1)}, s32[]{:S(2)}) async-start(f32[2,512]{1,0:T(2,128)} %param.10), calls=%async_computation.7 | async-start | bytes 4096 | tf_op jit(solution)/shard_map/slice | solution.py:309
  22.1 25.8 %all-to-all-start = ((bf16[16,72,512]{2,1,0:T(8,128)(2,1)}), bf16[16,72,512]{2,1,0:T(8,128)(2,1)S(1)}, u32[]{:S(2)}, u32[]{:S(2)}) async-start(bf16[16,72,512]{2,1,0:T(8,128)(2,1)} %copy-done.2), calls=%async_computation | async-start | bytes 2359296 | tf_op jit(solution)/shard_map/all_to_all | solution.py:318
  29.3 6.2 %collective-permute-start.4 = (f32[40,512]{1,0:T(8,128)S(1)}, f32[40,512]{1,0:T(8,128)S(1)}, u32[]{:S(2)}, u32[]{:S(2)}) collective-permute-start(f32[40,512]{1,0:T(8,128)S(1)} %maximum_maximum_fusion), channel_id=1, source_target_pairs={{1,0},{2,1},{3,2},{4,3},{5,4},{6,5},{7,6},{8,7},{9,8},{10,9},{11,1... | collective-permute-start | bytes 245768 | tf_op jit(solution)/shard_map/ppermute | solution.py:314
  48.0 34.5 %collective-permute-start.2 = (f32[32,512]{1,0:T(8,128)S(1)}, f32[32,512]{1,0:T(8,128)S(1)}, u32[]{:S(2)}, u32[]{:S(2)}) collective-permute-start(f32[32,512]{1,0:T(8,128)S(1)} %get-tuple-element.27.leaving_ref), channel_id=1, source_target_pairs={{0,1},{1,2},{2,3},{3,4},{4,5},{5,6},{6,7},{7,8},{8,9},{9,10},{10,1... | collective-permute-start | bytes 196616 | tf_op jit(solution)/shard_map/ppermute | solution.py:335
  51.6 30.9 %collective-permute-start.3 = (f32[32,512]{1,0:T(8,128)S(1)}, f32[32,512]{1,0:T(8,128)S(1)}, u32[]{:S(2)}, u32[]{:S(2)}) collective-permute-start(f32[32,512]{1,0:T(8,128)S(1)} %get-tuple-element.25.first_ref), channel_id=1, source_target_pairs={{1,0},{2,1},{3,2},{4,3},{5,4},{6,5},{7,6},{8,7},{9,8},{10,9},{11,1... | collective-permute-start | bytes 196616 | tf_op jit(solution)/shard_map/ppermute | solution.py:336
  52.9 53.1 %copy-start.11 = (bf16[2,512,512]{2,1,0:T(8,128)(2,1)S(1)}, bf16[2,512,512]{2,1,0:T(8,128)(2,1)}, u32[]{:S(2)}) copy-start(bf16[2,512,512]{2,1,0:T(8,128)(2,1)} %copy-done.10) | copy-start | bytes 3145732
  53.5 29.0 %all-to-all-start.1 = ((f32[32,1,128]{2,1,0:T(1,128)}), f32[32,1,128]{2,1,0:T(1,128)S(1)}, u32[]{:S(2)}, u32[]{:S(2)}) async-start(f32[32,1,128]{2,1,0:T(1,128)} %shard_map.97), calls=%async_computation.1 | async-start | bytes 32768 | tf_op jit(solution)/shard_map/all_to_all | solution.py:320
  83.5 22.5 %copy-start.5 = (bf16[1,2,512,512]{3,2,1,0:T(8,128)(2,1)S(1)}, bf16[1,2,512,512]{3,2,1,0:T(8,128)(2,1)}, u32[]{:S(2)}) copy-start(bf16[1,2,512,512]{3,2,1,0:T(8,128)(2,1)} %left_ref.5) | copy-start | bytes 3145732
  83.5 22.5 %copy-start.8 = (bf16[1,2,512,512]{3,2,1,0:T(8,128)(2,1)S(1)}, bf16[1,2,512,512]{3,2,1,0:T(8,128)(2,1)}, u32[]{:S(2)}) copy-start(bf16[1,2,512,512]{3,2,1,0:T(8,128)(2,1)} %right_ref.5) | copy-start | bytes 3145732
  131.6 18.3 %collective-permute-start.5 = (f32[32,512]{1,0:T(8,128)S(1)}, f32[32,512]{1,0:T(8,128)S(1)}, u32[]{:S(2)}, u32[]{:S(2)}) collective-permute-start(f32[32,512]{1,0:T(8,128)S(1)} %get-tuple-element.33), channel_id=1, source_target_pairs={{0,1},{1,2},{2,3},{3,4},{4,5},{5,6},{6,7},{7,8},{8,9},{9,10},{10,1... | collective-permute-start | bytes 196616 | tf_op jit(solution)/shard_map/ppermute | solution.py:353

commit v4 on v3

v4 whole, which is shorter than its diff:
```python
import jax
import jax.numpy as jnp
from jax import lax
from jax.experimental import pallas as pl
from jax.experimental.pallas import tpu as pltpu
from jax.sharding import Mesh, PartitionSpec as P

F32 = jnp.float32
BF16 = jnp.bfloat16
OP = ("yh", "x", "c")
SEC = ("yl", "z")
WIDTH = 512
ROWS = 32
NOP = 16
BLOCKS = 3
LANES = 128
TILES = WIDTH // LANES
PART = 2 * ROWS * TILES + 16
VMEM_LIMIT = 24 * 1024 * 1024
WHOLE_VMEM = 62 * 1024 * 1024

VM = pl.BlockSpec(memory_space=pltpu.VMEM)
SM = pl.BlockSpec(memory_space=pltpu.SMEM)
HBM = pl.BlockSpec(memory_space=pltpu.HBM)


def call(
    kernel, out_shape, in_specs, scratch=(), flops=0, nbytes=1 << 20, vmem=VMEM_LIMIT
):
    return pl.pallas_call(
        kernel,
        out_shape=out_shape,
        in_specs=in_specs,
        out_specs=jax.tree.map(lambda _: VM, out_shape),
        scratch_shapes=list(scratch),
        compiler_params=pltpu.CompilerParams(vmem_limit_bytes=vmem),
        cost_estimate=pl.CostEstimate(flops=flops, bytes_accessed=nbytes, transcendentals=0),
    )


def shaped(shape, dtype):
    return jax.ShapeDtypeStruct(shape, dtype)


def product(first, second, second_axis=0):
    return lax.dot_general(
        first, second, (((1,), (second_axis,)), ((), ())), preferred_element_type=F32
    )


def total(array):
    return jnp.sum(jnp.sum(array, axis=0, keepdims=True), axis=1, keepdims=True)


def lanes(values, width):
    place = lax.broadcasted_iota(jnp.int32, (1, width), 1)
    row = jnp.zeros((1, width), F32)
    for index, value in enumerate(values):
        row = jnp.where(place == index, value, row)
    return row


def own_rows(place_ref):
    return pl.multiple_of(place_ref[1] * ROWS, ROWS)


def inside(size, first_row, shape):
    rows = lax.broadcasted_iota(jnp.int32, shape, 0) + first_row
    columns = lax.broadcasted_iota(jnp.int32, shape, 1)
    return (rows < size) & (columns < size)


def size_of(place_ref, size_ref, block):
    return size_ref[jnp.minimum(place_ref[2] + block, size_ref.shape[0] - 1)]


def diagonal_of(left_row, right_row, first_row):
    rows = lax.broadcasted_iota(jnp.int32, (ROWS, WIDTH), 0) + first_row
    columns = lax.broadcasted_iota(jnp.int32, (ROWS, WIDTH), 1)
    chosen = jnp.where(rows == columns, left_row, 0.0)
    return jnp.sum(chosen, axis=1, keepdims=True) + right_row


def open_kernel(start_ref, left_ref, right_ref, halo_ref, send_ref, semaphores):
    there = 1 - lax.axis_index("c")
    copies = [
        pltpu.make_async_copy(start_ref.at[0], halo_ref, semaphores.at[0]),
        pltpu.make_async_copy(left_ref.at[0, there], send_ref.at[0], semaphores.at[1]),
        pltpu.make_async_copy(right_ref.at[0, there], send_ref.at[1], semaphores.at[2]),
    ]
    for copy in copies:
        copy.start()
    for copy in copies:
        copy.wait()


def rows_kernel(
    place_ref, size_ref, start_ref, left_levels_ref, right_levels_ref,
    rows_ref, diagonal_ref, scalar_ref, before_ref,
):
    first_row = own_rows(place_ref)
    norm = jnp.zeros((ROWS, WIDTH), F32)
    energy = jnp.zeros((ROWS, WIDTH), F32)
    for block in range(2):
        mask = inside(size_of(place_ref, size_ref, block), first_row, (ROWS, WIDTH))
        own = jnp.where(mask, start_ref[block, pl.ds(first_row, ROWS)].astype(F32), 0.0)
        rows_ref[block] = own
        square = own * own
        norm = norm + square
        diagonal = diagonal_of(
            left_levels_ref[block : block + 1], right_levels_ref[block : block + 1], first_row
        )
        diagonal_ref[block] = diagonal
        energy = energy + diagonal * square
    scalar_ref[...] = lanes([total(energy), total(norm)], LANES)
    before_ref[:ROWS] = rows_ref[0]
    place = lax.broadcasted_iota(jnp.int32, (8, WIDTH), 0)
    before_ref[ROWS:] = jnp.where(
        place == 0, left_levels_ref[0:1], jnp.where(place == 1, right_levels_ref[0:1], 0.0)
    )


def mask_kernel(place_ref, size_ref, start_ref, halo_ref, field_ref):
    core = place_ref[0]

    def masked(source, block):
        mask = inside(size_of(place_ref, size_ref, block), 0, (WIDTH, WIDTH))
        return jnp.where(mask, source.astype(F32), 0.0).astype(BF16)

    field_ref[0] = masked(start_ref[core], core)

    @pl.when(core == 0)
    def _():
        field_ref[1] = masked(start_ref[1], 1)

    @pl.when(core == 1)
    def _():
        field_ref[1] = masked(halo_ref[...], 2)


def images(place_ref, spin_ref, left_ref, right_ref, other_ref, field, after):
    core = place_ref[0]
    here = place_ref[2] + core
    following = jnp.minimum(here + 1, spin_ref.shape[0] - 1)
    above = jnp.full((1, WIDTH), spin_ref[following], jnp.int32).astype(F32) + 1.0
    below = jnp.full((1, WIDTH), spin_ref[here], jnp.int32).astype(F32) + 1.0
    linked = jnp.full((1, WIDTH), here, jnp.int32) + 1 < spin_ref.shape[0]
    coupling = jnp.where(linked, jnp.sqrt(above / below), 0.0)
    lowered = raised = None
    for left, right in (
        (left_ref[0, core], right_ref[0, core]),
        (other_ref[0], other_ref[1]),
    ):
        up = product(left, product(field, right, 1).astype(BF16))
        down = product(product(left.T, after).astype(BF16), right)
        raised = up if raised is None else raised + up
        lowered = down if lowered is None else lowered + down
    return coupling * lowered, coupling * raised


def put_parts(lowered, raised, after, scalars, parts_ref):
    energy = 2.0 * total(raised * after.astype(F32))
    row = lanes([energy], LANES) + scalars
    high = row.astype(BF16).astype(F32)
    middle = (row - high).astype(BF16).astype(F32)
    low = (row - high) - middle
    place = lax.broadcasted_iota(jnp.int32, (16, LANES), 0)
    coded = jnp.where(
        place == 0, high, jnp.where(place == 1, middle, jnp.where(place == 2, low, 0.0))
    ).astype(BF16)
    for device in range(NOP):
        here = slice(device * ROWS, (device + 1) * ROWS)
        for index, image in enumerate((lowered, raised)):
            rounded = image[here].astype(BF16)
            for tile in range(TILES):
                there = (index * TILES + tile) * ROWS
                columns = slice(tile * LANES, (tile + 1) * LANES)
                parts_ref[device, there : there + ROWS] = rounded[:, columns]
        parts_ref[device, 2 * ROWS * TILES :] = coded


def first_kernel(
    place_ref, spin_ref, field_ref, scalar_ref, left_ref, right_ref, other_ref, parts_ref
):
    after = field_ref[1]
    lowered, raised = images(
        place_ref, spin_ref, left_ref, right_ref, other_ref, field_ref[0], after
    )
    put_parts(lowered, raised, after, scalar_ref[...], parts_ref)


def second_kernel(
    place_ref, spin_ref, gathered_ref, scalar_ref, left_ref, right_ref, other_ref, parts_ref
):
    field = gathered_ref[:, :ROWS].reshape(WIDTH, WIDTH)
    after = gathered_ref[:, ROWS:].reshape(WIDTH, WIDTH)
    lowered, raised = images(place_ref, spin_ref, left_ref, right_ref, other_ref, field, after)
    put_parts(lowered, raised, after, scalar_ref[...], parts_ref)


def sum_kernel(
    received_ref, first_ref, second_ref, first_sent_ref, leaving_sent_ref, scalar_ref
):
    coded = jnp.zeros((16, LANES), F32)
    for device in range(NOP):
        coded = coded + received_ref[device, 2 * ROWS * TILES :].astype(F32)
    row = jnp.concatenate([jnp.sum(coded, axis=0, keepdims=True)] * 2, axis=1)
    scalar_ref[...] = jnp.broadcast_to(row[None], scalar_ref.shape)
    for tile in range(TILES):
        sums = [jnp.zeros((ROWS, LANES), F32) for _ in range(BLOCKS)]
        for device in range(NOP):
            for index in range(2):
                there = (index * TILES + tile) * ROWS
                block = device % 2 + index
                sums[block] = sums[block] + received_ref[device, there : there + ROWS].astype(F32)
        columns = slice(tile * LANES, (tile + 1) * LANES)
        first_ref[:, columns] = sums[0]
        second_ref[:, columns] = sums[1]
        first_sent_ref[:, columns] = sums[0].astype(BF16)
        leaving_sent_ref[:, columns] = sums[2].astype(BF16)


def scalars_of(gathered_ref, count):
    row = jnp.sum(gathered_ref[...], axis=0)
    return [row[:, index : index + 1] for index in range(count)]


def correction_kernel(
    place_ref, size_ref, gathered_ref, first_ref, second_ref, leaving_ref, arrived_ref,
    ahead_ref, diagonal_ref, rows_ref, beyond_ref,
    spread_ref, image_ref, change_ref, scalar_ref, known_ref,
):
    energy, norm = scalars_of(gathered_ref, 2)
    rayleigh = energy / norm
    scale = jnp.sqrt(norm)
    first_row = own_rows(place_ref)
    sums = [
        first_ref[...].astype(F32) + arrived_ref[...].astype(F32),
        second_ref[...],
        leaving_ref[...].astype(F32) + ahead_ref[...].astype(F32),
    ]
    amounts = [jnp.zeros((ROWS, WIDTH), F32) for _ in range(4)]
    for block in range(BLOCKS):
        mask = inside(size_of(place_ref, size_ref, block), first_row, (ROWS, WIDTH))
        if block == 2:
            values = beyond_ref[:ROWS]
            diagonal = diagonal_of(
                beyond_ref[ROWS : ROWS + 1], beyond_ref[ROWS + 1 : ROWS + 2], first_row
            )
        else:
            values = rows_ref[block]
            diagonal = diagonal_ref[block]
        unit = values / scale
        image = jnp.where(mask, sums[block] + diagonal * values, 0.0) / scale
        residual = image - rayleigh * unit
        change = residual / (jnp.abs(diagonal - rayleigh) + 1.0)
        rounded = change.astype(BF16)
        for device in range(NOP):
            part = block - device % 2
            if part in (0, 1):
                spread_ref[device, part * ROWS : (part + 1) * ROWS] = rounded
        if block < 2:
            image_ref[block] = image
            change_ref[block] = change
            again = rounded.astype(F32)
            amounts[0] = amounts[0] + diagonal * again * again
            amounts[1] = amounts[1] + unit * change
            amounts[2] = amounts[2] + change * change
            amounts[3] = amounts[3] + change * image
    scalar_ref[...] = lanes([total(amount) for amount in amounts], LANES)
    known_ref[...] = lanes([rayleigh, scale], LANES)


def ritz_kernel(
    place_ref, size_ref, gathered_ref, known_ref, first_ref, second_ref, arrived_ref,
    diagonal_ref, rows_ref, image_ref, change_ref,
    vector_ref, residual_ref, energies_ref,
):
    change_energy, correlation, square, change_image = scalars_of(gathered_ref, 4)
    rayleigh = known_ref[:, 0:1]
    scale = known_ref[:, 1:2]
    spread = square - correlation * correlation
    deviation = jnp.sqrt(spread)
    cross_term = (change_image - correlation * rayleigh) / deviation
    second_energy = (
        change_energy - 2.0 * correlation * change_image + correlation * correlation * rayleigh
    ) / spread
    half_gap = 0.5 * (rayleigh - second_energy)
    length = jnp.sqrt(half_gap * half_gap + cross_term * cross_term)
    lowest = 0.5 * (rayleigh + second_energy) - length
    apart = length > 0.0
    divisor = jnp.where(apart, length, 1.0)
    double_cosine = jnp.where(apart, half_gap / divisor, 1.0)
    double_sine = jnp.where(apart, cross_term / divisor, 0.0)
    larger = jnp.sqrt(0.5 * (1.0 + jnp.abs(double_cosine)))
    smaller = 0.5 * double_sine / larger
    ahead = double_cosine >= 0.0
    sign = jnp.where(cross_term < 0.0, -1.0, 1.0)
    cosine_angle = jnp.where(ahead, larger, jnp.abs(smaller))
    sine_angle = jnp.where(ahead, smaller, sign * larger)
    first_row = own_rows(place_ref)
    sums = [first_ref[...] + arrived_ref[...].astype(F32), second_ref[...]]
    for block in range(2):
        mask = inside(size_of(place_ref, size_ref, block), first_row, (ROWS, WIDTH))
        unit = rows_ref[block] / scale
        image = image_ref[block]
        change = change_ref[block]
        rounded = change.astype(BF16).astype(F32)
        change_picture = jnp.where(mask, sums[block] + diagonal_ref[block] * rounded, 0.0)
        unit_second = (change - correlation * unit) / deviation
        second_image = (change_picture - correlation * image) / deviation
        ritz_unit = sine_angle * unit - cosine_angle * unit_second
        vector_ref[block] = (scale * ritz_unit).astype(BF16)
        residual_ref[block] = (
            scale * (sine_angle * image - cosine_angle * second_image - lowest * ritz_unit)
        ).astype(BF16)
    energies_ref[...] = lanes([rayleigh, lowest], 2)


def line(distance):
    devices = range(lax.axis_size(SEC))
    return [(i, i + distance) for i in devices if i + distance in devices]


def body(start, left, right, left_energy, right_energy, sector_size, sector_spin):
    core = lax.axis_index("c")
    position = lax.axis_index(OP)
    sectors = lax.axis_size(SEC)
    place = jnp.stack([core, position, 2 * lax.axis_index(SEC)]).astype(jnp.int32)
    block_shape = shaped((WIDTH, WIDTH), BF16)
    two_shape = shaped((2, WIDTH, WIDTH), BF16)
    own_shape = shaped((2, ROWS, WIDTH), F32)
    row_shape = shaped((ROWS, WIDTH), F32)
    lane_shape = shaped((1, LANES), F32)
    parts_shape = shaped((NOP, PART, LANES), BF16)
    work = 16 * WIDTH * WIDTH * WIDTH

    halo_source, send = call(
        open_kernel, (block_shape, two_shape), [HBM] * 3, [pltpu.SemaphoreType.DMA((3,))],
        vmem=WHOLE_VMEM,
    )(start, left, right)
    to_second_core = [(sectors + i + 1, sectors + i) for i in range(sectors - 1)]
    halo = lax.ppermute(halo_source, ("c",) + SEC, to_second_core)
    other = lax.ppermute(send, "c", [(0, 1), (1, 0)])
    rows, diagonal, amounts, before = call(
        rows_kernel,
        (own_shape, own_shape, lane_shape, shaped((ROWS + 8, WIDTH), F32)),
        [SM] * 2 + [VM] * 3,
    )(place, sector_size, start, left_energy, right_energy)
    beyond = lax.ppermute(before, SEC, line(-1))
    field = call(mask_kernel, two_shape, [SM] * 2 + [VM] * 2, flops=4 * work)(
        place, sector_size, start, halo
    )

    def summed(received):
        sent_shape = shaped((ROWS, WIDTH), BF16)
        scalar_shape = shaped((sectors, 1, 2 * LANES), F32)
        *sums, scalars = call(
            sum_kernel, (row_shape,) * 2 + (sent_shape,) * 2 + (scalar_shape,), [VM]
        )(received)
        return (*sums, lax.all_to_all(scalars, SEC, 0, 0))

    parts = call(first_kernel, parts_shape, [SM] * 2 + [VM] * 5, flops=work, nbytes=4 << 20)(
        place, sector_spin, field, amounts, left, right, other
    )
    received = lax.all_to_all(parts, OP, 0, 0)
    received, beyond = lax.optimization_barrier((received, beyond))
    first, second, first_sent, leaving_sent, gathered = summed(received)
    arrived = lax.ppermute(leaving_sent, SEC, line(1))
    ahead = lax.ppermute(first_sent, SEC, line(-1))
    spread, image, change, amounts, known = call(
        correction_kernel,
        (shaped((NOP, 2 * ROWS, WIDTH), BF16), own_shape, own_shape, lane_shape, lane_shape),
        [SM] * 2 + [VM] * 9,
    )(
        place, sector_size, gathered, first_sent, second, leaving_sent, arrived, ahead,
        diagonal, rows, beyond,
    )
    fields = lax.all_to_all(spread, OP, 0, 0)
    parts = call(second_kernel, parts_shape, [SM] * 2 + [VM] * 5, flops=work, nbytes=4 << 20)(
        place, sector_spin, fields, amounts, left, right, other
    )
    first, second, first_sent, leaving_sent, gathered = summed(lax.all_to_all(parts, OP, 0, 0))
    arrived = lax.ppermute(leaving_sent, SEC, line(1))
    result = shaped((2, ROWS, WIDTH), BF16)
    vector, residual, energies = call(
        ritz_kernel, (result, result, shaped((1, 2), F32)), [SM] * 2 + [VM] * 9
    )(
        place, sector_size, gathered, known, first, second, arrived,
        diagonal, rows, image, change,
    )
    return vector, residual, energies.reshape(2)


def solution(mesh):
    fine = Mesh(mesh.devices.reshape(2, 4, 2, 2, 16), ("yh", "x", "c", "yl", "z"))
    return jax.shard_map(
        body,
        mesh=fine,
        in_specs=(
            P(SEC, None, None),
            P(OP, SEC, None, None),
            P(OP, SEC, None, None),
            P(SEC, None),
            P(SEC, None),
            P(),
            P(),
        ),
        out_specs=(P(SEC, OP, None), P(SEC, OP, None), P()),
        check_vma=False,
    )
```

time: 152 us -> 146 us (0.961)
  blocking collectives: 61.1 us -> 43.9 us
  starting transfers between devices: 41.5 us -> 49.8 us
  local copies, waits for them, and re-layouts: 4.99 us -> 1.27 us
  waiting for transfers between devices: 30.7 us -> 34.3 us
  Pallas kernels: 12.1 us -> 15.3 us
    all_to_all x2 -> x1, blocking collectives: 38.6 us -> 21.9 us  [body(): lax.all_to_all(parts, OP, 0, 0)]
    all_to_all x2 -> x3, starting transfers between devices: 23.8 us -> 30.6 us  [the longest x2 23.6 us: summed(): return (*sums, lax.all_to_all(scalars, SEC, 0, 0))]
    unnamed x30 -> x22, local copies, waits for them, and re-layouts: 4.75 us -> 1.27 us
    pallas_call x7 -> x6, Pallas kernels: 6.4 us -> 9.61 us  [the longest x1 4.03 us: body(): call(first_kernel, parts_shape, [SM] * 2 + [VM] * 5, flops=work, nbytes=4...]
    ppermute x3, waiting for transfers between devices: 0.01 us -> 2.13 us  [the longest x2 2.13 us: body(): arrived = lax.ppermute(leaving_sent, SEC, line(1))]
    all_to_all x2 -> x3, waiting for transfers between devices: 24.4 us -> 26.4 us  [the longest x2 14.5 us: summed(): return (*sums, lax.all_to_all(scalars, SEC, 0, 0))]
  transfers between devices with their start and end apart: 8 -> 9, of which waited for: 5 -> 7; matrix products, arithmetic and copies ran while one was open for 0% -> 0% of each run, Pallas kernels for 1% -> 1%
where the time goes in v4:
time: 146 us; the launch traced here: 145 us
  starting transfers between devices  49.8 us (34%)
  blocking collectives  43.9 us (30%)
  waiting for transfers between devices  34.3 us (23%)
  Pallas kernels  15.3 us (10%)
    all_to_all x2, starting transfers between devices, summed(): return (*sums, lax.all_to_all(scalars, SEC, 0, 0))  23.6 us
    all_to_all x1, blocking collectives, body(): fields = lax.all_to_all(spread, OP, 0, 0)  22 us
    all_to_all x1, blocking collectives, body(): lax.all_to_all(parts, OP, 0, 0)  21.9 us
    all_to_all x2, waiting for transfers between devices, summed(): return (*sums, lax.all_to_all(scalars, SEC, 0, 0))  14.5 us
    all_to_all x1, waiting for transfers between devices, body(): received = lax.all_to_all(parts, OP, 0, 0)  11.8 us
    ppermute x1, starting transfers between devices, body(): other = lax.ppermute(send, 'c', [(0, 1), (1, 0)])  8.19 us
    ppermute x2, starting transfers between devices, body(): arrived = lax.ppermute(leaving_sent, SEC, line(1))  7.12 us
    all_to_all x1, starting transfers between devices, body(): received = lax.all_to_all(parts, OP, 0, 0)  7.06 us
  transfers between devices with their start and end apart: 9, of which 7 were waited for; matrix products, arithmetic and copies ran while one was open for 0% of the time, Pallas kernels for 1%

profile of v4, /device:TPU:1, one launch (start us, length us, event | category | flops | bytes accessed | tf_op | source)
XLA Modules:
  0.0 145.5 jit_solution(17447047439228841922)
XLA Ops:
  0.6 0.0 copy-start
  0.6 0.0 copy-start.5
  0.7 0.0 copy-start.7
  0.7 0.0 copy-start.6
  0.7 2.7 %shard_map.94 = (bf16[512,512]{1,0:T(8,128)(2,1)}, bf16[2,512,512]{2,1,0:T(8,128)(2,1)}) custom-call(bf16[2,512,512]{2,1,0:T(8,128)(2,1)} %start_ref.5, bf16[1,2,512,512]{3,2,1,0:T(8,128)(2,1)} %left_ref.5, bf16[1,2,512,512]{3,2,1,0:T(8,128)(2,1)} %right_ref.5), custom_call_target="tpu_custom_call" | custom-call | bytes 1048576 | tf_op jit(solution)/shard_map/pallas_call | solution.py:338
  3.3 1.3 collective-permute-start
  4.6 8.2 %collective-permute-start.1 = (bf16[2,512,512]{2,1,0:T(8,128)(2,1)}, bf16[2,512,512]{2,1,0:T(8,128)(2,1)S(1)}, u32[]{:S(2)}, u32[]{:S(2)}) collective-permute-start(bf16[2,512,512]{2,1,0:T(8,128)(2,1)} %get-tuple-element.29), channel_id=1, source_target_pairs={{0,32},{32,0},{1,33},{33,1},{2,34},{34,2},{3,35},{35,3},{4,36},{36... | collective-permute-start | bytes 3145736 | tf_op jit(solution)/shard_map/ppermute | solution.py:344
  12.9 0.1 pad_add_fusion.place_ref
  12.9 0.0 copy-done
  12.9 0.0 copy-done.5
  12.9 0.0 copy-done.7
  12.9 0.0 copy-done.6
  12.9 0.7 shard_map.96
  13.7 0.0 copy-start.1
  13.7 0.0 copy-start.3
  13.7 0.8 collective-permute-done.halo_ref
  14.5 0.8 shard_map.95.field_ref
  15.3 0.0 collective-permute-done.1.other_ref
  15.3 0.0 copy-start.8
  15.3 0.0 copy-done.1
  15.4 0.0 copy-done.3
  15.4 0.0 copy-done.10
  15.4 4.0 %shard_map.97 = bf16[16,272,128]{2,1,0:T(8,128)(2,1)} custom-call(s32[3]{0:T(128)S(1)} %pad_add_fusion.place_ref, s32[64]{0:T(128)S(1)} %copy-done.10, bf16[2,512,512]{2,1,0:T(8,128)(2,1)S(1)} %shard_map.95.field_ref, f32[1,128]{1,0:T(1,128)S(1)} %get-tuple-element.28.scalar_ref, bf16[1,2,512,512]{3,2,1,0:T(8,128)(2,1)S(1)} %copy-done.1, ...), custom_call_target="tpu_custom_call" | custom-call | flops 2147483648 | bytes 4194304 | tf_op jit(solution)/shard_map/pallas_call | solution.py:363
  19.4 0.0 copy-done.8
  19.4 7.1 %all-to-all-start = ((bf16[16,272,128]{2,1,0:T(8,128)(2,1)}), bf16[16,272,128]{2,1,0:T(8,128)(2,1)S(1)}, u32[]{:S(2)}, u32[]{:S(2)}) async-start(bf16[16,272,128]{2,1,0:T(8,128)(2,1)} %shard_map.97), calls=%async_computation | async-start | bytes 2228224 | tf_op jit(solution)/shard_map/all_to_all | solution.py:366
  26.5 1.3 collective-permute-start.2
  27.8 4.9 %collective-permute-done.2.beyond_ref = f32[40,512]{1,0:T(8,128)S(1)} collective-permute-done((f32[40,512]{1,0:T(8,128)S(1)}, f32[40,512]{1,0:T(8,128)S(1)}, u32[]{:S(2)}, u32[]{:S(2)}) %collective-permute-start.2) | collective-permute-done | bytes 81952 | tf_op jit(solution)/shard_map/ppermute | solution.py:350
  32.7 11.8 %all-to-all-done.received_ref = bf16[16,272,128]{2,1,0:T(8,128)(2,1)S(1)} async-done(((bf16[16,272,128]{2,1,0:T(8,128)(2,1)}), bf16[16,272,128]{2,1,0:T(8,128)(2,1)S(1)}, u32[]{:S(2)}, u32[]{:S(2)}) %all-to-all-start) | async-done | bytes 1114144 | tf_op jit(solution)/shard_map/all_to_all | solution.py:366
  44.5 0.7 shard_map.98
  45.2 15.1 %all-to-all-start.1 = ((f32[32,1,256]{2,1,0:T(1,128)}), f32[32,1,256]{2,1,0:T(1,128)S(1)}, u32[]{:S(2)}, u32[]{:S(2)}) async-start(f32[32,1,256]{2,1,0:T(1,128)} %get-tuple-element.32), calls=%async_computation.1 | async-start | bytes 65536 | tf_op jit(solution)/shard_map/all_to_all | solution.py:361
  60.4 1.3 collective-permute-start.4
  61.7 4.0 %collective-permute-start.3 = (bf16[32,512]{1,0:T(8,128)(2,1)S(1)}, bf16[32,512]{1,0:T(8,128)(2,1)S(1)}, u32[]{:S(2)}, u32[]{:S(2)}) collective-permute-start(bf16[32,512]{1,0:T(8,128)(2,1)S(1)} %get-tuple-element.35.leaving_ref), channel_id=1, source_target_pairs={{0,1},{1,2},{2,3},{3,4},{4,5},{5,6},{6,7},{7,8},{8,9},{9,10},{10,1... | collective-permute-start | bytes 98312 | tf_op jit(solution)/shard_map/ppermute | solution.py:369
  65.7 0.0 collective-permute-done.4.ahead_ref
  65.7 1.0 collective-permute-done.3.arrived_ref
  66.7 6.2 %all-to-all-done.1.gathered_ref = f32[32,1,256]{2,1,0:T(1,128)S(1)} async-done(((f32[32,1,256]{2,1,0:T(1,128)}), f32[32,1,256]{2,1,0:T(1,128)S(1)}, u32[]{:S(2)}, u32[]{:S(2)}) %all-to-all-start.1) | async-done | bytes 32800 | tf_op jit(solution)/shard_map/all_to_all | solution.py:361
  72.9 0.9 shard_map.99
  73.8 22.0 %all_to_all.25.gathered_ref = bf16[16,64,512]{2,1,0:T(8,128)(2,1)S(1)} all-to-all(bf16[16,64,512]{2,1,0:T(8,128)(2,1)S(1)} %get-tuple-element.39), channel_id=1, replica_groups=mesh['yh'=2,'x'=4,'c'=2,'yl'=2,'z'=16] {'yh','x','c'}, dimensions={0} | all-to-all | bytes 2097152 | tf_op jit(solution)/shard_map/all_to_all | solution.py:379
  95.8 0.0 copy-done.2
  95.8 0.0 copy-done.4
  95.9 1.2 copy-done.9
  97.1 3.0 %shard_map.100 = bf16[16,272,128]{2,1,0:T(8,128)(2,1)S(1)} custom-call(s32[3]{0:T(128)S(1)} %pad_add_fusion.place_ref, s32[64]{0:T(128)S(1)} %copy-done.10, bf16[16,64,512]{2,1,0:T(8,128)(2,1)S(1)} %all_to_all.25.gathered_ref, f32[1,128]{1,0:T(1,128)S(1)} %get-tuple-element.40.scalar_ref, bf16[1,2,512,512]{3,2,1,0:T(8,128)(2,1)S(1)} %copy-done.2, ...), custom_call_target="tpu_custom_call" | custom-call | flops 2147483648 | bytes 4194304 | tf_op jit(solution)/shard_map/pallas_call | solution.py:380
  100.1 21.9 %all_to_all.26.received_ref = bf16[16,272,128]{2,1,0:T(8,128)(2,1)S(1)} all-to-all(bf16[16,272,128]{2,1,0:T(8,128)(2,1)S(1)} %shard_map.100), channel_id=1, replica_groups=mesh['yh'=2,'x'=4,'c'=2,'yl'=2,'z'=16] {'yh','x','c'}, dimensions={0} | all-to-all | bytes 2228224 | tf_op jit(solution)/shard_map/all_to_all | solution.py:383
  122.0 0.7 shard_map.101
  122.7 8.4 %all-to-all-start.4 = ((f32[32,1,256]{2,1,0:T(1,128)}), f32[32,1,256]{2,1,0:T(1,128)S(1)}, u32[]{:S(2)}, u32[]{:S(2)}) async-start(f32[32,1,256]{2,1,0:T(1,128)} %get-tuple-element.41), calls=%async_computation.4 | async-start | bytes 65536 | tf_op jit(solution)/shard_map/all_to_all | solution.py:361
  131.2 3.1 %collective-permute-start.5 = (bf16[32,512]{1,0:T(8,128)(2,1)S(1)}, bf16[32,512]{1,0:T(8,128)(2,1)S(1)}, u32[]{:S(2)}, u32[]{:S(2)}) collective-permute-start(bf16[32,512]{1,0:T(8,128)(2,1)S(1)} %get-tuple-element.45), channel_id=1, source_target_pairs={{0,1},{1,2},{2,3},{3,4},{4,5},{5,6},{6,7},{7,8},{8,9},{9,10},{10,1... | collective-permute-start | bytes 98312 | tf_op jit(solution)/shard_map/ppermute | solution.py:384
  134.3 1.1 collective-permute-done.5.arrived_ref
  135.4 8.3 %all-to-all-done.4.gathered_ref = f32[32,1,256]{2,1,0:T(1,128)S(1)} async-done(((f32[32,1,256]{2,1,0:T(1,128)}), f32[32,1,256]{2,1,0:T(1,128)S(1)}, u32[]{:S(2)}, u32[]{:S(2)}) %all-to-all-start.4) | async-done | bytes 32800 | tf_op jit(solution)/shard_map/all_to_all | solution.py:361
  143.7 1.8 %shard_map.102 = (bf16[2,32,512]{2,1,0:T(8,128)(2,1)}, bf16[2,32,512]{2,1,0:T(8,128)(2,1)}, f32[1,2]{1,0:T(1,128)}) custom-call(s32[3]{0:T(128)S(1)} %pad_add_fusion.place_ref, s32[64]{0:T(128)S(1)} %copy-done.5, f32[32,1,256]{2,1,0:T(1,128)S(1)} %all-to-all-done.4.gathered_ref, f32[1,128]{1,0:T(1,128)S(1)} %get-tuple-element.42.known_ref, ...), custom_call_target="tpu_custom_call" | custom-call | bytes 1048576 | tf_op jit(solution)/shard_map/pallas_call | solution.py:386
  (4 shorter events, 0.0 us)
Async XLA Ops:
  0.6 12.3 %copy-start = (bf16[2,512,512]{2,1,0:T(8,128)(2,1)S(1)}, bf16[2,512,512]{2,1,0:T(8,128)(2,1)}, u32[]{:S(2)}) copy-start(bf16[2,512,512]{2,1,0:T(8,128)(2,1)} %start_ref.5) | copy-start | bytes 3145732
  0.6 12.3 %copy-start.5 = (s32[64]{0:T(128)S(1)}, s32[64]{0:T(128)}, u32[]{:S(2)}) copy-start(s32[64]{0:T(128)} %size_ref.7) | copy-start | bytes 772
  0.7 12.3 %copy-start.7 = (f32[2,512]{1,0:T(2,128)S(1)}, f32[2,512]{1,0:T(2,128)}, u32[]{:S(2)}) copy-start(f32[2,512]{1,0:T(2,128)} %right_levels_ref.1) | copy-start | bytes 12292
  0.7 12.3 %copy-start.6 = (f32[2,512]{1,0:T(2,128)S(1)}, f32[2,512]{1,0:T(2,128)}, u32[]{:S(2)}) copy-start(f32[2,512]{1,0:T(2,128)} %left_levels_ref.1) | copy-start | bytes 12292
  3.3 11.1 %collective-permute-start = (bf16[512,512]{1,0:T(8,128)(2,1)}, bf16[512,512]{1,0:T(8,128)(2,1)S(1)}, u32[]{:S(2)}, u32[]{:S(2)}) collective-permute-start(bf16[512,512]{1,0:T(8,128)(2,1)} %get-tuple-element.27), channel_id=1, source_target_pairs={{33,32},{34,33},{35,34},{36,35},{37,36},{38,37},{39,38},{40,39},{4... | collective-permute-start | bytes 1572872 | tf_op jit(solution)/shard_map/ppermute | solution.py:343
  4.6 10.7 %collective-permute-start.1 = (bf16[2,512,512]{2,1,0:T(8,128)(2,1)}, bf16[2,512,512]{2,1,0:T(8,128)(2,1)S(1)}, u32[]{:S(2)}, u32[]{:S(2)}) collective-permute-start(bf16[2,512,512]{2,1,0:T(8,128)(2,1)} %get-tuple-element.29), channel_id=1, source_target_pairs={{0,32},{32,0},{1,33},{33,1},{2,34},{34,2},{3,35},{35,3},{4,36},{36... | collective-permute-start | bytes 3145736 | tf_op jit(solution)/shard_map/ppermute | solution.py:344
  13.7 1.7 %copy-start.1 = (bf16[1,2,512,512]{3,2,1,0:T(8,128)(2,1)S(1)}, bf16[1,2,512,512]{3,2,1,0:T(8,128)(2,1)}, u32[]{:S(2)}) copy-start(bf16[1,2,512,512]{3,2,1,0:T(8,128)(2,1)} %left_ref.5) | copy-start | bytes 3145732
  13.7 1.7 %copy-start.3 = (bf16[1,2,512,512]{3,2,1,0:T(8,128)(2,1)S(1)}, bf16[1,2,512,512]{3,2,1,0:T(8,128)(2,1)}, u32[]{:S(2)}) copy-start(bf16[1,2,512,512]{3,2,1,0:T(8,128)(2,1)} %right_ref.5) | copy-start | bytes 3145732
  13.7 1.7 %copy-start.10 = (s32[64]{0:T(128)S(1)}, s32[64]{0:T(128)}, u32[]{:S(2)}) copy-start(s32[64]{0:T(128)} %spin_ref.3) | copy-start | bytes 772
  15.3 4.1 %copy-start.8 = (bf16[2,512,512]{2,1,0:T(8,128)(2,1)}, bf16[2,512,512]{2,1,0:T(8,128)(2,1)S(1)}, u32[]{:S(2)}) copy-start(bf16[2,512,512]{2,1,0:T(8,128)(2,1)S(1)} %collective-permute-done.1.other_ref) | copy-start | bytes 3145732
  19.4 25.1 %all-to-all-start = ((bf16[16,272,128]{2,1,0:T(8,128)(2,1)}), bf16[16,272,128]{2,1,0:T(8,128)(2,1)S(1)}, u32[]{:S(2)}, u32[]{:S(2)}) async-start(bf16[16,272,128]{2,1,0:T(8,128)(2,1)} %shard_map.97), calls=%async_computation | async-start | bytes 2228224 | tf_op jit(solution)/shard_map/all_to_all | solution.py:366
  26.5 6.2 %collective-permute-start.2 = (f32[40,512]{1,0:T(8,128)S(1)}, f32[40,512]{1,0:T(8,128)S(1)}, u32[]{:S(2)}, u32[]{:S(2)}) collective-permute-start(f32[40,512]{1,0:T(8,128)S(1)} %get-tuple-element.30), channel_id=1, source_target_pairs={{1,0},{2,1},{3,2},{4,3},{5,4},{6,5},{7,6},{8,7},{9,8},{10,9},{11,1... | collective-permute-start | bytes 245768 | tf_op jit(solution)/shard_map/ppermute | solution.py:350
  45.2 27.7 %all-to-all-start.1 = ((f32[32,1,256]{2,1,0:T(1,128)}), f32[32,1,256]{2,1,0:T(1,128)S(1)}, u32[]{:S(2)}, u32[]{:S(2)}) async-start(f32[32,1,256]{2,1,0:T(1,128)} %get-tuple-element.32), calls=%async_computation.1 | async-start | bytes 65536 | tf_op jit(solution)/shard_map/all_to_all | solution.py:361
  60.4 5.3 %collective-permute-start.4 = (bf16[32,512]{1,0:T(8,128)(2,1)S(1)}, bf16[32,512]{1,0:T(8,128)(2,1)S(1)}, u32[]{:S(2)}, u32[]{:S(2)}) collective-permute-start(bf16[32,512]{1,0:T(8,128)(2,1)S(1)} %get-tuple-element.33.first_ref), channel_id=1, source_target_pairs={{1,0},{2,1},{3,2},{4,3},{5,4},{6,5},{7,6},{8,7},{9,8},{10,9},{11,1... | collective-permute-start | bytes 98312 | tf_op jit(solution)/shard_map/ppermute | solution.py:370
  61.7 5.0 %collective-permute-start.3 = (bf16[32,512]{1,0:T(8,128)(2,1)S(1)}, bf16[32,512]{1,0:T(8,128)(2,1)S(1)}, u32[]{:S(2)}, u32[]{:S(2)}) collective-permute-start(bf16[32,512]{1,0:T(8,128)(2,1)S(1)} %get-tuple-element.35.leaving_ref), channel_id=1, source_target_pairs={{0,1},{1,2},{2,3},{3,4},{4,5},{5,6},{6,7},{7,8},{8,9},{9,10},{10,1... | collective-permute-start | bytes 98312 | tf_op jit(solution)/shard_map/ppermute | solution.py:369
  73.8 22.0 %copy-start.2 = (bf16[1,2,512,512]{3,2,1,0:T(8,128)(2,1)S(1)}, bf16[1,2,512,512]{3,2,1,0:T(8,128)(2,1)}, u32[]{:S(2)}) copy-start(bf16[1,2,512,512]{3,2,1,0:T(8,128)(2,1)} %left_ref.5) | copy-start | bytes 3145732
  73.8 22.0 %copy-start.4 = (bf16[1,2,512,512]{3,2,1,0:T(8,128)(2,1)S(1)}, bf16[1,2,512,512]{3,2,1,0:T(8,128)(2,1)}, u32[]{:S(2)}) copy-start(bf16[1,2,512,512]{3,2,1,0:T(8,128)(2,1)} %right_ref.5) | copy-start | bytes 3145732
  95.8 1.2 copy-start.9
  122.7 21.0 %all-to-all-start.4 = ((f32[32,1,256]{2,1,0:T(1,128)}), f32[32,1,256]{2,1,0:T(1,128)S(1)}, u32[]{:S(2)}, u32[]{:S(2)}) async-start(f32[32,1,256]{2,1,0:T(1,128)} %get-tuple-element.41), calls=%async_computation.4 | async-start | bytes 65536 | tf_op jit(solution)/shard_map/all_to_all | solution.py:361
  131.2 4.3 %collective-permute-start.5 = (bf16[32,512]{1,0:T(8,128)(2,1)S(1)}, bf16[32,512]{1,0:T(8,128)(2,1)S(1)}, u32[]{:S(2)}, u32[]{:S(2)}) collective-permute-start(bf16[32,512]{1,0:T(8,128)(2,1)S(1)} %get-tuple-element.45), channel_id=1, source_target_pairs={{0,1},{1,2},{2,3},{3,4},{4,5},{5,6},{6,7},{7,8},{8,9},{9,10},{10,1... | collective-permute-start | bytes 98312 | tf_op jit(solution)/shard_map/ppermute | solution.py:384

commit v5 on v4

v5 whole, which is shorter than its diff:
```python
import jax
import jax.numpy as jnp
from jax import lax
from jax.experimental import pallas as pl
from jax.experimental.pallas import tpu as pltpu
from jax.sharding import Mesh, PartitionSpec as P

F32 = jnp.float32
BF16 = jnp.bfloat16
OP = ("yh", "x", "c")
SEC = ("yl", "z")
WIDTH = 512
ROWS = 32
NOP = 16
LANES = 128
TILES = WIDTH // LANES
PART = ROWS * TILES + 16
VMEM_LIMIT = 24 * 1024 * 1024
WHOLE_VMEM = 62 * 1024 * 1024

VM = pl.BlockSpec(memory_space=pltpu.VMEM)
SM = pl.BlockSpec(memory_space=pltpu.SMEM)
HBM = pl.BlockSpec(memory_space=pltpu.HBM)


def call(
    kernel, out_shape, in_specs, scratch=(), flops=0, nbytes=1 << 20, vmem=VMEM_LIMIT
):
    return pl.pallas_call(
        kernel,
        out_shape=out_shape,
        in_specs=in_specs,
        out_specs=jax.tree.map(lambda _: VM, out_shape),
        scratch_shapes=list(scratch),
        compiler_params=pltpu.CompilerParams(vmem_limit_bytes=vmem),
        cost_estimate=pl.CostEstimate(flops=flops, bytes_accessed=nbytes, transcendentals=0),
    )


def shaped(shape, dtype):
    return jax.ShapeDtypeStruct(shape, dtype)


def product(first, second, second_axis=0):
    return lax.dot_general(
        first, second, (((1,), (second_axis,)), ((), ())), preferred_element_type=F32
    )


def total(array):
    return jnp.sum(jnp.sum(array, axis=0, keepdims=True), axis=1, keepdims=True)


def lanes(values, width):
    place = lax.broadcasted_iota(jnp.int32, (1, width), 1)
    row = jnp.zeros((1, width), F32)
    for index, value in enumerate(values):
        row = jnp.where(place == index, value, row)
    return row


def three_parts(row):
    high = row.astype(BF16).astype(F32)
    middle = (row - high).astype(BF16).astype(F32)
    return high, middle, (row - high) - middle


def stacked(rows, count, width):
    place = lax.broadcasted_iota(jnp.int32, (count, width), 0)
    block = jnp.zeros((count, width), F32)
    for index, row in enumerate(rows):
        block = jnp.where(place == index, row, block)
    return block.astype(BF16)


def own_rows(place_ref):
    return pl.multiple_of(place_ref[1] * ROWS, ROWS)


def inside(size, first_row, shape):
    rows = lax.broadcasted_iota(jnp.int32, shape, 0) + first_row
    columns = lax.broadcasted_iota(jnp.int32, shape, 1)
    return (rows < size) & (columns < size)


def size_of(place_ref, size_ref, block):
    return size_ref[jnp.minimum(place_ref[2] + block, size_ref.shape[0] - 1)]


def diagonal_of(left_row, right_row, first_row):
    rows = lax.broadcasted_iota(jnp.int32, (ROWS, WIDTH), 0) + first_row
    columns = lax.broadcasted_iota(jnp.int32, (ROWS, WIDTH), 1)
    chosen = jnp.where(rows == columns, left_row, 0.0)
    return jnp.sum(chosen, axis=1, keepdims=True) + right_row


def open_kernel(start_ref, left_ref, right_ref, halo_ref, send_ref, semaphores):
    there = 1 - lax.axis_index("c")
    copies = [
        pltpu.make_async_copy(start_ref.at[0], halo_ref, semaphores.at[0]),
        pltpu.make_async_copy(left_ref.at[0, there], send_ref.at[0], semaphores.at[1]),
        pltpu.make_async_copy(right_ref.at[0, there], send_ref.at[1], semaphores.at[2]),
    ]
    for copy in copies:
        copy.start()
    for copy in copies:
        copy.wait()


def rows_kernel(
    place_ref, size_ref, start_ref, left_levels_ref, right_levels_ref,
    rows_ref, diagonal_ref, scalar_ref,
):
    first_row = own_rows(place_ref)
    norm = jnp.zeros((ROWS, WIDTH), F32)
    energy = jnp.zeros((ROWS, WIDTH), F32)
    for block in range(2):
        mask = inside(size_of(place_ref, size_ref, block), first_row, (ROWS, WIDTH))
        own = jnp.where(mask, start_ref[block, pl.ds(first_row, ROWS)].astype(F32), 0.0)
        rows_ref[block] = own
        square = own * own
        norm = norm + square
        diagonal = diagonal_of(
            left_levels_ref[block : block + 1], right_levels_ref[block : block + 1], first_row
        )
        diagonal_ref[block] = diagonal
        energy = energy + diagonal * square
    scalar_ref[...] = lanes([total(energy), total(norm)], LANES)


def masked(source, place_ref, size_ref, block):
    mask = inside(size_of(place_ref, size_ref, block), 0, (WIDTH, WIDTH))
    return jnp.where(mask, source.astype(F32), 0.0).astype(BF16)


def coupling_of(place_ref, spin_ref):
    here = place_ref[2] + place_ref[0]
    following = jnp.minimum(here + 1, spin_ref.shape[0] - 1)
    above = jnp.full((1, WIDTH), spin_ref[following], jnp.int32).astype(F32) + 1.0
    below = jnp.full((1, WIDTH), spin_ref[here], jnp.int32).astype(F32) + 1.0
    linked = jnp.full((1, WIDTH), here, jnp.int32) + 1 < spin_ref.shape[0]
    return jnp.where(linked, jnp.sqrt(above / below), 0.0)


def operator_pairs(place_ref, left_ref, right_ref, other_ref):
    core = place_ref[0]
    return (left_ref[0, core], right_ref[0, core]), (other_ref[0], other_ref[1])


def raise_into(place_ref, spin_ref, left_ref, right_ref, other_ref, field, raised_ref):
    image = jnp.zeros((WIDTH, WIDTH), F32)
    for left, right in operator_pairs(place_ref, left_ref, right_ref, other_ref):
        image = image + product(left, product(field, right, 1).astype(BF16))
    raised_ref[...] = (coupling_of(place_ref, spin_ref) * image).astype(BF16)


def lower_into(
    place_ref, spin_ref, left_ref, right_ref, other_ref, after, raised_ref, scalars,
    lowered_ref, scalar_ref,
):
    image = jnp.zeros((WIDTH, WIDTH), F32)
    for left, right in operator_pairs(place_ref, left_ref, right_ref, other_ref):
        image = image + product(product(left.T, after).astype(BF16), right)
    lowered_ref[...] = coupling_of(place_ref, spin_ref) * image
    energy = 2.0 * total(raised_ref[...].astype(F32) * after.astype(F32))
    scalar_ref[...] = lanes([energy], LANES) + scalars


def first_raise_kernel(
    place_ref, size_ref, spin_ref, start_ref, left_ref, right_ref, other_ref, raised_ref
):
    core = place_ref[0]
    field = masked(start_ref[core], place_ref, size_ref, core)
    raise_into(place_ref, spin_ref, left_ref, right_ref, other_ref, field, raised_ref)


def first_lower_kernel(
    place_ref, size_ref, spin_ref, start_ref, halo_ref, raised_ref, known_ref,
    left_ref, right_ref, other_ref, lowered_ref, scalar_ref,
):
    core = place_ref[0]
    source = jnp.where(core == 0, start_ref[1].astype(F32), halo_ref[...].astype(F32))
    after = masked(source, place_ref, size_ref, core + 1)
    lower_into(
        place_ref, spin_ref, left_ref, right_ref, other_ref, after, raised_ref, known_ref[...],
        lowered_ref, scalar_ref,
    )


def second_raise_kernel(
    place_ref, spin_ref, gathered_ref, left_ref, right_ref, other_ref, raised_ref
):
    field = gathered_ref[...].reshape(WIDTH, WIDTH)
    raise_into(place_ref, spin_ref, left_ref, right_ref, other_ref, field, raised_ref)


def second_lower_kernel(
    place_ref, spin_ref, after_ref, raised_ref, known_ref, left_ref, right_ref, other_ref,
    lowered_ref, scalar_ref,
):
    after = after_ref[...].reshape(WIDTH, WIDTH)
    lower_into(
        place_ref, spin_ref, left_ref, right_ref, other_ref, after, raised_ref, known_ref[...],
        lowered_ref, scalar_ref,
    )


def parts_kernel(lowered_ref, arrived_ref, scalar_ref, parts_ref):
    coded = stacked(three_parts(scalar_ref[...]), 16, LANES)
    for device in range(NOP):
        here = slice(device * ROWS, (device + 1) * ROWS)
        image = (lowered_ref[here] + arrived_ref[here].astype(F32)).astype(BF16)
        for tile in range(TILES):
            columns = slice(tile * LANES, (tile + 1) * LANES)
            parts_ref[device, tile * ROWS : (tile + 1) * ROWS] = image[:, columns]
        parts_ref[device, ROWS * TILES :] = coded


def sum_kernel(received_ref, sums_ref, scalar_ref):
    coded = jnp.zeros((16, LANES), F32)
    for device in range(NOP):
        coded = coded + received_ref[device, ROWS * TILES :].astype(F32)
    row = jnp.sum(coded, axis=0, keepdims=True)
    scalar_ref[...] = jnp.broadcast_to(row[None], scalar_ref.shape)
    for block in range(2):
        for tile in range(TILES):
            running = jnp.zeros((ROWS, LANES), F32)
            for device in range(block, NOP, 2):
                here = slice(tile * ROWS, (tile + 1) * ROWS)
                running = running + received_ref[device, here].astype(F32)
            sums_ref[block, :, tile * LANES : (tile + 1) * LANES] = running


def scalars_of(gathered_ref, count):
    row = jnp.sum(gathered_ref[...], axis=0)
    return [row[:, index : index + 1] for index in range(count)]


def correction_kernel(
    place_ref, size_ref, gathered_ref, sums_ref, diagonal_ref, rows_ref,
    spread_ref, image_ref, change_ref, scalar_ref, known_ref,
):
    energy, norm = scalars_of(gathered_ref, 2)
    rayleigh = energy / norm
    scale = jnp.sqrt(norm)
    first_row = own_rows(place_ref)
    amounts = [jnp.zeros((ROWS, WIDTH), F32) for _ in range(4)]
    for block in range(2):
        mask = inside(size_of(place_ref, size_ref, block), first_row, (ROWS, WIDTH))
        values = rows_ref[block]
        diagonal = diagonal_ref[block]
        unit = values / scale
        image = jnp.where(mask, sums_ref[block] + diagonal * values, 0.0) / scale
        residual = image - rayleigh * unit
        change = residual / (jnp.abs(diagonal - rayleigh) + 1.0)
        rounded = change.astype(BF16)
        for device in range(block, NOP, 2):
            spread_ref[device] = rounded
        image_ref[block] = image
        change_ref[block] = change
        again = rounded.astype(F32)
        amounts[0] = amounts[0] + diagonal * again * again
        amounts[1] = amounts[1] + unit * change
        amounts[2] = amounts[2] + change * change
        amounts[3] = amounts[3] + change * image
    scalar_ref[...] = lanes([total(amount) for amount in amounts], LANES)
    known_ref[...] = lanes([rayleigh, scale], LANES)


def ritz_kernel(
    place_ref, size_ref, gathered_ref, known_ref, sums_ref,
    diagonal_ref, rows_ref, image_ref, change_ref,
    vector_ref, residual_ref, energies_ref,
):
    change_energy, correlation, square, change_image = scalars_of(gathered_ref, 4)
    rayleigh = known_ref[:, 0:1]
    scale = known_ref[:, 1:2]
    spread = square - correlation * correlation
    deviation = jnp.sqrt(spread)
    cross_term = (change_image - correlation * rayleigh) / deviation
    second_energy = (
        change_energy - 2.0 * correlation * change_image + correlation * correlation * rayleigh
    ) / spread
    half_gap = 0.5 * (rayleigh - second_energy)
    length = jnp.sqrt(half_gap * half_gap + cross_term * cross_term)
    lowest = 0.5 * (rayleigh + second_energy) - length
    apart = length > 0.0
    divisor = jnp.where(apart, length, 1.0)
    double_cosine = jnp.where(apart, half_gap / divisor, 1.0)
    double_sine = jnp.where(apart, cross_term / divisor, 0.0)
    larger = jnp.sqrt(0.5 * (1.0 + jnp.abs(double_cosine)))
    smaller = 0.5 * double_sine / larger
    ahead = double_cosine >= 0.0
    sign = jnp.where(cross_term < 0.0, -1.0, 1.0)
    cosine_angle = jnp.where(ahead, larger, jnp.abs(smaller))
    sine_angle = jnp.where(ahead, smaller, sign * larger)
    first_row = own_rows(place_ref)
    for block in range(2):
        mask = inside(size_of(place_ref, size_ref, block), first_row, (ROWS, WIDTH))
        unit = rows_ref[block] / scale
        image = image_ref[block]
        change = change_ref[block]
        rounded = change.astype(BF16).astype(F32)
        change_picture = jnp.where(mask, sums_ref[block] + diagonal_ref[block] * rounded, 0.0)
        unit_second = (change - correlation * unit) / deviation
        second_image = (change_picture - correlation * image) / deviation
        ritz_unit = sine_angle * unit - cosine_angle * unit_second
        vector_ref[block] = (scale * ritz_unit).astype(BF16)
        residual_ref[block] = (
            scale * (sine_angle * image - cosine_angle * second_image - lowest * ritz_unit)
        ).astype(BF16)
    energies_ref[...] = lanes([rayleigh, lowest], 2)


def body(start, left, right, left_energy, right_energy, sector_size, sector_spin):
    core = lax.axis_index("c")
    position = lax.axis_index(OP)
    sectors = lax.axis_size(SEC)
    place = jnp.stack([core, position, 2 * lax.axis_index(SEC)]).astype(jnp.int32)
    block_shape = shaped((WIDTH, WIDTH), BF16)
    two_shape = shaped((2, WIDTH, WIDTH), BF16)
    own_shape = shaped((2, ROWS, WIDTH), F32)
    lane_shape = shaped((1, LANES), F32)
    work = 8 * WIDTH * WIDTH * WIDTH
    owners = ("c",) + SEC
    within = [(i, sectors + i) for i in range(sectors)]
    across = [(sectors + i, i + 1) for i in range(sectors - 1)]
    to_next = within + across
    to_previous = [(there, here) for here, there in to_next]

    halo_source, send = call(
        open_kernel, (block_shape, two_shape), [HBM] * 3, [pltpu.SemaphoreType.DMA((3,))],
        vmem=WHOLE_VMEM,
    )(start, left, right)
    other = lax.ppermute(send, "c", [(0, 1), (1, 0)])
    halo = lax.ppermute(halo_source, owners, [(there, here) for here, there in across])
    operators = (left, right, other)
    rows, diagonal, amounts = call(
        rows_kernel, (own_shape, own_shape, lane_shape), [SM] * 2 + [VM] * 3
    )(place, sector_size, start, left_energy, right_energy)

    def summed(lowered, raised, amounts):
        arrived = lax.ppermute(raised, owners, to_next)
        parts = call(parts_kernel, shaped((NOP, PART, LANES), BF16), [VM] * 3)(
            lowered, arrived, amounts
        )
        sums, scalars = call(sum_kernel, (own_shape, shaped((sectors, 1, LANES), F32)), [VM])(
            lax.all_to_all(parts, OP, 0, 0)
        )
        return sums, lax.all_to_all(scalars, SEC, 0, 0)

    lowered_shapes = (shaped((WIDTH, WIDTH), F32), lane_shape)
    raised = call(
        first_raise_kernel, block_shape, [SM] * 3 + [VM] * 4, flops=work, nbytes=4 << 20
    )(place, sector_size, sector_spin, start, *operators)
    lowered, amounts = call(
        first_lower_kernel, lowered_shapes, [SM] * 3 + [VM] * 7, flops=work, nbytes=4 << 20
    )(place, sector_size, sector_spin, start, halo, raised, amounts, *operators)
    sums, gathered = summed(lowered, raised, amounts)
    spread, image, change, amounts, known = call(
        correction_kernel,
        (shaped((NOP, ROWS, WIDTH), BF16), own_shape, own_shape, lane_shape, lane_shape),
        [SM] * 2 + [VM] * 4,
    )(place, sector_size, gathered, sums, diagonal, rows)
    field = lax.all_to_all(spread, OP, 0, 0)
    after = lax.ppermute(field, owners, to_previous)
    raised = call(
        second_raise_kernel, block_shape, [SM] * 2 + [VM] * 4, flops=work, nbytes=4 << 20
    )(place, sector_spin, field, *operators)
    lowered, amounts = call(
        second_lower_kernel, lowered_shapes, [SM] * 2 + [VM] * 6, flops=work, nbytes=4 << 20
    )(place, sector_spin, after, raised, amounts, *operators)
    sums, gathered = summed(lowered, raised, amounts)
    result = shaped((2, ROWS, WIDTH), BF16)
    vector, residual, energies = call(
        ritz_kernel, (result, result, shaped((1, 2), F32)), [SM] * 2 + [VM] * 7
    )(place, sector_size, gathered, known, sums, diagonal, rows, image, change)
    return vector, residual, energies.reshape(2)


def solution(mesh):
    fine = Mesh(mesh.devices.reshape(2, 4, 2, 2, 16), ("yh", "x", "c", "yl", "z"))
    return jax.shard_map(
        body,
        mesh=fine,
        in_specs=(
            P(SEC, None, None),
            P(OP, SEC, None, None),
            P(OP, SEC, None, None),
            P(SEC, None),
            P(SEC, None),
            P(),
            P(),
        ),
        out_specs=(P(SEC, OP, None), P(SEC, OP, None), P()),
        check_vma=False,
    )
```

time: 146 us -> 140 us (0.959)
  blocking collectives: 43.9 us -> 94.3 us
  starting transfers between devices: 49.8 us -> 19.6 us
  waiting for transfers between devices: 34.3 us -> 8.68 us
    all_to_all x2 -> x5, blocking collectives: 43.9 us -> 94.3 us  [the longest x2 46.8 us: summed(): return (sums, lax.all_to_all(scalars, SEC, 0, 0))]
    all_to_all x3 -> x0, starting transfers between devices: 30.6 us -> none  [the longest x2 23.6 us: summed(): return (*sums, lax.all_to_all(scalars, SEC, 0, 0))]
    all_to_all x3 -> x0, waiting for transfers between devices: 26.4 us -> none  [the longest x2 14.5 us: summed(): return (*sums, lax.all_to_all(scalars, SEC, 0, 0))]
    pallas_call x7 -> x10, Pallas kernels: 10.9 us -> 9.59 us  [the longest x1 2.01 us: body(): call(first_lower_kernel, lowered_shapes, [SM] * 3 + [VM] * 7, flops=work,...]
    ppermute x5 -> x4, waiting for transfers between devices: 7.87 us -> 7.62 us  [the longest x2 4.6 us: summed(): arrived = lax.ppermute(raised, owners, to_next)]
    ppermute x5 -> x4, starting transfers between devices: 11 us -> 10.8 us  [the longest x2 6.52 us: summed(): arrived = lax.ppermute(raised, owners, to_next)]
  transfers between devices with their start and end apart: 9 -> 5, of which waited for: 7 -> 4; matrix products, arithmetic and copies ran while one was open for 0% -> 0% of each run, Pallas kernels for 1% -> 6%
where the time goes in v5:
time: 140 us
  blocking collectives  94.3 us (67%)
  starting transfers between devices  19.6 us (14%)
  Pallas kernels  14 us (10%)
  waiting for transfers between devices  8.68 us (6%)
  local copies, waits for them, and re-layouts  2.48 us (2%)
    all_to_all x2, blocking collectives, summed(): return (sums, lax.all_to_all(scalars, SEC, 0, 0))  46.8 us
    all_to_all x2, blocking collectives, summed(): lax.all_to_all(parts, OP, 0, 0)  31.3 us
    all_to_all x1, blocking collectives, body(): field = lax.all_to_all(spread, OP, 0, 0)  16.2 us
    ppermute x1, starting transfers between devices, body(): other = lax.ppermute(send, 'c', [(0, 1), (1, 0)])  8.79 us
    ppermute x2, starting transfers between devices, summed(): arrived = lax.ppermute(raised, owners, to_next)  6.52 us
    ppermute x2, waiting for transfers between devices, summed(): arrived = lax.ppermute(raised, owners, to_next)  4.6 us
    ppermute x1, waiting for transfers between devices, body(): after = lax.ppermute(field, owners, to_previous)  3.01 us
    ppermute x1, starting transfers between devices, body(): after = lax.ppermute(field, owners, to_previous)  2.97 us
  transfers between devices with their start and end apart: 5, of which 4 were waited for; matrix products, arithmetic and copies ran while one was open for 0% of the time, Pallas kernels for 6%

profile of v5, /device:TPU:1, one launch (start us, length us, event | category | flops | bytes accessed | tf_op | source)
XLA Modules:
  0.0 139.9 jit_solution(3769553540097578962)
XLA Ops:
  0.6 0.0 copy-start
  0.6 2.6 %shard_map.94 = (bf16[512,512]{1,0:T(8,128)(2,1)}, bf16[2,512,512]{2,1,0:T(8,128)(2,1)}) custom-call(bf16[2,512,512]{2,1,0:T(8,128)(2,1)} %start_ref.7, bf16[1,2,512,512]{3,2,1,0:T(8,128)(2,1)} %left_ref.9, bf16[1,2,512,512]{3,2,1,0:T(8,128)(2,1)} %right_ref.9), custom_call_target="tpu_custom_call" | custom-call | bytes 1048576 | tf_op jit(solution)/shard_map/pallas_call | solution.py:331
  3.3 8.8 %collective-permute-start.1 = (bf16[2,512,512]{2,1,0:T(8,128)(2,1)}, bf16[2,512,512]{2,1,0:T(8,128)(2,1)S(1)}, u32[]{:S(2)}, u32[]{:S(2)}) collective-permute-start(bf16[2,512,512]{2,1,0:T(8,128)(2,1)} %get-tuple-element.25), channel_id=1, source_target_pairs={{0,32},{32,0},{1,33},{33,1},{2,34},{34,2},{3,35},{35,3},{4,36},{36... | collective-permute-start | bytes 3145736 | tf_op jit(solution)/shard_map/ppermute | solution.py:335
  12.1 1.3 collective-permute-start
  13.4 0.0 copy-start.4
  13.4 0.0 copy-start.5
  13.4 0.1 pad_add_fusion.place_ref
  13.5 1.1 collective-permute-done.1.other_ref
  14.6 0.0 copy-done
  14.6 0.0 copy-done.4
  14.6 0.0 copy-done.5
  14.6 0.0 copy-start.1
  14.6 1.2 copy-done.1
  15.8 0.0 copy-start.3
  15.8 1.2 copy-done.3
  17.0 0.0 copy-start.6
  17.0 0.0 copy-start.7
  17.0 1.9 %shard_map.95.raised_ref = bf16[512,512]{1,0:T(8,128)(2,1)S(1)} custom-call(s32[3]{0:T(128)S(1)} %pad_add_fusion.place_ref, s32[64]{0:T(128)S(1)} %copy-done.4, s32[64]{0:T(128)S(1)} %copy-done.5, bf16[2,512,512]{2,1,0:T(8,128)(2,1)S(1)} %copy-done.3, bf16[1,2,512,512]{3,2,1,0:T(8,128)(2,1)S(1)} %copy-done, bf16[1,2,512,512]{3,2,1,0:T(8,128)(2,1)S(1)} %copy-done.1, ...), custom_call_target="tpu_custom_call" | custom-call | flops 1073741824 | bytes 4194304 | tf_op jit(solution)/shard_map/pallas_call | solution.py:353
  19.0 0.0 copy-start.2
  19.0 3.9 %collective-permute-start.2 = (bf16[512,512]{1,0:T(8,128)(2,1)S(1)}, bf16[512,512]{1,0:T(8,128)(2,1)S(1)}, u32[]{:S(2)}, u32[]{:S(2)}) collective-permute-start(bf16[512,512]{1,0:T(8,128)(2,1)S(1)} %shard_map.95.raised_ref), channel_id=1, source_target_pairs={{0,32},{1,33},{2,34},{3,35},{4,36},{5,37},{6,38},{7,39},{8,40},{9,... | collective-permute-start | bytes 1572872 | tf_op jit(solution)/shard_map/ppermute | solution.py:343
  22.9 0.0 copy-done.6
  22.9 0.0 copy-done.7
  22.9 0.7 shard_map.96
  23.6 0.0 collective-permute-done.halo_ref
  23.7 0.0 copy-done.2
  23.7 2.0 %shard_map.97 = (f32[512,512]{1,0:T(8,128)S(1)}, f32[1,128]{1,0:T(1,128)S(1)}) custom-call(s32[3]{0:T(128)S(1)} %pad_add_fusion.place_ref, s32[64]{0:T(128)S(1)} %copy-done.4, s32[64]{0:T(128)S(1)} %copy-done.5, bf16[2,512,512]{2,1,0:T(8,128)(2,1)S(1)} %copy-done.3, bf16[512,512]{1,0:T(8,128)(2,1)S(1)} %collective-permute-done.halo_ref, ...), custom_call_target="tpu_custom_call" | custom-call | flops 1073741824 | bytes 4194304 | tf_op jit(solution)/shard_map/pallas_call | solution.py:356
  25.7 3.3 %collective-permute-done.2.arrived_ref = bf16[512,512]{1,0:T(8,128)(2,1)S(1)} collective-permute-done((bf16[512,512]{1,0:T(8,128)(2,1)S(1)}, bf16[512,512]{1,0:T(8,128)(2,1)S(1)}, u32[]{:S(2)}, u32[]{:S(2)}) %collective-permute-start.2) | collective-permute-done | bytes 524320 | tf_op jit(solution)/shard_map/ppermute | solution.py:343
  29.0 0.1 shard_map.98
  29.1 15.5 %all_to_all.25.received_ref = bf16[16,144,128]{2,1,0:T(8,128)(2,1)S(1)} all-to-all(bf16[16,144,128]{2,1,0:T(8,128)(2,1)S(1)} %shard_map.98), channel_id=1, replica_groups=mesh['yh'=2,'x'=4,'c'=2,'yl'=2,'z'=16] {'yh','x','c'}, dimensions={0} | all-to-all | bytes 1179648 | tf_op jit(solution)/shard_map/all_to_all | solution.py:348
  44.6 0.1 shard_map.99
  44.7 28.2 %all_to_all.26.gathered_ref = f32[32,1,128]{2,1,0:T(1,128)S(1)} all-to-all(f32[32,1,128]{2,1,0:T(1,128)S(1)} %get-tuple-element.29), channel_id=1, replica_groups=mesh['yh'=2,'x'=4,'c'=2,'yl'=2,'z'=16] {'yl','z'}, dimensions={0} | all-to-all | bytes 32768 | tf_op jit(solution)/shard_map/all_to_all | solution.py:350
  72.9 0.9 shard_map.100
  73.8 16.2 %all_to_all.27.gathered_ref = bf16[16,32,512]{2,1,0:T(8,128)(2,1)S(1)} all-to-all(bf16[16,32,512]{2,1,0:T(8,128)(2,1)S(1)} %get-tuple-element.33), channel_id=1, replica_groups=mesh['yh'=2,'x'=4,'c'=2,'yl'=2,'z'=16] {'yh','x','c'}, dimensions={0} | all-to-all | bytes 1048576 | tf_op jit(solution)/shard_map/all_to_all | solution.py:365
  90.0 3.0 %collective-permute-start.3 = (bf16[16,32,512]{2,1,0:T(8,128)(2,1)S(1)}, bf16[16,32,512]{2,1,0:T(8,128)(2,1)S(1)}, u32[]{:S(2)}, u32[]{:S(2)}) collective-permute-start(bf16[16,32,512]{2,1,0:T(8,128)(2,1)S(1)} %all_to_all.27.gathered_ref), channel_id=1, source_target_pairs={{32,0},{33,1},{34,2},{35,3},{36,4},{37,5},{38,6},{39,7},{40,8},{41... | collective-permute-start | bytes 1572872 | tf_op jit(solution)/shard_map/ppermute | solution.py:366
  93.0 1.9 %shard_map.101.raised_ref = bf16[512,512]{1,0:T(8,128)(2,1)S(1)} custom-call(s32[3]{0:T(128)S(1)} %pad_add_fusion.place_ref, s32[64]{0:T(128)S(1)} %copy-done.5, bf16[16,32,512]{2,1,0:T(8,128)(2,1)S(1)} %all_to_all.27.gathered_ref, bf16[1,2,512,512]{3,2,1,0:T(8,128)(2,1)S(1)} %copy-done, bf16[1,2,512,512]{3,2,1,0:T(8,128)(2,1)S(1)} %copy-done.2, ...), custom_call_target="tpu_custom_call" | custom-call | flops 1073741824 | bytes 4194304 | tf_op jit(solution)/shard_map/pallas_call | solution.py:367
  94.9 2.6 %collective-permute-start.4 = (bf16[512,512]{1,0:T(8,128)(2,1)S(1)}, bf16[512,512]{1,0:T(8,128)(2,1)S(1)}, u32[]{:S(2)}, u32[]{:S(2)}) collective-permute-start(bf16[512,512]{1,0:T(8,128)(2,1)S(1)} %shard_map.101.raised_ref), channel_id=1, source_target_pairs={{0,32},{1,33},{2,34},{3,35},{4,36},{5,37},{6,38},{7,39},{8,40},{9,... | collective-permute-start | bytes 1572872 | tf_op jit(solution)/shard_map/ppermute | solution.py:343
  97.5 3.0 %collective-permute-done.3.after_ref = bf16[16,32,512]{2,1,0:T(8,128)(2,1)S(1)} collective-permute-done((bf16[16,32,512]{2,1,0:T(8,128)(2,1)S(1)}, bf16[16,32,512]{2,1,0:T(8,128)(2,1)S(1)}, u32[]{:S(2)}, u32[]{:S(2)}) %collective-permute-start.3) | collective-permute-done | bytes 524320 | tf_op jit(solution)/shard_map/ppermute | solution.py:366
  100.5 1.8 %shard_map.102 = (f32[512,512]{1,0:T(8,128)S(1)}, f32[1,128]{1,0:T(1,128)S(1)}) custom-call(s32[3]{0:T(128)S(1)} %pad_add_fusion.place_ref, s32[64]{0:T(128)S(1)} %copy-done.5, bf16[16,32,512]{2,1,0:T(8,128)(2,1)S(1)} %collective-permute-done.3.after_ref, bf16[512,512]{1,0:T(8,128)(2,1)S(1)} %shard_map.101.raised_ref, ...), custom_call_target="tpu_custom_call" | custom-call | flops 1073741824 | bytes 4194304 | tf_op jit(solution)/shard_map/pallas_call | solution.py:370
  102.3 1.3 collective-permute-done.4.arrived_ref
  103.6 0.1 shard_map.103
  103.7 15.8 %all_to_all.28.received_ref = bf16[16,144,128]{2,1,0:T(8,128)(2,1)S(1)} all-to-all(bf16[16,144,128]{2,1,0:T(8,128)(2,1)S(1)} %shard_map.103), channel_id=1, replica_groups=mesh['yh'=2,'x'=4,'c'=2,'yl'=2,'z'=16] {'yh','x','c'}, dimensions={0} | all-to-all | bytes 1179648 | tf_op jit(solution)/shard_map/all_to_all | solution.py:348
  119.5 0.1 shard_map.104
  119.6 18.6 %all_to_all.29.gathered_ref = f32[32,1,128]{2,1,0:T(1,128)S(1)} all-to-all(f32[32,1,128]{2,1,0:T(1,128)S(1)} %get-tuple-element.37), channel_id=1, replica_groups=mesh['yh'=2,'x'=4,'c'=2,'yl'=2,'z'=16] {'yl','z'}, dimensions={0} | all-to-all | bytes 32768 | tf_op jit(solution)/shard_map/all_to_all | solution.py:350
  138.2 1.8 %shard_map.105 = (bf16[2,32,512]{2,1,0:T(8,128)(2,1)}, bf16[2,32,512]{2,1,0:T(8,128)(2,1)}, f32[1,2]{1,0:T(1,128)}) custom-call(s32[3]{0:T(128)S(1)} %pad_add_fusion.place_ref, s32[64]{0:T(128)S(1)} %copy-done.4, f32[32,1,128]{2,1,0:T(1,128)S(1)} %all_to_all.29.gathered_ref, f32[1,128]{1,0:T(1,128)S(1)} %get-tuple-element.38.known_ref, ...), custom_call_target="tpu_custom_call" | custom-call | bytes 1048576 | tf_op jit(solution)/shard_map/pallas_call | solution.py:375
Async XLA Ops:
  0.6 13.9 %copy-start = (bf16[1,2,512,512]{3,2,1,0:T(8,128)(2,1)S(1)}, bf16[1,2,512,512]{3,2,1,0:T(8,128)(2,1)}, u32[]{:S(2)}) copy-start(bf16[1,2,512,512]{3,2,1,0:T(8,128)(2,1)} %left_ref.9) | copy-start | bytes 3145732
  3.3 11.3 %collective-permute-start.1 = (bf16[2,512,512]{2,1,0:T(8,128)(2,1)}, bf16[2,512,512]{2,1,0:T(8,128)(2,1)S(1)}, u32[]{:S(2)}, u32[]{:S(2)}) collective-permute-start(bf16[2,512,512]{2,1,0:T(8,128)(2,1)} %get-tuple-element.25), channel_id=1, source_target_pairs={{0,32},{32,0},{1,33},{33,1},{2,34},{34,2},{3,35},{35,3},{4,36},{36... | collective-permute-start | bytes 3145736 | tf_op jit(solution)/shard_map/ppermute | solution.py:335
  12.1 11.6 %collective-permute-start = (bf16[512,512]{1,0:T(8,128)(2,1)}, bf16[512,512]{1,0:T(8,128)(2,1)S(1)}, u32[]{:S(2)}, u32[]{:S(2)}) collective-permute-start(bf16[512,512]{1,0:T(8,128)(2,1)} %get-tuple-element.24), channel_id=1, source_target_pairs={{1,32},{2,33},{3,34},{4,35},{5,36},{6,37},{7,38},{8,39},{9,40},{10... | collective-permute-start | bytes 1572872 | tf_op jit(solution)/shard_map/ppermute | solution.py:336
  13.4 1.2 copy-start.4
  13.4 1.2 copy-start.5
  14.6 1.2 copy-start.1
  15.8 1.2 copy-start.3
  17.0 5.9 %copy-start.6 = (f32[2,512]{1,0:T(2,128)S(1)}, f32[2,512]{1,0:T(2,128)}, u32[]{:S(2)}) copy-start(f32[2,512]{1,0:T(2,128)} %left_levels_ref.1) | copy-start | bytes 12292
  17.0 5.9 %copy-start.7 = (f32[2,512]{1,0:T(2,128)S(1)}, f32[2,512]{1,0:T(2,128)}, u32[]{:S(2)}) copy-start(f32[2,512]{1,0:T(2,128)} %right_levels_ref.1) | copy-start | bytes 12292
  19.0 4.7 %copy-start.2 = (bf16[1,2,512,512]{3,2,1,0:T(8,128)(2,1)S(1)}, bf16[1,2,512,512]{3,2,1,0:T(8,128)(2,1)}, u32[]{:S(2)}) copy-start(bf16[1,2,512,512]{3,2,1,0:T(8,128)(2,1)} %right_ref.9) | copy-start | bytes 3145732
  19.0 10.1 %collective-permute-start.2 = (bf16[512,512]{1,0:T(8,128)(2,1)S(1)}, bf16[512,512]{1,0:T(8,128)(2,1)S(1)}, u32[]{:S(2)}, u32[]{:S(2)}) collective-permute-start(bf16[512,512]{1,0:T(8,128)(2,1)S(1)} %shard_map.95.raised_ref), channel_id=1, source_target_pairs={{0,32},{1,33},{2,34},{3,35},{4,36},{5,37},{6,38},{7,39},{8,40},{9,... | collective-permute-start | bytes 1572872 | tf_op jit(solution)/shard_map/ppermute | solution.py:343
  90.0 10.5 %collective-permute-start.3 = (bf16[16,32,512]{2,1,0:T(8,128)(2,1)S(1)}, bf16[16,32,512]{2,1,0:T(8,128)(2,1)S(1)}, u32[]{:S(2)}, u32[]{:S(2)}) collective-permute-start(bf16[16,32,512]{2,1,0:T(8,128)(2,1)S(1)} %all_to_all.27.gathered_ref), channel_id=1, source_target_pairs={{32,0},{33,1},{34,2},{35,3},{36,4},{37,5},{38,6},{39,7},{40,8},{41... | collective-permute-start | bytes 1572872 | tf_op jit(solution)/shard_map/ppermute | solution.py:366
  94.9 8.7 %collective-permute-start.4 = (bf16[512,512]{1,0:T(8,128)(2,1)S(1)}, bf16[512,512]{1,0:T(8,128)(2,1)S(1)}, u32[]{:S(2)}, u32[]{:S(2)}) collective-permute-start(bf16[512,512]{1,0:T(8,128)(2,1)S(1)} %shard_map.101.raised_ref), channel_id=1, source_target_pairs={{0,32},{1,33},{2,34},{3,35},{4,36},{5,37},{6,38},{7,39},{8,40},{9,... | collective-permute-start | bytes 1572872 | tf_op jit(solution)/shard_map/ppermute | solution.py:343

commit v6 on v5

--- a/solution.py
+++ b/solution.py
@@ -55,7 +55,7 @@
     place = lax.broadcasted_iota(jnp.int32, (1, width), 1)
     row = jnp.zeros((1, width), F32)
     for index, value in enumerate(values):
-        row = jnp.where(place == index, value, row)
+        row = jnp.where(place == index, value if value.shape[1] == 1 else value[:, :width], row)
     return row
 
 
@@ -94,12 +94,20 @@
     return jnp.sum(chosen, axis=1, keepdims=True) + right_row
 
 
-def open_kernel(start_ref, left_ref, right_ref, halo_ref, send_ref, semaphores):
-    there = 1 - lax.axis_index("c")
+def open_kernel(start_ref, left_ref, right_ref, halo_ref, send_ref, own_ref, semaphores):
+    core = lax.axis_index("c")
     copies = [
-        pltpu.make_async_copy(start_ref.at[0], halo_ref, semaphores.at[0]),
-        pltpu.make_async_copy(left_ref.at[0, there], send_ref.at[0], semaphores.at[1]),
-        pltpu.make_async_copy(right_ref.at[0, there], send_ref.at[1], semaphores.at[2]),
+        pltpu.make_async_copy(source, target, semaphores.at[index])
+        for index, (source, target) in enumerate(
+            (
+                (left_ref.at[0, 1 - core], send_ref.at[0]),
+                (right_ref.at[0, 1 - core], send_ref.at[1]),
+                (start_ref.at[0], halo_ref),
+                (left_ref.at[0, core], own_ref.at[0]),
+                (right_ref.at[0, core], own_ref.at[1]),
+                (start_ref.at[core], own_ref.at[2]),
+            )
+        )
     ]
     for copy in copies:
         copy.start()
@@ -142,24 +150,23 @@
     return jnp.where(linked, jnp.sqrt(above / below), 0.0)
 
 
-def operator_pairs(place_ref, left_ref, right_ref, other_ref):
-    core = place_ref[0]
-    return (left_ref[0, core], right_ref[0, core]), (other_ref[0], other_ref[1])
-
-
-def raise_into(place_ref, spin_ref, left_ref, right_ref, other_ref, field, raised_ref):
+def operator_pairs(own_ref, other_ref):
+    return (own_ref[0], own_ref[1]), (other_ref[0], other_ref[1])
+
+
+def raise_into(place_ref, spin_ref, own_ref, other_ref, field, raised_ref):
     image = jnp.zeros((WIDTH, WIDTH), F32)
-    for left, right in operator_pairs(place_ref, left_ref, right_ref, other_ref):
+    for left, right in operator_pairs(own_ref, other_ref):
         image = image + product(left, product(field, right, 1).astype(BF16))
     raised_ref[...] = (coupling_of(place_ref, spin_ref) * image).astype(BF16)
 
 
 def lower_into(
-    place_ref, spin_ref, left_ref, right_ref, other_ref, after, raised_ref, scalars,
+    place_ref, spin_ref, own_ref, other_ref, after, raised_ref, scalars,
     lowered_ref, scalar_ref,
 ):
     image = jnp.zeros((WIDTH, WIDTH), F32)
-    for left, right in operator_pairs(place_ref, left_ref, right_ref, other_ref):
+    for left, right in operator_pairs(own_ref, other_ref):
         image = image + product(product(left.T, after).astype(BF16), right)
     lowered_ref[...] = coupling_of(place_ref, spin_ref) * image
     energy = 2.0 * total(raised_ref[...].astype(F32) * after.astype(F32))
@@ -167,40 +174,40 @@
 
 
 def first_raise_kernel(
-    place_ref, size_ref, spin_ref, start_ref, left_ref, right_ref, other_ref, raised_ref
+    place_ref, size_ref, spin_ref, own_ref, other_ref, raised_ref
 ):
     core = place_ref[0]
-    field = masked(start_ref[core], place_ref, size_ref, core)
-    raise_into(place_ref, spin_ref, left_ref, right_ref, other_ref, field, raised_ref)
+    field = masked(own_ref[2], place_ref, size_ref, core)
+    raise_into(place_ref, spin_ref, own_ref, other_ref, field, raised_ref)
 
 
 def first_lower_kernel(
     place_ref, size_ref, spin_ref, start_ref, halo_ref, raised_ref, known_ref,
-    left_ref, right_ref, other_ref, lowered_ref, scalar_ref,
+    own_ref, other_ref, lowered_ref, scalar_ref,
 ):
     core = place_ref[0]
     source = jnp.where(core == 0, start_ref[1].astype(F32), halo_ref[...].astype(F32))
     after = masked(source, place_ref, size_ref, core + 1)
     lower_into(
-        place_ref, spin_ref, left_ref, right_ref, other_ref, after, raised_ref, known_ref[...],
+        place_ref, spin_ref, own_ref, other_ref, after, raised_ref, known_ref[...],
         lowered_ref, scalar_ref,
     )
 
 
 def second_raise_kernel(
-    place_ref, spin_ref, gathered_ref, left_ref, right_ref, other_ref, raised_ref
+    place_ref, spin_ref, gathered_ref, own_ref, other_ref, raised_ref
 ):
     field = gathered_ref[...].reshape(WIDTH, WIDTH)
-    raise_into(place_ref, spin_ref, left_ref, right_ref, other_ref, field, raised_ref)
+    raise_into(place_ref, spin_ref, own_ref, other_ref, field, raised_ref)
 
 
 def second_lower_kernel(
-    place_ref, spin_ref, after_ref, raised_ref, known_ref, left_ref, right_ref, other_ref,
+    place_ref, spin_ref, after_ref, raised_ref, known_ref, own_ref, other_ref,
     lowered_ref, scalar_ref,
 ):
     after = after_ref[...].reshape(WIDTH, WIDTH)
     lower_into(
-        place_ref, spin_ref, left_ref, right_ref, other_ref, after, raised_ref, known_ref[...],
+        place_ref, spin_ref, own_ref, other_ref, after, raised_ref, known_ref[...],
         lowered_ref, scalar_ref,
     )
 
@@ -231,9 +238,13 @@
             sums_ref[block, :, tile * LANES : (tile + 1) * LANES] = running
 
 
+def widened(row, index):
+    return jnp.broadcast_to(row[:, index : index + 1], (1, WIDTH))
+
+
 def scalars_of(gathered_ref, count):
     row = jnp.sum(gathered_ref[...], axis=0)
-    return [row[:, index : index + 1] for index in range(count)]
+    return [widened(row, index) for index in range(count)]
 
 
 def correction_kernel(
@@ -243,14 +254,15 @@
     energy, norm = scalars_of(gathered_ref, 2)
     rayleigh = energy / norm
     scale = jnp.sqrt(norm)
+    shrink = 1.0 / scale
     first_row = own_rows(place_ref)
     amounts = [jnp.zeros((ROWS, WIDTH), F32) for _ in range(4)]
     for block in range(2):
         mask = inside(size_of(place_ref, size_ref, block), first_row, (ROWS, WIDTH))
         values = rows_ref[block]
         diagonal = diagonal_ref[block]
-        unit = values / scale
-        image = jnp.where(mask, sums_ref[block] + diagonal * values, 0.0) / scale
+        unit = values * shrink
+        image = jnp.where(mask, sums_ref[block] + diagonal * values, 0.0) * shrink
         residual = image - rayleigh * unit
         change = residual / (jnp.abs(diagonal - rayleigh) + 1.0)
         rounded = change.astype(BF16)
@@ -273,11 +285,14 @@
     vector_ref, residual_ref, energies_ref,
 ):
     change_energy, correlation, square, change_image = scalars_of(gathered_ref, 4)
-    rayleigh = known_ref[:, 0:1]
-    scale = known_ref[:, 1:2]
+    known = known_ref[...]
+    rayleigh = widened(known, 0)
+    scale = widened(known, 1)
     spread = square - correlation * correlation
     deviation = jnp.sqrt(spread)
-    cross_term = (change_image - correlation * rayleigh) / deviation
+    inverse = 1.0 / deviation
+    shrink = 1.0 / scale
+    cross_term = (change_image - correlation * rayleigh) * inverse
     second_energy = (
         change_energy - 2.0 * correlation * change_image + correlation * correlation * rayleigh
     ) / spread
@@ -297,13 +312,13 @@
     first_row = own_rows(place_ref)
     for block in range(2):
         mask = inside(size_of(place_ref, size_ref, block), first_row, (ROWS, WIDTH))
-        unit = rows_ref[block] / scale
+        unit = rows_ref[block] * shrink
         image = image_ref[block]
         change = change_ref[block]
         rounded = change.astype(BF16).astype(F32)
         change_picture = jnp.where(mask, sums_ref[block] + diagonal_ref[block] * rounded, 0.0)
-        unit_second = (change - correlation * unit) / deviation
-        second_image = (change_picture - correlation * image) / deviation
+        unit_second = (change - correlation * unit) * inverse
+        second_image = (change_picture - correlation * image) * inverse
         ritz_unit = sine_angle * unit - cosine_angle * unit_second
         vector_ref[block] = (scale * ritz_unit).astype(BF16)
         residual_ref[block] = (
@@ -328,13 +343,16 @@
     to_next = within + across
     to_previous = [(there, here) for here, there in to_next]
 
-    halo_source, send = call(
-        open_kernel, (block_shape, two_shape), [HBM] * 3, [pltpu.SemaphoreType.DMA((3,))],
+    halo_source, send, own = call(
+        open_kernel,
+        (block_shape, two_shape, shaped((3, WIDTH, WIDTH), BF16)),
+        [HBM] * 3,
+        [pltpu.SemaphoreType.DMA((6,))],
         vmem=WHOLE_VMEM,
     )(start, left, right)
     other = lax.ppermute(send, "c", [(0, 1), (1, 0)])
     halo = lax.ppermute(halo_source, owners, [(there, here) for here, there in across])
-    operators = (left, right, other)
+    operators = (own, other)
     rows, diagonal, amounts = call(
         rows_kernel, (own_shape, own_shape, lane_shape), [SM] * 2 + [VM] * 3
     )(place, sector_size, start, left_energy, right_energy)
@@ -351,10 +369,10 @@
 
     lowered_shapes = (shaped((WIDTH, WIDTH), F32), lane_shape)
     raised = call(
-        first_raise_kernel, block_shape, [SM] * 3 + [VM] * 4, flops=work, nbytes=4 << 20
-    )(place, sector_size, sector_spin, start, *operators)
+        first_raise_kernel, block_shape, [SM] * 3 + [VM] * 2, flops=work, nbytes=4 << 20
+    )(place, sector_size, sector_spin, *operators)
     lowered, amounts = call(
-        first_lower_kernel, lowered_shapes, [SM] * 3 + [VM] * 7, flops=work, nbytes=4 << 20
+        first_lower_kernel, lowered_shapes, [SM] * 3 + [VM] * 6, flops=work, nbytes=4 << 20
     )(place, sector_size, sector_spin, start, halo, raised, amounts, *operators)
     sums, gathered = summed(lowered, raised, amounts)
     spread, image, change, amounts, known = call(
@@ -365,10 +383,10 @@
     field = lax.all_to_all(spread, OP, 0, 0)
     after = lax.ppermute(field, owners, to_previous)
     raised = call(
-        second_raise_kernel, block_shape, [SM] * 2 + [VM] * 4, flops=work, nbytes=4 << 20
+        second_raise_kernel, block_shape, [SM] * 2 + [VM] * 3, flops=work, nbytes=4 << 20
     )(place, sector_spin, field, *operators)
     lowered, amounts = call(
-        second_lower_kernel, lowered_shapes, [SM] * 2 + [VM] * 6, flops=work, nbytes=4 << 20
+        second_lower_kernel, lowered_shapes, [SM] * 2 + [VM] * 5, flops=work, nbytes=4 << 20
     )(place, sector_spin, after, raised, amounts, *operators)
     sums, gathered = summed(lowered, raised, amounts)
     result = shaped((2, ROWS, WIDTH), BF16)

time: 140 us -> 140 us (level)
  transfers between devices with their start and end apart: 5 -> 5, of which waited for: 4 -> 5; matrix products, arithmetic and copies ran while one was open for 0% -> 0% of each run, Pallas kernels for 6% -> 6%
where the time goes in v6:
time: 140 us; the launch traced here: 139 us
  blocking collectives  94.8 us (68%)
  starting transfers between devices  18.8 us (13%)
  Pallas kernels  14.6 us (10%)
  waiting for transfers between devices  8.67 us (6%)
  local copies, waits for them, and re-layouts  1.43 us (1%)
    all_to_all x2, blocking collectives, summed(): return (sums, lax.all_to_all(scalars, SEC, 0, 0))  47.3 us
    all_to_all x2, blocking collectives, summed(): lax.all_to_all(parts, OP, 0, 0)  31.3 us
    all_to_all x1, blocking collectives, body(): field = lax.all_to_all(spread, OP, 0, 0)  16.2 us
    ppermute x1, starting transfers between devices, body(): other = lax.ppermute(send, 'c', [(0, 1), (1, 0)])  8.79 us
    ppermute x2, starting transfers between devices, summed(): arrived = lax.ppermute(raised, owners, to_next)  5.8 us
    ppermute x2, waiting for transfers between devices, summed(): arrived = lax.ppermute(raised, owners, to_next)  3.68 us
    pallas_call x1, Pallas kernels, body(): call(open_kernel, (block_shape, two_shape, shaped((3, WIDTH, WIDTH), BF16...  3.55 us
    ppermute x1, waiting for transfers between devices, body(): after = lax.ppermute(field, owners, to_previous)  3.01 us
  transfers between devices with their start and end apart: 5, of which 5 were waited for; matrix products, arithmetic and copies ran while one was open for 0% of the time, Pallas kernels for 6%

profile of v6, /device:TPU:1, one launch (start us, length us, event | category | flops | bytes accessed | tf_op | source)
XLA Modules:
  0.0 139.2 jit_solution(7074702656357184550)
XLA Ops:
  0.6 0.0 copy-start.3
  0.6 0.0 copy-start.6
  0.7 3.5 %shard_map.94 = (bf16[512,512]{1,0:T(8,128)(2,1)}, bf16[2,512,512]{2,1,0:T(8,128)(2,1)}, bf16[3,512,512]{2,1,0:T(8,128)(2,1)}) custom-call(bf16[2,512,512]{2,1,0:T(8,128)(2,1)} %start_ref.5, bf16[1,2,512,512]{3,2,1,0:T(8,128)(2,1)} %left_ref.1, bf16[1,2,512,512]{3,2,1,0:T(8,128)(2,1)} %right_ref.1), custom_call_target="tpu_custom_call" | custom-call | bytes 1048576 | tf_op jit(solution)/shard_map/pallas_call | solution.py:346
  4.2 8.8 %collective-permute-start.1 = (bf16[2,512,512]{2,1,0:T(8,128)(2,1)}, bf16[2,512,512]{2,1,0:T(8,128)(2,1)S(1)}, u32[]{:S(2)}, u32[]{:S(2)}) collective-permute-start(bf16[2,512,512]{2,1,0:T(8,128)(2,1)} %get-tuple-element.27), channel_id=1, source_target_pairs={{0,32},{32,0},{1,33},{33,1},{2,34},{34,2},{3,35},{35,3},{4,36},{36... | collective-permute-start | bytes 3145736 | tf_op jit(solution)/shard_map/ppermute | solution.py:353
  13.0 1.3 collective-permute-start
  14.3 0.1 pad_add_fusion.place_ref
  14.4 1.1 collective-permute-done.1.other_ref
  15.5 0.0 copy-done.3
  15.5 0.0 copy-done.6
  15.5 0.0 copy-start.1
  15.5 1.4 %copy-done.1 = bf16[3,512,512]{2,1,0:T(8,128)(2,1)S(1)} copy-done((bf16[3,512,512]{2,1,0:T(8,128)(2,1)S(1)}, bf16[3,512,512]{2,1,0:T(8,128)(2,1)}, u32[]{:S(2)}) %copy-start.1) | copy-done | bytes 1572888
  16.9 0.0 copy-start
  16.9 0.0 copy-start.4
  16.9 0.0 copy-start.5
  16.9 0.0 copy-start.2
  16.9 1.9 %shard_map.95.raised_ref = bf16[512,512]{1,0:T(8,128)(2,1)S(1)} custom-call(s32[3]{0:T(128)S(1)} %pad_add_fusion.place_ref, s32[64]{0:T(128)S(1)} %copy-done.3, s32[64]{0:T(128)S(1)} %copy-done.6, bf16[3,512,512]{2,1,0:T(8,128)(2,1)S(1)} %copy-done.1, bf16[2,512,512]{2,1,0:T(8,128)(2,1)S(1)} %collective-permute-done.1.other_ref), custom_call_target="tpu_custom_call" | custom-call | flops 1073741824 | bytes 4194304 | tf_op jit(solution)/shard_map/pallas_call | solution.py:371
  18.8 3.2 %collective-permute-start.2 = (bf16[512,512]{1,0:T(8,128)(2,1)S(1)}, bf16[512,512]{1,0:T(8,128)(2,1)S(1)}, u32[]{:S(2)}, u32[]{:S(2)}) collective-permute-start(bf16[512,512]{1,0:T(8,128)(2,1)S(1)} %shard_map.95.raised_ref), channel_id=1, source_target_pairs={{0,32},{1,33},{2,34},{3,35},{4,36},{5,37},{6,38},{7,39},{8,40},{9,... | collective-permute-start | bytes 1572872 | tf_op jit(solution)/shard_map/ppermute | solution.py:361
  22.1 0.0 copy-done
  22.1 0.0 copy-done.4
  22.1 0.0 copy-done.5
  22.1 0.7 shard_map.96
  22.8 0.9 collective-permute-done.halo_ref
  23.7 0.0 copy-done.2
  23.7 2.0 %shard_map.97 = (f32[512,512]{1,0:T(8,128)S(1)}, f32[1,128]{1,0:T(1,128)S(1)}) custom-call(s32[3]{0:T(128)S(1)} %pad_add_fusion.place_ref, s32[64]{0:T(128)S(1)} %copy-done.3, s32[64]{0:T(128)S(1)} %copy-done.6, bf16[2,512,512]{2,1,0:T(8,128)(2,1)S(1)} %copy-done, bf16[512,512]{1,0:T(8,128)(2,1)S(1)} %collective-permute-done.halo_ref, ...), custom_call_target="tpu_custom_call" | custom-call | flops 1073741824 | bytes 4194304 | tf_op jit(solution)/shard_map/pallas_call | solution.py:374
  25.7 2.4 %collective-permute-done.2.arrived_ref = bf16[512,512]{1,0:T(8,128)(2,1)S(1)} collective-permute-done((bf16[512,512]{1,0:T(8,128)(2,1)S(1)}, bf16[512,512]{1,0:T(8,128)(2,1)S(1)}, u32[]{:S(2)}, u32[]{:S(2)}) %collective-permute-start.2) | collective-permute-done | bytes 524320 | tf_op jit(solution)/shard_map/ppermute | solution.py:361
  28.2 0.1 shard_map.98
  28.3 15.5 %all_to_all.25.received_ref = bf16[16,144,128]{2,1,0:T(8,128)(2,1)S(1)} all-to-all(bf16[16,144,128]{2,1,0:T(8,128)(2,1)S(1)} %shard_map.98), channel_id=1, replica_groups=mesh['yh'=2,'x'=4,'c'=2,'yl'=2,'z'=16] {'yh','x','c'}, dimensions={0} | all-to-all | bytes 1179648 | tf_op jit(solution)/shard_map/all_to_all | solution.py:366
  43.8 0.1 shard_map.99
  43.8 28.7 %all_to_all.26.gathered_ref = f32[32,1,128]{2,1,0:T(1,128)S(1)} all-to-all(f32[32,1,128]{2,1,0:T(1,128)S(1)} %get-tuple-element.31), channel_id=1, replica_groups=mesh['yh'=2,'x'=4,'c'=2,'yl'=2,'z'=16] {'yl','z'}, dimensions={0} | all-to-all | bytes 32768 | tf_op jit(solution)/shard_map/all_to_all | solution.py:368
  72.5 0.8 shard_map.100
  73.4 16.2 %all_to_all.27.gathered_ref = bf16[16,32,512]{2,1,0:T(8,128)(2,1)S(1)} all-to-all(bf16[16,32,512]{2,1,0:T(8,128)(2,1)S(1)} %get-tuple-element.35), channel_id=1, replica_groups=mesh['yh'=2,'x'=4,'c'=2,'yl'=2,'z'=16] {'yh','x','c'}, dimensions={0} | all-to-all | bytes 1048576 | tf_op jit(solution)/shard_map/all_to_all | solution.py:383
  89.6 3.0 %collective-permute-start.3 = (bf16[16,32,512]{2,1,0:T(8,128)(2,1)S(1)}, bf16[16,32,512]{2,1,0:T(8,128)(2,1)S(1)}, u32[]{:S(2)}, u32[]{:S(2)}) collective-permute-start(bf16[16,32,512]{2,1,0:T(8,128)(2,1)S(1)} %all_to_all.27.gathered_ref), channel_id=1, source_target_pairs={{32,0},{33,1},{34,2},{35,3},{36,4},{37,5},{38,6},{39,7},{40,8},{41... | collective-permute-start | bytes 1572872 | tf_op jit(solution)/shard_map/ppermute | solution.py:384
  92.6 1.9 %shard_map.101.raised_ref = bf16[512,512]{1,0:T(8,128)(2,1)S(1)} custom-call(s32[3]{0:T(128)S(1)} %pad_add_fusion.place_ref, s32[64]{0:T(128)S(1)} %copy-done.6, bf16[16,32,512]{2,1,0:T(8,128)(2,1)S(1)} %all_to_all.27.gathered_ref, bf16[3,512,512]{2,1,0:T(8,128)(2,1)S(1)} %copy-done.2, bf16[2,512,512]{2,1,0:T(8,128)(2,1)S(1)} %collective-permute-done.1.other_ref), custom_call_target="tpu_custom_call" | custom-call | flops 1073741824 | bytes 4194304 | tf_op jit(solution)/shard_map/pallas_call | solution.py:385
  94.5 2.6 %collective-permute-start.4 = (bf16[512,512]{1,0:T(8,128)(2,1)S(1)}, bf16[512,512]{1,0:T(8,128)(2,1)S(1)}, u32[]{:S(2)}, u32[]{:S(2)}) collective-permute-start(bf16[512,512]{1,0:T(8,128)(2,1)S(1)} %shard_map.101.raised_ref), channel_id=1, source_target_pairs={{0,32},{1,33},{2,34},{3,35},{4,36},{5,37},{6,38},{7,39},{8,40},{9,... | collective-permute-start | bytes 1572872 | tf_op jit(solution)/shard_map/ppermute | solution.py:361
  97.1 3.0 %collective-permute-done.3.after_ref = bf16[16,32,512]{2,1,0:T(8,128)(2,1)S(1)} collective-permute-done((bf16[16,32,512]{2,1,0:T(8,128)(2,1)S(1)}, bf16[16,32,512]{2,1,0:T(8,128)(2,1)S(1)}, u32[]{:S(2)}, u32[]{:S(2)}) %collective-permute-start.3) | collective-permute-done | bytes 524320 | tf_op jit(solution)/shard_map/ppermute | solution.py:384
  100.1 1.9 %shard_map.102 = (f32[512,512]{1,0:T(8,128)S(1)}, f32[1,128]{1,0:T(1,128)S(1)}) custom-call(s32[3]{0:T(128)S(1)} %pad_add_fusion.place_ref, s32[64]{0:T(128)S(1)} %copy-done.6, bf16[16,32,512]{2,1,0:T(8,128)(2,1)S(1)} %collective-permute-done.3.after_ref, bf16[512,512]{1,0:T(8,128)(2,1)S(1)} %shard_map.101.raised_ref, ...), custom_call_target="tpu_custom_call" | custom-call | flops 1073741824 | bytes 4194304 | tf_op jit(solution)/shard_map/pallas_call | solution.py:388
  101.9 1.2 collective-permute-done.4.arrived_ref
  103.2 0.1 shard_map.103
  103.3 15.8 %all_to_all.28.received_ref = bf16[16,144,128]{2,1,0:T(8,128)(2,1)S(1)} all-to-all(bf16[16,144,128]{2,1,0:T(8,128)(2,1)S(1)} %shard_map.103), channel_id=1, replica_groups=mesh['yh'=2,'x'=4,'c'=2,'yl'=2,'z'=16] {'yh','x','c'}, dimensions={0} | all-to-all | bytes 1179648 | tf_op jit(solution)/shard_map/all_to_all | solution.py:366
  119.1 0.1 shard_map.104
  119.2 18.6 %all_to_all.29.gathered_ref = f32[32,1,128]{2,1,0:T(1,128)S(1)} all-to-all(f32[32,1,128]{2,1,0:T(1,128)S(1)} %get-tuple-element.39), channel_id=1, replica_groups=mesh['yh'=2,'x'=4,'c'=2,'yl'=2,'z'=16] {'yl','z'}, dimensions={0} | all-to-all | bytes 32768 | tf_op jit(solution)/shard_map/all_to_all | solution.py:368
  137.8 1.4 %shard_map.105 = (bf16[2,32,512]{2,1,0:T(8,128)(2,1)}, bf16[2,32,512]{2,1,0:T(8,128)(2,1)}, f32[1,2]{1,0:T(1,128)}) custom-call(s32[3]{0:T(128)S(1)} %pad_add_fusion.place_ref, s32[64]{0:T(128)S(1)} %copy-done.3, f32[32,1,128]{2,1,0:T(1,128)S(1)} %all_to_all.29.gathered_ref, f32[1,128]{1,0:T(1,128)S(1)} %get-tuple-element.40.known_ref, ...), custom_call_target="tpu_custom_call" | custom-call | bytes 1048576 | tf_op jit(solution)/shard_map/pallas_call | solution.py:393
Async XLA Ops:
  0.6 14.8 %copy-start.3 = (s32[64]{0:T(128)S(1)}, s32[64]{0:T(128)}, u32[]{:S(2)}) copy-start(s32[64]{0:T(128)} %size_ref.9) | copy-start | bytes 772
  0.6 14.8 %copy-start.6 = (s32[64]{0:T(128)S(1)}, s32[64]{0:T(128)}, u32[]{:S(2)}) copy-start(s32[64]{0:T(128)} %spin_ref.7) | copy-start | bytes 772
  4.2 11.3 %collective-permute-start.1 = (bf16[2,512,512]{2,1,0:T(8,128)(2,1)}, bf16[2,512,512]{2,1,0:T(8,128)(2,1)S(1)}, u32[]{:S(2)}, u32[]{:S(2)}) collective-permute-start(bf16[2,512,512]{2,1,0:T(8,128)(2,1)} %get-tuple-element.27), channel_id=1, source_target_pairs={{0,32},{32,0},{1,33},{33,1},{2,34},{34,2},{3,35},{35,3},{4,36},{36... | collective-permute-start | bytes 3145736 | tf_op jit(solution)/shard_map/ppermute | solution.py:353
  13.0 10.7 %collective-permute-start = (bf16[512,512]{1,0:T(8,128)(2,1)}, bf16[512,512]{1,0:T(8,128)(2,1)S(1)}, u32[]{:S(2)}, u32[]{:S(2)}) collective-permute-start(bf16[512,512]{1,0:T(8,128)(2,1)} %get-tuple-element.25), channel_id=1, source_target_pairs={{1,32},{2,33},{3,34},{4,35},{5,36},{6,37},{7,38},{8,39},{9,40},{10... | collective-permute-start | bytes 1572872 | tf_op jit(solution)/shard_map/ppermute | solution.py:354
  15.5 1.4 %copy-start.1 = (bf16[3,512,512]{2,1,0:T(8,128)(2,1)S(1)}, bf16[3,512,512]{2,1,0:T(8,128)(2,1)}, u32[]{:S(2)}) copy-start(bf16[3,512,512]{2,1,0:T(8,128)(2,1)} %get-tuple-element.26.own_ref) | copy-start | bytes 4718596
  16.9 5.2 %copy-start = (bf16[2,512,512]{2,1,0:T(8,128)(2,1)S(1)}, bf16[2,512,512]{2,1,0:T(8,128)(2,1)}, u32[]{:S(2)}) copy-start(bf16[2,512,512]{2,1,0:T(8,128)(2,1)} %start_ref.5) | copy-start | bytes 3145732
  16.9 5.2 %copy-start.4 = (f32[2,512]{1,0:T(2,128)S(1)}, f32[2,512]{1,0:T(2,128)}, u32[]{:S(2)}) copy-start(f32[2,512]{1,0:T(2,128)} %left_levels_ref.1) | copy-start | bytes 12292
  16.9 5.2 %copy-start.5 = (f32[2,512]{1,0:T(2,128)S(1)}, f32[2,512]{1,0:T(2,128)}, u32[]{:S(2)}) copy-start(f32[2,512]{1,0:T(2,128)} %right_levels_ref.1) | copy-start | bytes 12292
  16.9 6.8 %copy-start.2 = (bf16[3,512,512]{2,1,0:T(8,128)(2,1)S(1)}, bf16[3,512,512]{2,1,0:T(8,128)(2,1)}, u32[]{:S(2)}) copy-start(bf16[3,512,512]{2,1,0:T(8,128)(2,1)} %get-tuple-element.26.own_ref) | copy-start | bytes 4718596
  18.8 9.3 %collective-permute-start.2 = (bf16[512,512]{1,0:T(8,128)(2,1)S(1)}, bf16[512,512]{1,0:T(8,128)(2,1)S(1)}, u32[]{:S(2)}, u32[]{:S(2)}) collective-permute-start(bf16[512,512]{1,0:T(8,128)(2,1)S(1)} %shard_map.95.raised_ref), channel_id=1, source_target_pairs={{0,32},{1,33},{2,34},{3,35},{4,36},{5,37},{6,38},{7,39},{8,40},{9,... | collective-permute-start | bytes 1572872 | tf_op jit(solution)/shard_map/ppermute | solution.py:361
  89.6 10.5 %collective-permute-start.3 = (bf16[16,32,512]{2,1,0:T(8,128)(2,1)S(1)}, bf16[16,32,512]{2,1,0:T(8,128)(2,1)S(1)}, u32[]{:S(2)}, u32[]{:S(2)}) collective-permute-start(bf16[16,32,512]{2,1,0:T(8,128)(2,1)S(1)} %all_to_all.27.gathered_ref), channel_id=1, source_target_pairs={{32,0},{33,1},{34,2},{35,3},{36,4},{37,5},{38,6},{39,7},{40,8},{41... | collective-permute-start | bytes 1572872 | tf_op jit(solution)/shard_map/ppermute | solution.py:384
  94.5 8.7 %collective-permute-start.4 = (bf16[512,512]{1,0:T(8,128)(2,1)S(1)}, bf16[512,512]{1,0:T(8,128)(2,1)S(1)}, u32[]{:S(2)}, u32[]{:S(2)}) collective-permute-start(bf16[512,512]{1,0:T(8,128)(2,1)S(1)} %shard_map.101.raised_ref), channel_id=1, source_target_pairs={{0,32},{1,33},{2,34},{3,35},{4,36},{5,37},{6,38},{7,39},{8,40},{9,... | collective-permute-start | bytes 1572872 | tf_op jit(solution)/shard_map/ppermute | solution.py:361

commit v7 on v6

--- a/solution.py
+++ b/solution.py
@@ -16,7 +16,7 @@
 TILES = WIDTH // LANES
 PART = ROWS * TILES + 16
 VMEM_LIMIT = 24 * 1024 * 1024
-WHOLE_VMEM = 62 * 1024 * 1024
+WHOLE_VMEM = 54 * 1024 * 1024
 
 VM = pl.BlockSpec(memory_space=pltpu.VMEM)
 SM = pl.BlockSpec(memory_space=pltpu.SMEM)
@@ -345,7 +345,7 @@
 
     halo_source, send, own = call(
         open_kernel,
-        (block_shape, two_shape, shaped((3, WIDTH, WIDTH), BF16)),
+        (block_shape, two_shape, pltpu.VMEM((3, WIDTH, WIDTH), BF16)),
         [HBM] * 3,
         [pltpu.SemaphoreType.DMA((6,))],
         vmem=WHOLE_VMEM,

time: 140 us -> 138 us (0.986)
  local copies, waits for them, and re-layouts: 1.43 us -> 0.02 us
    unnamed x14 -> x10, local copies, waits for them, and re-layouts: 1.43 us -> 0.02 us
where the time goes in v7:
time: 138 us; the launch traced here: 137 us
  blocking collectives  94.8 us (69%)
  starting transfers between devices  18.9 us (14%)
  Pallas kernels  14.1 us (10%)
  waiting for transfers between devices  8.7 us (6%)
    all_to_all x2, blocking collectives, summed(): return (sums, lax.all_to_all(scalars, SEC, 0, 0))  47.3 us
    all_to_all x2, blocking collectives, summed(): lax.all_to_all(parts, OP, 0, 0)  31.3 us
    all_to_all x1, blocking collectives, body(): field = lax.all_to_all(spread, OP, 0, 0)  16.2 us
    ppermute x1, starting transfers between devices, body(): other = lax.ppermute(send, 'c', [(0, 1), (1, 0)])  8.82 us
    ppermute x2, starting transfers between devices, summed(): arrived = lax.ppermute(raised, owners, to_next)  5.82 us
    pallas_call x1, Pallas kernels, body(): call(open_kernel, (block_shape, two_shape, pltpu.VMEM((3, WIDTH, WIDTH),...  3.06 us
    ppermute x1, waiting for transfers between devices, body(): after = lax.ppermute(field, owners, to_previous)  3.02 us
    ppermute x1, starting transfers between devices, body(): after = lax.ppermute(field, owners, to_previous)  2.97 us
  transfers between devices with their start and end apart: 5, of which 5 were waited for; matrix products, arithmetic and copies ran while one was open for 0% of the time, Pallas kernels for 6%

profile of v7, /device:TPU:1, one launch (start us, length us, event | category | flops | bytes accessed | tf_op | source)
XLA Modules:
  0.0 137.3 jit_solution(5655492928243506076)
XLA Ops:
  0.6 0.0 copy-start.1
  0.6 0.0 copy-start.4
  0.7 3.1 %shard_map.94 = (bf16[512,512]{1,0:T(8,128)(2,1)}, bf16[2,512,512]{2,1,0:T(8,128)(2,1)}, bf16[3,512,512]{2,1,0:T(8,128)(2,1)S(1)}) custom-call(bf16[2,512,512]{2,1,0:T(8,128)(2,1)} %start_ref.5, bf16[1,2,512,512]{3,2,1,0:T(8,128)(2,1)} %left_ref.1, bf16[1,2,512,512]{3,2,1,0:T(8,128)(2,1)} %right_ref.1), custom_call_target="tpu_custom_call" | custom-call | bytes 1048576 | tf_op jit(solution)/shard_map/pallas_call | solution.py:346
  3.7 8.8 %collective-permute-start.1 = (bf16[2,512,512]{2,1,0:T(8,128)(2,1)}, bf16[2,512,512]{2,1,0:T(8,128)(2,1)S(1)}, u32[]{:S(2)}, u32[]{:S(2)}) collective-permute-start(bf16[2,512,512]{2,1,0:T(8,128)(2,1)} %get-tuple-element.27), channel_id=1, source_target_pairs={{0,32},{32,0},{1,33},{33,1},{2,34},{34,2},{3,35},{35,3},{4,36},{36... | collective-permute-start | bytes 3145736 | tf_op jit(solution)/shard_map/ppermute | solution.py:353
  12.6 1.3 collective-permute-start
  13.9 0.1 pad_add_fusion.place_ref
  13.9 1.1 collective-permute-done.1.other_ref
  15.0 0.0 copy-done.1
  15.0 0.0 copy-done.4
  15.0 0.0 copy-start
  15.0 0.0 copy-start.2
  15.0 0.0 copy-start.3
  15.1 1.9 %shard_map.95.raised_ref = bf16[512,512]{1,0:T(8,128)(2,1)S(1)} custom-call(s32[3]{0:T(128)S(1)} %pad_add_fusion.place_ref, s32[64]{0:T(128)S(1)} %copy-done.1, s32[64]{0:T(128)S(1)} %copy-done.4, bf16[3,512,512]{2,1,0:T(8,128)(2,1)S(1)} %get-tuple-element.26.own_ref, bf16[2,512,512]{2,1,0:T(8,128)(2,1)S(1)} %collective-permute-done.1.other_ref), custom_call_target="tpu_custom_call" | custom-call | flops 1073741824 | bytes 4194304 | tf_op jit(solution)/shard_map/pallas_call | solution.py:371
  17.0 3.2 %collective-permute-start.2 = (bf16[512,512]{1,0:T(8,128)(2,1)S(1)}, bf16[512,512]{1,0:T(8,128)(2,1)S(1)}, u32[]{:S(2)}, u32[]{:S(2)}) collective-permute-start(bf16[512,512]{1,0:T(8,128)(2,1)S(1)} %shard_map.95.raised_ref), channel_id=1, source_target_pairs={{0,32},{1,33},{2,34},{3,35},{4,36},{5,37},{6,38},{7,39},{8,40},{9,... | collective-permute-start | bytes 1572872 | tf_op jit(solution)/shard_map/ppermute | solution.py:361
  20.2 0.0 copy-done
  20.2 0.0 copy-done.2
  20.3 0.0 copy-done.3
  20.3 0.7 shard_map.96
  21.0 2.3 %collective-permute-done.halo_ref = bf16[512,512]{1,0:T(8,128)(2,1)S(1)} collective-permute-done((bf16[512,512]{1,0:T(8,128)(2,1)}, bf16[512,512]{1,0:T(8,128)(2,1)S(1)}, u32[]{:S(2)}, u32[]{:S(2)}) %collective-permute-start) | collective-permute-done | bytes 524320 | tf_op jit(solution)/shard_map/ppermute | solution.py:354
  23.3 2.0 %shard_map.97 = (f32[512,512]{1,0:T(8,128)S(1)}, f32[1,128]{1,0:T(1,128)S(1)}) custom-call(s32[3]{0:T(128)S(1)} %pad_add_fusion.place_ref, s32[64]{0:T(128)S(1)} %copy-done.1, s32[64]{0:T(128)S(1)} %copy-done.4, bf16[2,512,512]{2,1,0:T(8,128)(2,1)S(1)} %copy-done, bf16[512,512]{1,0:T(8,128)(2,1)S(1)} %collective-permute-done.halo_ref, ...), custom_call_target="tpu_custom_call" | custom-call | flops 1073741824 | bytes 4194304 | tf_op jit(solution)/shard_map/pallas_call | solution.py:374
  25.3 1.1 collective-permute-done.2.arrived_ref
  26.3 0.1 shard_map.98
  26.5 15.5 %all_to_all.25.received_ref = bf16[16,144,128]{2,1,0:T(8,128)(2,1)S(1)} all-to-all(bf16[16,144,128]{2,1,0:T(8,128)(2,1)S(1)} %shard_map.98), channel_id=1, replica_groups=mesh['yh'=2,'x'=4,'c'=2,'yl'=2,'z'=16] {'yh','x','c'}, dimensions={0} | all-to-all | bytes 1179648 | tf_op jit(solution)/shard_map/all_to_all | solution.py:366
  41.9 0.1 shard_map.99
  42.0 28.7 %all_to_all.26.gathered_ref = f32[32,1,128]{2,1,0:T(1,128)S(1)} all-to-all(f32[32,1,128]{2,1,0:T(1,128)S(1)} %get-tuple-element.31), channel_id=1, replica_groups=mesh['yh'=2,'x'=4,'c'=2,'yl'=2,'z'=16] {'yl','z'}, dimensions={0} | all-to-all | bytes 32768 | tf_op jit(solution)/shard_map/all_to_all | solution.py:368
  70.7 0.8 shard_map.100
  71.5 16.2 %all_to_all.27.gathered_ref = bf16[16,32,512]{2,1,0:T(8,128)(2,1)S(1)} all-to-all(bf16[16,32,512]{2,1,0:T(8,128)(2,1)S(1)} %get-tuple-element.35), channel_id=1, replica_groups=mesh['yh'=2,'x'=4,'c'=2,'yl'=2,'z'=16] {'yh','x','c'}, dimensions={0} | all-to-all | bytes 1048576 | tf_op jit(solution)/shard_map/all_to_all | solution.py:383
  87.7 3.0 %collective-permute-start.3 = (bf16[16,32,512]{2,1,0:T(8,128)(2,1)S(1)}, bf16[16,32,512]{2,1,0:T(8,128)(2,1)S(1)}, u32[]{:S(2)}, u32[]{:S(2)}) collective-permute-start(bf16[16,32,512]{2,1,0:T(8,128)(2,1)S(1)} %all_to_all.27.gathered_ref), channel_id=1, source_target_pairs={{32,0},{33,1},{34,2},{35,3},{36,4},{37,5},{38,6},{39,7},{40,8},{41... | collective-permute-start | bytes 1572872 | tf_op jit(solution)/shard_map/ppermute | solution.py:384
  90.7 1.9 %shard_map.101.raised_ref = bf16[512,512]{1,0:T(8,128)(2,1)S(1)} custom-call(s32[3]{0:T(128)S(1)} %pad_add_fusion.place_ref, s32[64]{0:T(128)S(1)} %copy-done.4, bf16[16,32,512]{2,1,0:T(8,128)(2,1)S(1)} %all_to_all.27.gathered_ref, bf16[3,512,512]{2,1,0:T(8,128)(2,1)S(1)} %get-tuple-element.26.own_ref, bf16[2,512,512]{2,1,0:T(8,128)(2,1)S(1)} %collective-permute-done.1.other_ref), custom_call_target="tpu_custom_call" | custom-call | flops 1073741824 | bytes 4194304 | tf_op jit(solution)/shard_map/pallas_call | solution.py:385
  92.6 2.6 %collective-permute-start.4 = (bf16[512,512]{1,0:T(8,128)(2,1)S(1)}, bf16[512,512]{1,0:T(8,128)(2,1)S(1)}, u32[]{:S(2)}, u32[]{:S(2)}) collective-permute-start(bf16[512,512]{1,0:T(8,128)(2,1)S(1)} %shard_map.101.raised_ref), channel_id=1, source_target_pairs={{0,32},{1,33},{2,34},{3,35},{4,36},{5,37},{6,38},{7,39},{8,40},{9,... | collective-permute-start | bytes 1572872 | tf_op jit(solution)/shard_map/ppermute | solution.py:361
  95.2 3.0 %collective-permute-done.3.after_ref = bf16[16,32,512]{2,1,0:T(8,128)(2,1)S(1)} collective-permute-done((bf16[16,32,512]{2,1,0:T(8,128)(2,1)S(1)}, bf16[16,32,512]{2,1,0:T(8,128)(2,1)S(1)}, u32[]{:S(2)}, u32[]{:S(2)}) %collective-permute-start.3) | collective-permute-done | bytes 524320 | tf_op jit(solution)/shard_map/ppermute | solution.py:384
  98.2 1.8 %shard_map.102 = (f32[512,512]{1,0:T(8,128)S(1)}, f32[1,128]{1,0:T(1,128)S(1)}) custom-call(s32[3]{0:T(128)S(1)} %pad_add_fusion.place_ref, s32[64]{0:T(128)S(1)} %copy-done.4, bf16[16,32,512]{2,1,0:T(8,128)(2,1)S(1)} %collective-permute-done.3.after_ref, bf16[512,512]{1,0:T(8,128)(2,1)S(1)} %shard_map.101.raised_ref, ...), custom_call_target="tpu_custom_call" | custom-call | flops 1073741824 | bytes 4194304 | tf_op jit(solution)/shard_map/pallas_call | solution.py:388
  100.1 1.2 collective-permute-done.4.arrived_ref
  101.3 0.1 shard_map.103
  101.4 15.8 %all_to_all.28.received_ref = bf16[16,144,128]{2,1,0:T(8,128)(2,1)S(1)} all-to-all(bf16[16,144,128]{2,1,0:T(8,128)(2,1)S(1)} %shard_map.103), channel_id=1, replica_groups=mesh['yh'=2,'x'=4,'c'=2,'yl'=2,'z'=16] {'yh','x','c'}, dimensions={0} | all-to-all | bytes 1179648 | tf_op jit(solution)/shard_map/all_to_all | solution.py:366
  117.2 0.1 shard_map.104
  117.3 18.6 %all_to_all.29.gathered_ref = f32[32,1,128]{2,1,0:T(1,128)S(1)} all-to-all(f32[32,1,128]{2,1,0:T(1,128)S(1)} %get-tuple-element.39), channel_id=1, replica_groups=mesh['yh'=2,'x'=4,'c'=2,'yl'=2,'z'=16] {'yl','z'}, dimensions={0} | all-to-all | bytes 32768 | tf_op jit(solution)/shard_map/all_to_all | solution.py:368
  135.9 1.4 %shard_map.105 = (bf16[2,32,512]{2,1,0:T(8,128)(2,1)}, bf16[2,32,512]{2,1,0:T(8,128)(2,1)}, f32[1,2]{1,0:T(1,128)}) custom-call(s32[3]{0:T(128)S(1)} %pad_add_fusion.place_ref, s32[64]{0:T(128)S(1)} %copy-done.1, f32[32,1,128]{2,1,0:T(1,128)S(1)} %all_to_all.29.gathered_ref, f32[1,128]{1,0:T(1,128)S(1)} %get-tuple-element.40.known_ref, ...), custom_call_target="tpu_custom_call" | custom-call | bytes 1048576 | tf_op jit(solution)/shard_map/pallas_call | solution.py:393
Async XLA Ops:
  0.6 14.4 %copy-start.1 = (s32[64]{0:T(128)S(1)}, s32[64]{0:T(128)}, u32[]{:S(2)}) copy-start(s32[64]{0:T(128)} %size_ref.9) | copy-start | bytes 772
  0.6 14.4 %copy-start.4 = (s32[64]{0:T(128)S(1)}, s32[64]{0:T(128)}, u32[]{:S(2)}) copy-start(s32[64]{0:T(128)} %spin_ref.7) | copy-start | bytes 772
  3.7 11.3 %collective-permute-start.1 = (bf16[2,512,512]{2,1,0:T(8,128)(2,1)}, bf16[2,512,512]{2,1,0:T(8,128)(2,1)S(1)}, u32[]{:S(2)}, u32[]{:S(2)}) collective-permute-start(bf16[2,512,512]{2,1,0:T(8,128)(2,1)} %get-tuple-element.27), channel_id=1, source_target_pairs={{0,32},{32,0},{1,33},{33,1},{2,34},{34,2},{3,35},{35,3},{4,36},{36... | collective-permute-start | bytes 3145736 | tf_op jit(solution)/shard_map/ppermute | solution.py:353
  12.6 10.7 %collective-permute-start = (bf16[512,512]{1,0:T(8,128)(2,1)}, bf16[512,512]{1,0:T(8,128)(2,1)S(1)}, u32[]{:S(2)}, u32[]{:S(2)}) collective-permute-start(bf16[512,512]{1,0:T(8,128)(2,1)} %get-tuple-element.25), channel_id=1, source_target_pairs={{1,32},{2,33},{3,34},{4,35},{5,36},{6,37},{7,38},{8,39},{9,40},{10... | collective-permute-start | bytes 1572872 | tf_op jit(solution)/shard_map/ppermute | solution.py:354
  15.0 5.2 %copy-start = (bf16[2,512,512]{2,1,0:T(8,128)(2,1)S(1)}, bf16[2,512,512]{2,1,0:T(8,128)(2,1)}, u32[]{:S(2)}) copy-start(bf16[2,512,512]{2,1,0:T(8,128)(2,1)} %start_ref.5) | copy-start | bytes 3145732
  15.0 5.2 %copy-start.2 = (f32[2,512]{1,0:T(2,128)S(1)}, f32[2,512]{1,0:T(2,128)}, u32[]{:S(2)}) copy-start(f32[2,512]{1,0:T(2,128)} %left_levels_ref.1) | copy-start | bytes 12292
  15.0 5.2 %copy-start.3 = (f32[2,512]{1,0:T(2,128)S(1)}, f32[2,512]{1,0:T(2,128)}, u32[]{:S(2)}) copy-start(f32[2,512]{1,0:T(2,128)} %right_levels_ref.1) | copy-start | bytes 12292
  17.0 9.4 %collective-permute-start.2 = (bf16[512,512]{1,0:T(8,128)(2,1)S(1)}, bf16[512,512]{1,0:T(8,128)(2,1)S(1)}, u32[]{:S(2)}, u32[]{:S(2)}) collective-permute-start(bf16[512,512]{1,0:T(8,128)(2,1)S(1)} %shard_map.95.raised_ref), channel_id=1, source_target_pairs={{0,32},{1,33},{2,34},{3,35},{4,36},{5,37},{6,38},{7,39},{8,40},{9,... | collective-permute-start | bytes 1572872 | tf_op jit(solution)/shard_map/ppermute | solution.py:361
  87.7 10.5 %collective-permute-start.3 = (bf16[16,32,512]{2,1,0:T(8,128)(2,1)S(1)}, bf16[16,32,512]{2,1,0:T(8,128)(2,1)S(1)}, u32[]{:S(2)}, u32[]{:S(2)}) collective-permute-start(bf16[16,32,512]{2,1,0:T(8,128)(2,1)S(1)} %all_to_all.27.gathered_ref), channel_id=1, source_target_pairs={{32,0},{33,1},{34,2},{35,3},{36,4},{37,5},{38,6},{39,7},{40,8},{41... | collective-permute-start | bytes 1572872 | tf_op jit(solution)/shard_map/ppermute | solution.py:384
  92.6 8.7 %collective-permute-start.4 = (bf16[512,512]{1,0:T(8,128)(2,1)S(1)}, bf16[512,512]{1,0:T(8,128)(2,1)S(1)}, u32[]{:S(2)}, u32[]{:S(2)}) collective-permute-start(bf16[512,512]{1,0:T(8,128)(2,1)S(1)} %shard_map.101.raised_ref), channel_id=1, source_target_pairs={{0,32},{1,33},{2,34},{3,35},{4,36},{5,37},{6,38},{7,39},{8,40},{9,... | collective-permute-start | bytes 1572872 | tf_op jit(solution)/shard_map/ppermute | solution.py:361
